TPU v7x, 512 devices: a whole 4x4x16 slice. The times are simulated.
512 devices in a mesh: seq: 64 (over x, z), tp: 8 (over y, core).
Axes of the slice: x: 4, y: 4, z: 16, core: 2. Of those that a mesh axis runs over, the one named last changes fastest.
Arguments:
- x_in: bfloat16 [32768, 5120], P('seq', 'tp'), may hold values from -17 to 17
- bc_in: bfloat16 [32768, 256], P('seq'), may hold values from -17 to 17
- z_gate: bfloat16 [32768, 5120], P('seq', 'tp'), may hold values from -6 to 6
- dt_in: bfloat16 [32768, 80], P('seq', 'tp'), may hold values from -3 to 3
- conv_x: float32 [4, 5120], P(None, 'tp'), may hold values from -3.05 to 3.05
- conv_bc: float32 [4, 256], replicated, may hold values from -3.05 to 3.05
- dt_bias: float32 [80], P('tp'), may hold values from -9 to 0
- a_log: float32 [80], P('tp'), may hold values from -7 to 0
- d_skip: float32 [80], P('tp'), may hold values from 0.5 to 1.5
- norm_gain: float32 [5120], P('tp'), may hold values from 0.5 to 1.5
- out_weight: bfloat16 [5120, 2560], P('tp', 'seq'), may hold values from -0.078125 to 0.078125
Outputs:
- mixed: bfloat16 [32768, 2560], P('seq', 'tp')
All inputs are finite; a program needn't handle non-finite values.
Results may differ from a plain program's by a relative error of at most 0.017.
Values may be sent and summed in bfloat16 or wider, within the bound.
No kernel may reach another device: no remote copies, remote signals or barrier semaphores. Data moves between devices by JAX's collectives and lax.ppermute only.
A program may use at most 128 MiB of HBM per device.

v0:
```python
import jax
import jax.numpy as jnp
from jax import lax
from jax.sharding import PartitionSpec as P

HEADS = 80
HEADDIM = 64
STATE = 128
CONV = 4
GROUP = 256


EPSILON = 1e-05
HIGH = lax.Precision.HIGHEST


def shifted(value, axis, steps):
    count = lax.axis_size(axis)
    initial, last = (max(0, -steps), min(count, count - steps))
    return lax.ppermute(value, axis, [(source, source + steps) for source in range(initial, last)])


def carried_in(part, axis, combine, identity):
    place = lax.axis_index(axis)
    gathered = jax.tree.map(lambda a: lax.all_gather(a, axis), part)
    state = jax.tree.map(lambda a, e: jnp.zeros_like(a) + jnp.asarray(e, a.dtype), part, identity)

    def one(lap, state):
        return combine(
            state, jax.tree.map(lambda a: lax.dynamic_index_in_dim(a, lap, 0, False), gathered)
        )

    return lax.fori_loop(0, place, one, state)


def causal_mix(extended, weights, tok_rows):
    total = weights[0][None, :] * extended[0:tok_rows].astype(jnp.float32)
    for offset in range(1, CONV):
        total = total + weights[offset][None, :] * extended[offset : offset + tok_rows].astype(
            jnp.float32
        )
    return jax.nn.silu(total).astype(jnp.bfloat16)


def combine_states(earlier, later):
    return (earlier[0] + later[0], jnp.exp(later[0])[:, None, None] * earlier[1] + later[1])


def on_device(
    x_in, bc_in, z_gate, dt_in, conv_x, conv_bc, dt_bias, a_log, d_skip, norm_gain, out_weight
):
    tok_rows = x_in.shape[0]
    rim_rows = CONV - 1
    x_rim, bc_rim = shifted((x_in[tok_rows - rim_rows :], bc_in[tok_rows - rim_rows :]), "seq", 1)
    xc = causal_mix(jnp.concatenate([x_rim, x_in], axis=0), conv_x, tok_rows)
    bcc = causal_mix(jnp.concatenate([bc_rim, bc_in], axis=0), conv_bc, tok_rows)
    head_count = dt_in.shape[1]
    blocks = tok_rows // GROUP
    step = jax.nn.softplus(dt_in.astype(jnp.float32) + dt_bias[None, :])
    rate = -jnp.exp(a_log)[None, :] * step
    x_blocks = xc.astype(jnp.float32).reshape(blocks, GROUP, head_count, HEADDIM)
    b_blocks = bcc[:, :STATE].astype(jnp.float32).reshape(blocks, GROUP, STATE)
    c_blocks = bcc[:, STATE:].astype(jnp.float32).reshape(blocks, GROUP, STATE)
    step_blocks = step.reshape(blocks, GROUP, head_count)
    cumul = jnp.cumsum(rate.reshape(blocks, GROUP, head_count), axis=1)
    causal = (jnp.arange(GROUP)[:, None] >= jnp.arange(GROUP)[None, :])[None, :, :, None]
    spread = cumul[:, :, None, :] - cumul[:, None, :, :]
    decays = jnp.where(causal, jnp.exp(jnp.where(causal, spread, 0.0)), 0.0)
    inner_cb = jnp.einsum("ktn,ksn->kts", c_blocks, b_blocks, precision=HIGH)
    mix_weights = inner_cb[:, :, :, None] * decays * step_blocks[:, None, :, :]
    result = jnp.einsum("ktsh,kshp->kthp", mix_weights, x_blocks, precision=HIGH)
    last_cumul = cumul[:, GROUP - 1, :]
    tail = jnp.exp(last_cumul[:, None, :] - cumul) * step_blocks
    block_states = jnp.einsum("ksh,kshp,ksn->khpn", tail, x_blocks, b_blocks, precision=HIGH)
    carry = jnp.zeros((head_count, HEADDIM, STATE), jnp.float32)
    entering = []
    for block in range(blocks):
        entering.append(carry)
        carry = jnp.exp(last_cumul[block])[:, None, None] * carry + block_states[block]
    decay_total = jnp.sum(last_cumul, axis=0)
    before = jnp.cumsum(last_cumul, axis=0) - last_cumul
    result = result + jnp.exp(cumul)[..., None] * jnp.einsum(
        "ktn,khpn->kthp", c_blocks, jnp.stack(entering), precision=HIGH
    )
    zero_state = (
        jnp.zeros((head_count,), jnp.float32),
        jnp.zeros((head_count, HEADDIM, STATE), jnp.float32),
    )
    prior_decay, incoming = carried_in((decay_total, carry), "seq", combine_states, zero_state)
    reach = jnp.exp(cumul + before[:, None, :])
    result = result + reach[..., None] * jnp.einsum(
        "ktn,hpn->kthp", c_blocks, incoming, precision=HIGH
    )
    result = result.reshape(tok_rows, head_count, HEADDIM) + d_skip[None, :, None] * xc.astype(
        jnp.float32
    ).reshape(tok_rows, head_count, HEADDIM)
    gated = result.reshape(tok_rows, head_count * HEADDIM) * jax.nn.silu(z_gate.astype(jnp.float32))
    squares = lax.psum(jnp.sum(gated * gated, axis=1), "tp")
    mean_square = squares / (HEADS * HEADDIM)
    normed = (gated * lax.rsqrt(mean_square + EPSILON)[:, None] * norm_gain[None, :]).astype(
        jnp.bfloat16
    )
    partial_terms = jnp.dot(
        normed,
        lax.all_gather(out_weight, "seq", axis=1, tiled=True),
        preferred_element_type=jnp.float32,
    )
    summed = lax.psum_scatter(
        partial_terms.astype(jnp.bfloat16), "tp", scatter_dimension=1, tiled=True
    )
    return summed


def solution(mesh):
    in_specs = (
        P("seq", "tp"),
        P("seq", None),
        P("seq", "tp"),
        P("seq", "tp"),
        P(None, "tp"),
        P(),
        P("tp"),
        P("tp"),
        P("tp"),
        P("tp"),
        P("tp", "seq"),
    )
    out_specs = P("seq", "tp")
    return jax.shard_map(
        on_device, mesh=mesh, in_specs=in_specs, out_specs=out_specs, check_vma=False
    )
```

profile of v0, /device:TPU:1, one launch (start us, length us, event | category | flops | bytes accessed | tf_op | source)
XLA Modules:
  0.0 440.5 jit_solution(4616630238121668325)
XLA Ops:
  6.5 0.8 slice.80
  7.5 4.4 collective-permute-start
  11.9 0.7 slice.88
  12.6 3.5 collective-permute-start.1
  16.1 0.7 exponential_negate_fusion
  16.8 0.8 broadcast_multiply_fusion
  17.7 1.2 reduce-window.6
  19.4 0.3 fusion.34
  19.7 0.3 slice_reduce_fusion.5
  20.3 0.8 fusion.40
  21.2 0.9 slice_reduce_fusion.4
  22.1 0.3 copy.58
  22.4 0.3 multiply_convert_fusion.3
  22.8 1.5 multiply_convert_fusion.1
  24.4 0.6 convert_multiply_fusion.1
  25.0 0.7 fusion.22
  25.7 0.8 slice_add_fusion
  26.6 0.7 all-gather.6.cloned.1.call-update
  27.4 1.3 dynamic-slice
  29.5 0.2 dynamic-update-slice
  29.7 118.0 %all-reduce.1 = f32[640]{0:T(1024)S(1)} all-reduce(f32[640]{0:T(1024)S(1)} %dynamic-update-slice), channel_id=2, replica_groups=mesh['seq'=64,'tp'=8] {'seq'}, use_global_device_ids=true, to_apply=%add.1 | all-reduce | flops 640 | bytes 5120
  147.9 1.3 copy.74
  149.6 4.2 fusion.15
  153.8 0.7 fusion.14
  154.5 94.4 %all-gather.4.cloned.1.call-done = f32[64,10,64,128]{3,2,1,0:T(8,128)} async-done(((f32[1,10,64,128]{3,2,1,0:T(8,128)}), f32[64,10,64,128]{3,2,1,0:T(8,128)}) %all-gather.4.cloned.1.call-update) | async-done | bytes 20971536 | tf_op jit(solution)/shard_map/all_gather | solution.py:25
  249.2 0.7 fusion.13
  249.9 1.0 copy.73
  251.1 0.6 multiply_reduce_fusion
  251.6 12.8 %psum.7 = f32[512]{0:T(512)S(1)} all-reduce(f32[512]{0:T(512)S(1)} %get-tuple-element.66), channel_id=1, replica_groups=mesh['seq'=64,'tp'=8] {'tp'}, use_global_device_ids=true, to_apply=%region_7.8 | all-reduce | flops 512 | bytes 4096 | tf_op jit(solution)/shard_map/psum | solution.py:98
  264.5 119.9 %all-gather.6.cloned.1.call-done = bf16[640,2560]{0,1:T(8,128)(2,1)} async-done(((bf16[640,40]{0,1:T(8,128)(2,1)}), bf16[640,2560]{0,1:T(8,128)(2,1)}) %all-gather.6.cloned.1.call-update) | async-done | bytes 3276816 | tf_op jit(solution)/shard_map/all_gather | solution.py:105
  384.4 5.7 %convolution_convert_fusion = bf16[512,2560]{0,1:T(8,128)(2,1)} fusion(bf16[640,2560]{0,1:T(8,128)(2,1)} %all-gather.6.cloned.1.call-done, f32[512,640]{0,1:T(8,128)S(1)} %get-tuple-element.67, f32[640]{0:T(1024)S(1)} %copy-done.3, f32[512]{0:T(512)S(1)} %add_rsqrt_fusion), kind=kOutput, calls=%fused_computation.9 | convolution fusion | flops 1680015360 | bytes 7213568 | tf_op jit(solution)/shard_map/dot_general | solution.py:103
  390.1 43.9 %reduce-scatter.2.cloned.1.call-done = bf16[512,320]{0,1:T(8,128)(2,1)} async-done(((bf16[512,2560]{0,1:T(8,128)(2,1)}), bf16[512,320]{0,1:T(8,128)(2,1)}) %reduce-scatter.2.cloned.1.call-update) | async-done | bytes 327696 | tf_op jit(solution)/shard_map/reduce_scatter | solution.py:108
  (49 shorter events, 2.4 us)
Async XLA Ops:
  6.5 15.6 %copy-start = (bf16[512,640]{1,0:T(8,128)(2,1)S(1)}, bf16[512,640]{1,0:T(8,128)(2,1)}, u32[]{:S(2)}) copy-start(bf16[512,640]{1,0:T(8,128)(2,1)} %param.13) | copy-start | bytes 1966084
  6.5 15.8 %copy-start.1 = (bf16[512,256]{1,0:T(8,128)(2,1)S(1)}, bf16[512,256]{1,0:T(8,128)(2,1)}, u32[]{:S(2)}) copy-start(bf16[512,256]{1,0:T(8,128)(2,1)} %param.14) | copy-start | bytes 786436
  6.5 242.4 %all-gather.4.cloned.1.call-start = ((), (), s32[]{:S(2)}) async-start(), calls=%async_computation.1 | async-start | bytes 21299200 | tf_op jit(solution)/shard_map/all_gather | solution.py:25
  7.5 15.2 %collective-permute-start = (bf16[3,640]{0,1:T(8,128)(2,1)S(1)}, bf16[3,640]{0,1:T(8,128)(2,1)S(1)}, u32[]{:S(2)}, u32[]{:S(2)}) collective-permute-start(bf16[3,640]{0,1:T(8,128)(2,1)S(1)} %copy.57), channel_id=1, source_target_pairs={{0,8},{8,16},{16,24},{24,32},{32,40},{40,48},{48,56},{56,64},{64,7... | collective-permute-start | bytes 11528 | tf_op jit(solution)/shard_map/ppermute | solution.py:20
  12.6 9.8 %collective-permute-start.1 = (bf16[3,256]{1,0:T(4,128)(2,1)S(1)}, bf16[3,256]{1,0:T(4,128)(2,1)S(1)}, u32[]{:S(2)}, u32[]{:S(2)}) collective-permute-start(bf16[3,256]{1,0:T(4,128)(2,1)S(1)} %slice.88), channel_id=1, source_target_pairs={{0,8},{8,16},{16,24},{24,32},{32,40},{40,48},{48,56},{56,64},{64,7... | collective-permute-start | bytes 4616 | tf_op jit(solution)/shard_map/ppermute | solution.py:20
  26.6 122.6 %copy-start.2 = (f32[10]{0:T(128)S(1)}, f32[10]{0:T(128)}, u32[]{:S(2)}) copy-start(f32[10]{0:T(128)} %param.21) | copy-start | bytes 124
  26.6 357.8 %all-gather.6.cloned.1.call-start = ((), (), s32[]{:S(2)}) async-start(), calls=%async_computation.2 | async-start | bytes 3328000 | tf_op jit(solution)/shard_map/all_gather | solution.py:105
  27.3 406.7 %reduce-scatter.2.cloned.1.call-start = ((), (), s32[]{:S(2)}) async-start(), calls=%async_computation.3 | async-start | bytes 2949120 | tf_op jit(solution)/shard_map/reduce_scatter | solution.py:108
  251.0 133.3 %copy-start.3 = (f32[640]{0:T(1024)S(1)}, f32[640]{0:T(1024)}, u32[]{:S(2)}) copy-start(f32[640]{0:T(1024)} %param.22) | copy-start | bytes 7684
Sparse Core Ops, SparseCore 0:
  26.7 222.2 all-gather.3
  251.9 132.4 all-gather.5
  390.2 43.7 reduce-scatter.1
where the time goes:
time: 444 us; the launch traced here: 441 us
  waiting for transfers between devices  259 us (58%)
  blocking collectives  131 us (30%)
  between operations  14.1 us (3%)
  matrix products  12.3 us (3%)
  local copies, waits for them, and re-layouts  8.95 us (2%)
  starting transfers between devices  7.99 us (2%)
  other arithmetic  7.25 us (2%)
    all_gather x1, waiting for transfers between devices, on_device(): lax.all_gather(out_weight, 'seq', axis=1, tiled=True)  120 us
    unnamed x1, blocking collectives  118 us
    all_gather x1, waiting for transfers between devices, carried_in(): gathered = jax.tree.map(lambda a: lax.all_gather(a, axis), part)  94.4 us
    reduce_scatter x1, waiting for transfers between devices, on_device(): lax.psum_scatter(partial_terms.astype(jnp.bfloat16), 'tp', scatter_dimens...  43.9 us
    psum x1, blocking collectives, on_device(): squares = lax.psum(jnp.sum(gated * gated, axis=1), 'tp')  12.8 us
  transfers between devices with their start and end apart: 5, of which 3 were waited for; matrix products, arithmetic and copies ran while one was open for 4% of the time, Pallas kernels for 0%

commit v1 on v0

v1 whole, which is shorter than its diff:
```python
import jax
import jax.numpy as jnp
from jax import lax
from jax.experimental import pallas as pl
from jax.experimental.pallas import tpu as pltpu
from jax.sharding import PartitionSpec as P

CHANNELS = 5120
HEADDIM = 64
STATE = 128
CONV = 4
CHUNK = 128
LANES = 128
RIM = 16
PAD_HEADS = 16
PIECE = 16
EPSILON = 1e-05
HIGH = lax.Precision.HIGHEST
F32 = jnp.float32
BF16 = jnp.bfloat16
MASKED = -1e30
INTERPRET = False

NT = (((1,), (1,)), ((), ()))
TN = (((0,), (0,)), ((), ()))
NN = (((1,), (0,)), ((), ()))


def dot(a, b, dims=NN, precision=None):
    return lax.dot_general(a, b, dims, precision=precision, preferred_element_type=F32)


def call(body, outs, flops, *args, scratch=()):
    moved = sum(a.size * a.dtype.itemsize for a in args) + sum(
        o.size * o.dtype.itemsize for o in outs
    )
    return pl.pallas_call(
        body,
        out_shape=outs,
        in_specs=[pl.BlockSpec(memory_space=pltpu.VMEM)] * len(args),
        out_specs=[pl.BlockSpec(memory_space=pltpu.VMEM)] * len(outs),
        scratch_shapes=list(scratch),
        compiler_params=pltpu.CompilerParams(vmem_limit_bytes=40 * 2**20),
        cost_estimate=pl.CostEstimate(flops=flops, bytes_accessed=moved, transcendentals=0),
        interpret=INTERPRET,
    )(*args)


def silu(v):
    half = 0.5 * v
    return half + half * jnp.tanh(half)


def split(v):
    hi = v.astype(BF16)
    return hi, (v - hi.astype(F32)).astype(BF16)


def iota(shape, dim):
    return lax.broadcasted_iota(jnp.int32, shape, dim)


def as_column(row):
    heads = row.shape[1]
    same = iota((PAD_HEADS, heads), 0) == iota((PAD_HEADS, heads), 1)
    return jnp.sum(jnp.where(same, row, 0.0), axis=1, keepdims=True)


def head_spread(width, dtype):
    return (iota((PAD_HEADS, width), 1) // HEADDIM == iota((PAD_HEADS, width), 0)).astype(dtype)


def spread_tokens(per_head, spread2):
    hi, lo = split(per_head)
    return dot(jnp.concatenate([hi, lo], axis=0), spread2, TN)


def spread_row(column, spread_f32):
    return jnp.sum(spread_f32 * column, axis=0, keepdims=True)


def conv_silu(rim, value, taps_ref, scratch, out_ref):
    rows, width = value.shape
    scratch[0:8, :] = rim[RIM - 8 :, :].astype(F32)
    scratch[8 : 8 + rows, :] = value[...].astype(F32)
    first = 8 - (CONV - 1)
    for at in range(0, rows, CHUNK):
        total = taps_ref[0:1, :] * scratch[first + at : first + at + CHUNK, :]
        for k in range(1, CONV):
            total += taps_ref[k : k + 1, :] * scratch[first + at + k : first + at + k + CHUNK, :]
        out_ref[at : at + CHUNK, :] = silu(total).astype(BF16)


def front_kernel(
    x_ref, bc_ref, rim_ref, dt_ref, tap_x_ref, tap_bc_ref, bias_ref, alog_ref,
    xc_ref, bcc_ref, cum_ref, logstep_ref, piece_ref, x_scr, bc_scr, piece_scr,
):
    tokens, width = x_ref.shape
    heads = dt_ref.shape[1]
    rim = rim_ref[...]
    conv_silu(rim[:, :width], x_ref, tap_x_ref, x_scr, xc_ref)
    conv_silu(rim[:, width:], bc_ref, tap_bc_ref, bc_scr, bcc_ref)

    eye = (iota((PAD_HEADS, heads), 0) == iota((PAD_HEADS, heads), 1)).astype(BF16)
    logits = dot(eye, dt_ref[...], NT) + as_column(bias_ref[...])
    small = jnp.exp(-jnp.abs(logits))
    series = small * (1.0 - small * (0.5 - small * (1.0 / 3.0 - small * 0.25)))
    step = jnp.maximum(logits, 0.0) + jnp.where(small < 0.015625, series, jnp.log(1.0 + small))
    logstep = jnp.log(step)
    rate = -jnp.exp(as_column(alog_ref[...])) * step

    upto = (iota((CHUNK, CHUNK), 0) <= iota((CHUNK, CHUNK), 1)).astype(F32)
    run = jnp.zeros((PAD_HEADS, 1), F32)
    sums = []
    for at in range(0, tokens, CHUNK):
        within = dot(rate[:, at : at + CHUNK], upto, precision=HIGH) + run
        run = within[:, CHUNK - 1 :]
        sums.append(within)
    cum = jnp.concatenate(sums, axis=1)
    cum_ref[...] = cum
    logstep_ref[...] = logstep

    spread = head_spread(width, BF16)
    spread2 = jnp.concatenate([spread, spread], axis=0)
    tail = spread_tokens(jnp.exp(run - cum + logstep), spread2)
    fed = (xc_ref[...].astype(F32) * tail).astype(BF16)
    state = dot(bcc_ref[:, :STATE], fed, TN)

    spread_f = head_spread(width, F32)
    hi, lo = split(run)
    even = iota((1, width), 1) % 2 == 0
    decay = jnp.where(
        even, spread_row(hi.astype(F32), spread_f), spread_row(lo.astype(F32), spread_f)
    )
    half = STATE // 2
    blocks = width // LANES
    for b in range(blocks):
        cols = slice(b * LANES, (b + 1) * LANES)
        piece_scr[pl.ds(b, half, PIECE), :] = state[:half, cols]
        piece_scr[pl.ds(blocks + b, half, PIECE), :] = state[half:, cols]
        piece_scr[pl.ds(2 * blocks + b, half, PIECE), :] = jnp.broadcast_to(
            decay[:, cols], (half, LANES)
        )
    piece_scr[pl.ds(3 * blocks, half, PIECE), :] = jnp.zeros((half, LANES), F32)
    piece_ref[...] = piece_scr[...].astype(BF16)


def local_kernel(
    xc_ref, bcc_ref, cum_ref, logstep_ref, z_ref, skip_ref, own_ref, reach_ref, held,
):
    tokens, width = xc_ref.shape
    spread = head_spread(width, BF16)
    spread2 = jnp.concatenate([spread, spread], axis=0)
    spread_f = head_spread(width, F32)
    skip = spread_row(as_column(skip_ref[...]), spread_f)
    causal = iota((CHUNK, CHUNK), 0) >= iota((CHUNK, CHUNK), 1)
    left = iota((CHUNK, LANES), 1) < HEADDIM
    held[...] = jnp.zeros_like(held)
    before = jnp.zeros((PAD_HEADS, 1), F32)
    for at in range(0, tokens, CHUNK):
        rows = slice(at, at + CHUNK)
        b_part, c_part = bcc_ref[rows, :STATE], bcc_ref[rows, STATE:]
        cum = cum_ref[:, rows]
        source = logstep_ref[:, rows] - cum
        cum_cols = cum.T
        last = cum[:, CHUNK - 1 :]
        cb = dot(c_part, b_part, NT)
        gate = silu(z_ref[rows, :].astype(F32))
        reach_ref[rows, :] = spread_tokens(jnp.exp(cum), spread2) * gate
        fresh = spread_tokens(jnp.exp(cum - before), spread2)
        carried = dot(c_part, held[...].astype(BF16)) * fresh
        for pair in range(width // LANES):
            cols = slice(pair * LANES, (pair + 1) * LANES)
            mixes = []
            for head in (2 * pair, 2 * pair + 1):
                power = cum_cols[:, head : head + 1] + source[head : head + 1, :]
                mixes.append((cb * jnp.exp(jnp.where(causal, power, MASKED))).astype(BF16))
            x_part = xc_ref[rows, cols]
            blank = jnp.zeros_like(x_part)
            x_two = jnp.concatenate(
                [jnp.where(left, x_part, blank), jnp.where(left, blank, x_part)], axis=0
            )
            y = dot(jnp.concatenate(mixes, axis=1), x_two) + carried[:, cols]
            y += skip[:, cols] * x_part.astype(F32)
            own_ref[rows, cols] = y * gate[:, cols]
        if at + CHUNK < tokens:
            tail = spread_tokens(jnp.exp(last + source), spread2)
            fed = (xc_ref[rows, :].astype(F32) * tail).astype(BF16)
            kept = spread_row(jnp.exp(last - before), spread_f)
            held[...] = held[...] * kept + dot(b_part, fed, TN)
            before = last


def scan_kernel(blocks, in_ref, out_ref, wide):
    count = in_ref.shape[0] // PIECE
    wide[...] = in_ref[...].astype(F32)
    even = iota((blocks, LANES), 1) % 2 == 0
    low = jnp.zeros((blocks, LANES), F32)
    high = jnp.zeros((blocks, LANES), F32)
    for place in range(count):
        at = place * PIECE
        part = wide[at : at + blocks, :]
        part_high = wide[at + blocks : at + 2 * blocks, :]
        wide_decay = wide[at + 2 * blocks : at + 3 * blocks, :]
        other = jnp.where(
            even, pltpu.roll(wide_decay, LANES - 1, 1), pltpu.roll(wide_decay, 1, 1)
        )
        kept = jnp.exp(wide_decay + other)
        wide[at : at + blocks, :] = low
        wide[at + blocks : at + 2 * blocks, :] = high
        low = kept * low + part
        high = kept * high + part_high
    out_ref[...] = wide[...].astype(BF16)


def back_kernel(
    own_ref, reach_ref, c_ref, piece_ref, w_ref, gain_ref, place_ref, out_ref, wide, state, gated,
):
    tokens, width = own_ref.shape
    blocks = width // LANES
    half = STATE // 2
    wide[...] = piece_ref[...].astype(F32)
    for b in range(blocks):
        cols = slice(b * LANES, (b + 1) * LANES)
        state[:half, cols] = wide[pl.ds(b, half, PIECE), :]
        state[half:, cols] = wide[pl.ds(blocks + b, half, PIECE), :]
    incoming = state[...].astype(BF16)
    ones = jnp.ones((16, 2 * width), BF16)
    totals = []
    for at in range(0, tokens, CHUNK):
        rows = slice(at, at + CHUNK)
        y = own_ref[rows, :] + reach_ref[rows, :] * dot(c_ref[rows, STATE:], incoming)
        gated[rows, :] = (y * gain_ref[...]).astype(BF16)
        hi, lo = split(y * y)
        totals.append(dot(ones, jnp.concatenate([hi, lo], axis=1), NT))
    hi, lo = split(jnp.concatenate(totals, axis=1))
    row = iota((16, tokens), 0)
    mine = 2 * place_ref[0, 0]
    zero = jnp.zeros((16, tokens), F32)
    squares = jnp.where(
        row == mine, hi.astype(F32), jnp.where(row == mine + 1, lo.astype(F32), zero)
    ).astype(BF16)
    targets = 8
    each = w_ref.shape[0] // targets
    for d in range(targets):
        to = d * (each + 16)
        out_ref[to : to + each, :] = dot(
            w_ref[d * each : (d + 1) * each, :], gated[...], NT
        ).astype(BF16)
        out_ref[to + each : to + each + 16, :] = squares


def scale_kernel(in_ref, out_ref):
    each = out_ref.shape[1]
    total = jnp.sum(in_ref[each:, :].astype(F32), axis=0, keepdims=True)
    scale = lax.rsqrt(total / CHANNELS + EPSILON)
    out_ref[...] = (in_ref[:each, :].astype(F32) * scale).T.astype(BF16)


def front(x_in, bc_in, rim, dt_in, conv_x, conv_bc, dt_bias, a_log):
    tokens, width = x_in.shape
    return call(
        front_kernel,
        [
            jax.ShapeDtypeStruct((tokens, width), BF16),
            jax.ShapeDtypeStruct((tokens, 2 * STATE), BF16),
            jax.ShapeDtypeStruct((PAD_HEADS, tokens), F32),
            jax.ShapeDtypeStruct((PAD_HEADS, tokens), F32),
            jax.ShapeDtypeStruct((STATE // 2 * PIECE, LANES), BF16),
        ],
        2 * tokens * width * STATE,
        x_in, bc_in, rim, dt_in, conv_x, conv_bc, dt_bias[None], a_log[None],
        scratch=(
            pltpu.VMEM((tokens + 8, width), F32),
            pltpu.VMEM((tokens + 8, 2 * STATE), F32),
            pltpu.VMEM((STATE // 2 * PIECE, LANES), F32),
        ),
    )


def local(xc, bcc, cum, logstep, z_gate, d_skip):
    tokens, width = xc.shape
    return call(
        local_kernel,
        [jax.ShapeDtypeStruct((tokens, width), F32)] * 2,
        6 * tokens * width * STATE,
        xc, bcc, cum, logstep, z_gate, d_skip[None],
        scratch=(pltpu.VMEM((STATE, width), F32),),
    )


def scan(pieces, width):
    def body(*refs):
        scan_kernel(width // LANES, *refs)

    return call(
        body,
        [jax.ShapeDtypeStruct(pieces.shape, BF16)],
        pieces.size * 4,
        pieces,
        scratch=(pltpu.VMEM(pieces.shape, F32),),
    )[0]


def back(own, reach, bcc, pieces, weight, norm_gain, place):
    tokens, width = own.shape
    columns = weight.shape[0]
    return pl.pallas_call(
        back_kernel,
        out_shape=jax.ShapeDtypeStruct((columns + 8 * 16, tokens), BF16),
        in_specs=[pl.BlockSpec(memory_space=pltpu.VMEM)] * 6
        + [pl.BlockSpec(memory_space=pltpu.SMEM)],
        out_specs=pl.BlockSpec(memory_space=pltpu.VMEM),
        scratch_shapes=[
            pltpu.VMEM(pieces.shape, F32),
            pltpu.VMEM((STATE, width), F32),
            pltpu.VMEM((tokens, width), BF16),
        ],
        compiler_params=pltpu.CompilerParams(vmem_limit_bytes=40 * 2**20),
        cost_estimate=pl.CostEstimate(
            flops=2 * tokens * width * (columns + STATE), bytes_accessed=10**7, transcendentals=0
        ),
        interpret=INTERPRET,
    )(own, reach, bcc, pieces, weight, norm_gain[None], place)


def scaled(summed):
    rows, tokens = summed.shape
    return call(
        scale_kernel, [jax.ShapeDtypeStruct((tokens, rows - 16), BF16)], rows * tokens, summed
    )[0]


def on_device(
    x_in, bc_in, z_gate, dt_in, conv_x, conv_bc, dt_bias, a_log, d_skip, norm_gain, out_weight
):
    tokens, width = x_in.shape
    count = lax.axis_size("seq")
    rim = jnp.concatenate([x_in[tokens - RIM :], bc_in[tokens - RIM :]], axis=1)
    rim = lax.ppermute(rim, "seq", [(i, i + 1) for i in range(count - 1)])
    weight = lax.all_gather(out_weight.T, "seq", axis=0, tiled=True)
    xc, bcc, cum, logstep, pieces = front(
        x_in, bc_in, rim, dt_in, conv_x, conv_bc, dt_bias, a_log
    )
    pieces = lax.all_to_all(pieces, "seq", 0, 0, tiled=True)
    own, reach = local(xc, bcc, cum, logstep, z_gate, d_skip)
    pieces = lax.all_to_all(scan(pieces, width), "seq", 0, 0, tiled=True)
    place = lax.axis_index("tp").astype(jnp.int32).reshape(1, 1)
    partial = back(own, reach, bcc, pieces, weight, norm_gain, place)
    return scaled(lax.psum_scatter(partial, "tp", scatter_dimension=0, tiled=True))


def solution(mesh):
    in_specs = (
        P("seq", "tp"),
        P("seq", None),
        P("seq", "tp"),
        P("seq", "tp"),
        P(None, "tp"),
        P(),
        P("tp"),
        P("tp"),
        P("tp"),
        P("tp"),
        P("tp", "seq"),
    )
    return jax.shard_map(
        on_device, mesh=mesh, in_specs=in_specs, out_specs=P("seq", "tp"), check_vma=False
    )
```

time: 444 us -> 215 us (0.48)
  waiting for transfers between devices: 259 us -> 125 us
  blocking collectives: 131 us -> 38 us
  matrix products: 12.3 us -> 0 us
  Pallas kernels: 0 us -> 10.8 us
  other arithmetic: 7.25 us -> 0.01 us
  starting transfers between devices: 7.99 us -> 13.5 us
    all_gather x2 -> x1, waiting for transfers between devices: 214 us -> 64.6 us  [on_device(): weight = lax.all_gather(out_weight.T, 'seq', axis=0, tiled=True)]
    unnamed x1 -> x0, blocking collectives: 118 us -> none
    all_to_all x0 -> x1, blocking collectives: none -> 38 us  [on_device(): pieces = lax.all_to_all(pieces, 'seq', 0, 0, tiled=True)]
    all_to_all x0 -> x1, waiting for transfers between devices: none -> 15 us  [on_device(): pieces = lax.all_to_all(scan(pieces, width), 'seq', 0, 0, tiled=True)]
    psum x1 -> x0, blocking collectives: 12.8 us -> none  [on_device(): squares = lax.psum(jnp.sum(gated * gated, axis=1), 'tp')]
    dot_general x6 -> x0, matrix products: 12.3 us -> none  [the longest x1 5.71 us: on_device(): jnp.dot(normed, lax.all_gather(out_weight, 'seq', axis=1, tiled=True), pr...]
    pallas_call x0 -> x5, Pallas kernels: none -> 10.8 us  [the longest x4 6.2 us: call(): pl.pallas_call(body, out_shape=outs, in_specs=[pl.BlockSpec(memory_space=...]
    all_to_all x0 -> x1, starting transfers between devices: none -> 9.06 us  [on_device(): pieces = lax.all_to_all(scan(pieces, width), 'seq', 0, 0, tiled=True)]
  transfers between devices with their start and end apart: 5 -> 4, of which waited for: 3 -> 4; matrix products, arithmetic and copies ran while one was open for 4% -> 1% of each run, Pallas kernels for 0% -> 3%
where the time goes in v1:
time: 215 us; the launch traced here: 213 us
  waiting for transfers between devices  125 us (58%)
  blocking collectives  38 us (18%)
  starting transfers between devices  13.5 us (6%)
  between operations  13.5 us (6%)
  local copies, waits for them, and re-layouts  13 us (6%)
  Pallas kernels  10.8 us (5%)
    all_gather x1, waiting for transfers between devices, on_device(): weight = lax.all_gather(out_weight.T, 'seq', axis=0, tiled=True)  64.6 us
    reduce_scatter x1, waiting for transfers between devices, on_device(): lax.psum_scatter(partial, 'tp', scatter_dimension=0, tiled=True)  44.2 us
    all_to_all x1, blocking collectives, on_device(): pieces = lax.all_to_all(pieces, 'seq', 0, 0, tiled=True)  38 us
    all_to_all x1, waiting for transfers between devices, on_device(): pieces = lax.all_to_all(scan(pieces, width), 'seq', 0, 0, tiled=True)  15 us
    unnamed x27, local copies, waits for them, and re-layouts  10.7 us
    all_to_all x1, starting transfers between devices, on_device(): pieces = lax.all_to_all(scan(pieces, width), 'seq', 0, 0, tiled=True)  9.06 us
    pallas_call x4, Pallas kernels, call(): pl.pallas_call(body, out_shape=outs, in_specs=[pl.BlockSpec(memory_space=...  6.2 us
    pallas_call x1, Pallas kernels, back(): pl.pallas_call(back_kernel, out_shape=jax.ShapeDtypeStruct((columns + 8 *...  4.59 us
  transfers between devices with their start and end apart: 4, of which 4 were waited for; matrix products, arithmetic and copies ran while one was open for 1% of the time, Pallas kernels for 3%

profile of v1, /device:TPU:1, one launch (start us, length us, event | category | flops | bytes accessed | tf_op | source)
XLA Modules:
  0.0 213.4 jit_solution(16641090715936646730)
XLA Ops:
  6.5 0.7 all-gather.2.cloned.1.call-update
  7.3 0.7 slice.7
  8.0 0.7 slice.6
  8.7 4.4 %collective-permute-start = (bf16[16,896]{1,0:T(8,128)(2,1)S(1)}, bf16[16,896]{1,0:T(8,128)(2,1)S(1)}, u32[]{:S(2)}, u32[]{:S(2)}) collective-permute-start(bf16[16,896]{1,0:T(8,128)(2,1)S(1)} %pad_maximum_fusion), channel_id=1, source_target_pairs={{0,8},{8,16},{16,24},{24,32},{32,40},{40,48},{48,56},{56,64},{64,7... | collective-permute-start | bytes 86024 | tf_op jit(solution)/shard_map/ppermute | solution.py:340
  13.1 0.9 copy.12.dt_ref
  13.9 0.1 collective-permute-done.rim_ref
  14.0 1.1 copy-done.1
  15.1 0.9 copy-done.6
  16.1 0.7 copy-done.7
  16.8 0.7 copy-done.8
  17.5 0.7 copy-done.9
  18.1 0.7 copy-done.10
  18.8 2.9 %shard_map.109 = (bf16[512,640]{1,0:T(8,128)(2,1)S(1)}, bf16[512,256]{1,0:T(8,128)(2,1)S(1)}, f32[16,512]{1,0:T(8,128)S(1)}, f32[16,512]{1,0:T(8,128)S(1)}, bf16[1024,128]{1,0:T(8,128)(2,1)S(1)}) custom-call(bf16[512,640]{1,0:T(8,128)(2,1)S(1)} %copy-done.1, bf16[512,256]{1,0:T(8,128)(2,1)S(1)} %copy-done.6, ...), custom_call_target="tpu_custom_call" | custom-call | flops 83886080 | bytes 2216016 | tf_op jit(solution)/shard_map/pallas_call | solution.py:37
  21.7 38.0 %all_to_all.22 = bf16[64,16,128]{2,1,0:T(8,128)(2,1)S(1)} all-to-all(bf16[64,16,128]{2,1,0:T(8,128)(2,1)S(1)} %bitcast.11), channel_id=1, replica_groups=mesh['seq'=64,'tp'=8] {'seq'}, dimensions={0} | all-to-all | bytes 524288 | tf_op jit(solution)/shard_map/all_to_all | solution.py:345
  59.7 1.0 shard_map.111
  60.7 9.1 %all-to-all-start.1 = ((bf16[64,16,128]{2,1,0:T(8,128)(2,1)}), bf16[64,16,128]{2,1,0:T(8,128)(2,1)S(1)}, u32[]{:S(2)}, u32[]{:S(2)}) async-start(bf16[64,16,128]{2,1,0:T(8,128)(2,1)} %bitcast.5), calls=%async_computation.1 | async-start | bytes 524288 | tf_op jit(solution)/shard_map/all_to_all | solution.py:347
  69.7 0.0 reduce-scatter.2.cloned.1.call-start
  69.8 0.0 copy-done.12
  69.8 0.0 copy-done.11
  69.8 0.0 copy-start.2
  69.8 1.1 copy-done.2
  70.9 1.1 copy-done.4
  72.0 2.1 %shard_map.110 = (f32[512,640]{1,0:T(8,128)S(1)}, f32[512,640]{1,0:T(8,128)S(1)}) custom-call(bf16[512,640]{1,0:T(8,128)(2,1)S(1)} %copy-done.4, bf16[512,256]{1,0:T(8,128)(2,1)S(1)} %get-tuple-element.13.bcc_ref.c_ref, f32[16,512]{1,0:T(8,128)S(1)} %get-tuple-element.14.cum_ref, f32[16,512]{1,0:T(8,128)S(1)} %get-tuple-element.15.logstep_ref, ...), custom_call_target="tpu_custom_call" | custom-call | flops 251658240 | bytes 4259880 | tf_op jit(solution)/shard_map/pallas_call | solution.py:37
  74.1 15.0 %all-to-all-done.1 = bf16[64,16,128]{2,1,0:T(8,128)(2,1)S(1)} async-done(((bf16[64,16,128]{2,1,0:T(8,128)(2,1)}), bf16[64,16,128]{2,1,0:T(8,128)(2,1)S(1)}, u32[]{:S(2)}, u32[]{:S(2)}) %all-to-all-start.1) | async-done | bytes 262176 | tf_op jit(solution)/shard_map/all_to_all | solution.py:347
  89.1 64.6 %all-gather.2.cloned.1.call-done.w_ref = bf16[2560,640]{1,0:T(8,128)(2,1)} async-done(((bf16[40,640]{1,0:T(8,128)(2,1)}), bf16[2560,640]{1,0:T(8,128)(2,1)}) %all-gather.2.cloned.1.call-update) | async-done | bytes 3276816 | tf_op jit(solution)/shard_map/all_gather | solution.py:341
  153.7 1.9 copy-done
  155.7 4.6 %shard_map.112 = bf16[2688,512]{1,0:T(8,128)(2,1)} custom-call(f32[512,640]{1,0:T(8,128)S(1)} %get-tuple-element.16.own_ref, f32[512,640]{1,0:T(8,128)S(1)} %get-tuple-element.17.reach_ref, bf16[512,256]{1,0:T(8,128)(2,1)S(1)} %get-tuple-element.13.bcc_ref.c_ref, bf16[1024,128]{1,0:T(8,128)(2,1)S(1)} %bitcast.9, bf16[2560,640]{1,0:T(8,128)(2,1)S(1)} %copy-done, ...), custom_call_target="tpu_custom_call" | custom-call | flops 1761607680 | bytes 10000000 | tf_op jit(solution)/shard_map/pallas_call | solution.py:308
  160.3 0.0 reduce-scatter.2.cloned.1.call-update
  160.3 44.2 %reduce-scatter.2.cloned.1.call-done.in_ref = bf16[336,512]{1,0:T(8,128)(2,1)} async-done(((bf16[2688,512]{1,0:T(8,128)(2,1)}), bf16[336,512]{1,0:T(8,128)(2,1)}) %reduce-scatter.2.cloned.1.call-update) | async-done | bytes 344080 | tf_op jit(solution)/shard_map/reduce_scatter | solution.py:350
  204.5 1.0 copy-done.5
  205.5 0.2 shard_map.113
  205.7 0.9 copy.13
  (16 shorter events, 0.0 us)
Async XLA Ops:
  6.5 63.2 %copy-start.12 = (f32[640]{0:T(1024)S(1)}, f32[640]{0:T(1024)}, u32[]{:S(2)}) copy-start(f32[640]{0:T(1024)} %param.20) | copy-start | bytes 7684
  6.5 63.3 %copy-start.11 = (f32[10]{0:T(128)S(1)}, f32[10]{0:T(128)}, u32[]{:S(2)}) copy-start(f32[10]{0:T(128)} %param.19) | copy-start | bytes 124
  6.5 147.2 %all-gather.2.cloned.1.call-start = ((), (), s32[]{:S(2)}) async-start(), calls=%async_computation.3 | async-start | bytes 3328000 | tf_op jit(solution)/shard_map/all_gather | solution.py:341
  8.7 5.3 %collective-permute-start = (bf16[16,896]{1,0:T(8,128)(2,1)S(1)}, bf16[16,896]{1,0:T(8,128)(2,1)S(1)}, u32[]{:S(2)}, u32[]{:S(2)}) collective-permute-start(bf16[16,896]{1,0:T(8,128)(2,1)S(1)} %pad_maximum_fusion), channel_id=1, source_target_pairs={{0,8},{8,16},{16,24},{24,32},{32,40},{40,48},{48,56},{56,64},{64,7... | collective-permute-start | bytes 86024 | tf_op jit(solution)/shard_map/ppermute | solution.py:340
  14.0 1.1 copy-start.1
  15.1 0.9 copy-start.6
  16.1 0.7 copy-start.7
  16.8 0.7 copy-start.8
  17.5 0.7 copy-start.9
  18.1 0.7 copy-start.10
  21.7 39.0 %copy-start.3 = (bf16[512,640]{1,0:T(8,128)(2,1)}, bf16[512,640]{1,0:T(8,128)(2,1)S(1)}, u32[]{:S(2)}) copy-start(bf16[512,640]{1,0:T(8,128)(2,1)S(1)} %get-tuple-element.12.xc_ref) | copy-start | bytes 1966084
  60.7 28.5 %all-to-all-start.1 = ((bf16[64,16,128]{2,1,0:T(8,128)(2,1)}), bf16[64,16,128]{2,1,0:T(8,128)(2,1)S(1)}, u32[]{:S(2)}, u32[]{:S(2)}) async-start(bf16[64,16,128]{2,1,0:T(8,128)(2,1)} %bitcast.5), calls=%async_computation.1 | async-start | bytes 524288 | tf_op jit(solution)/shard_map/all_to_all | solution.py:347
  69.7 134.8 %reduce-scatter.2.cloned.1.call-start = ((), (), s32[]{:S(2)}) async-start(), calls=%async_computation.4 | async-start | bytes 3096576 | tf_op jit(solution)/shard_map/reduce_scatter | solution.py:350
  69.8 1.1 copy-start.2
  70.9 1.1 copy-start.4
  153.7 1.9 copy-start
  204.5 1.0 copy-start.5
Sparse Core Ops, SparseCore 0:
  10.3 143.3 all-gather.1
  160.4 44.0 reduce-scatter.1

commit v2 on v1

v2 whole, which is shorter than its diff:
```python
import jax
import jax.numpy as jnp
from jax import lax
from jax.experimental import pallas as pl
from jax.experimental.pallas import tpu as pltpu
from jax.sharding import PartitionSpec as P

CHANNELS = 5120
HEADDIM = 64
STATE = 128
CONV = 4
CHUNK = 128
LANES = 128
RIM = 16
PAD_HEADS = 16
Z_RING = 16
PIECE = 48
EPSILON = 1e-05
HIGH = lax.Precision.HIGHEST
F32 = jnp.float32
BF16 = jnp.bfloat16
MASKED = -1e30
INTERPRET = False

NT = (((1,), (1,)), ((), ()))
TN = (((0,), (0,)), ((), ()))
NN = (((1,), (0,)), ((), ()))


def dot(a, b, dims=NN, precision=None):
    return lax.dot_general(a, b, dims, precision=precision, preferred_element_type=F32)


def call(body, outs, flops, *args, scratch=(), spaces=None):
    spaces = spaces or [pltpu.VMEM] * len(args)
    moved = sum(a.size * a.dtype.itemsize for a in args) + sum(
        o.size * o.dtype.itemsize for o in outs
    )
    return pl.pallas_call(
        body,
        out_shape=outs,
        in_specs=[pl.BlockSpec(memory_space=space) for space in spaces],
        out_specs=[pl.BlockSpec(memory_space=pltpu.VMEM)] * len(outs),
        scratch_shapes=list(scratch),
        compiler_params=pltpu.CompilerParams(vmem_limit_bytes=40 * 2**20),
        cost_estimate=pl.CostEstimate(flops=flops, bytes_accessed=moved, transcendentals=0),
        interpret=INTERPRET,
    )(*args)


def silu(v):
    half = 0.5 * v
    return half + half * jnp.tanh(half)


def split(v):
    hi = v.astype(BF16)
    return hi, (v - hi.astype(F32)).astype(BF16)


def iota(shape, dim):
    return lax.broadcasted_iota(jnp.int32, shape, dim)


def as_column(row):
    heads = row.shape[1]
    same = iota((PAD_HEADS, heads), 0) == iota((PAD_HEADS, heads), 1)
    return jnp.sum(jnp.where(same, row, 0.0), axis=1, keepdims=True)


def head_spread(width, dtype):
    return (iota((PAD_HEADS, width), 1) // HEADDIM == iota((PAD_HEADS, width), 0)).astype(dtype)


def spread_tokens(per_head, spread2):
    hi, lo = split(per_head)
    return dot(jnp.concatenate([hi, lo], axis=0), spread2, TN)


def spread_row(column, spread_f32):
    return jnp.sum(spread_f32 * column, axis=0, keepdims=True)


def fetch(sems, *pairs):
    copies = [pltpu.make_async_copy(a, b, sems.at[i]) for i, (a, b) in enumerate(pairs)]
    for copy in copies:
        copy.start()
    return copies


def conv_silu(padded, taps_ref, at, rows):
    first = 8 - (CONV - 1) + at
    total = taps_ref[0:1, :] * padded[first : first + rows, :]
    for k in range(1, CONV):
        total += taps_ref[k : k + 1, :] * padded[first + k : first + k + rows, :]
    return silu(total).astype(BF16)


def front_kernel(
    x_hbm, bc_hbm, dt_hbm, tap_x_hbm, tap_bc_hbm, bias_hbm, alog_hbm,
    xc_ref, bcc_ref, cum_ref, logstep_ref, state_ref, tail_ref,
    x_ref, bc_ref, dt_ref, tap_x_ref, tap_bc_ref, bias_ref, alog_ref,
    x_scr, bc_scr, logit_scr, fed_scr, sems,
):
    copies = fetch(
        sems, (dt_hbm, dt_ref), (bias_hbm, bias_ref), (alog_hbm, alog_ref), (bc_hbm, bc_ref),
        (tap_bc_hbm, tap_bc_ref), (tap_x_hbm, tap_x_ref), (x_hbm, x_ref),
    )
    tokens, width = x_ref.shape
    heads = dt_ref.shape[0]
    for copy in copies[:3]:
        copy.wait()
    logit_scr[...] = jnp.zeros_like(logit_scr)
    logit_scr[0:heads, :] = dt_ref[...].astype(F32)
    logits = logit_scr[...] + as_column(bias_ref[...])
    small = jnp.exp(-jnp.abs(logits))
    series = small * (1.0 - small * (0.5 - small * (1.0 / 3.0 - small * 0.25)))
    step = jnp.maximum(logits, 0.0) + jnp.where(small < 0.015625, series, jnp.log(1.0 + small))
    logstep = jnp.log(step)
    rate = -jnp.exp(as_column(alog_ref[...])) * step
    upto = (iota((CHUNK, CHUNK), 0) <= iota((CHUNK, CHUNK), 1)).astype(F32)
    run = jnp.zeros((PAD_HEADS, 1), F32)
    sums = []
    for at in range(0, tokens, CHUNK):
        within = dot(rate[:, at : at + CHUNK], upto, precision=HIGH) + run
        run = within[:, CHUNK - 1 :]
        sums.append(within)
    cum = jnp.concatenate(sums, axis=1)
    cum_ref[...] = cum
    logstep_ref[...] = logstep
    spread = head_spread(width, BF16)
    tail = spread_tokens(jnp.exp(run - cum + logstep), jnp.concatenate([spread, spread], axis=0))
    tail_ref[...] = tail[:RIM, :]

    for copy in copies[3:]:
        copy.wait()
    bc_scr[0:8, :] = jnp.zeros((8, bc_scr.shape[1]), F32)
    bc_scr[8:, :] = bc_ref[...].astype(F32)
    x_scr[0:8, :] = jnp.zeros((8, width), F32)
    x_scr[8:, :] = x_ref[...].astype(F32)
    for at in range(0, tokens, CHUNK):
        rows = slice(at, at + CHUNK)
        bcc_ref[rows, :] = conv_silu(bc_scr, tap_bc_ref, at, CHUNK)
        xc = conv_silu(x_scr, tap_x_ref, at, CHUNK)
        xc_ref[rows, :] = xc
        fed_scr[rows, :] = (xc.astype(F32) * tail[rows, :]).astype(BF16)
    fed_scr[0:RIM, :] = jnp.zeros((RIM, width), BF16)
    state_ref[...] = dot(bcc_ref[:, :STATE], fed_scr[...], TN)


def pack_decay(total, width):
    spread = head_spread(width, F32)
    hi, lo = split(total)
    even = iota((1, width), 1) % 2 == 0
    return jnp.where(even, spread_row(hi.astype(F32), spread), spread_row(lo.astype(F32), spread))


def rim_kernel(
    rim_ref, x_hbm, bc_hbm, tap_x_hbm, tap_bc_hbm, cum_ref, tail_ref, state_ref,
    xc_ref, bcc_ref, piece_ref, x_ref, bc_ref, tap_x_ref, tap_bc_ref, x_scr, bc_scr, piece_scr, sems,
):
    copies = fetch(
        sems, (x_hbm.at[0:RIM, :], x_ref), (bc_hbm.at[0:RIM, :], bc_ref),
        (tap_x_hbm, tap_x_ref), (tap_bc_hbm, tap_bc_ref),
    )
    width = x_ref.shape[1]
    rim = rim_ref[...].astype(F32)
    x_scr[0:8, :] = rim[RIM - 8 :, :width]
    bc_scr[0:8, :] = rim[RIM - 8 :, width:]
    last = cum_ref.shape[1] - 1
    decay = pack_decay(cum_ref[:, last:], width)
    for copy in copies:
        copy.wait()
    x_scr[8:, :] = x_ref[...].astype(F32)
    bc_scr[8:, :] = bc_ref[...].astype(F32)
    xc = conv_silu(x_scr, tap_x_ref, 0, RIM)
    bcc = conv_silu(bc_scr, tap_bc_ref, 0, RIM)
    xc_ref[...] = xc
    bcc_ref[...] = bcc
    fed = (xc.astype(F32) * tail_ref[...]).astype(BF16)
    state = state_ref[...] + dot(bcc[:, :STATE], fed, TN)
    each = STATE // Z_RING
    blocks = width // LANES
    for j in range(Z_RING):
        for b in range(blocks):
            at = j * PIECE + b * each
            piece_scr[at : at + each, :] = state[
                j * each : (j + 1) * each, b * LANES : (b + 1) * LANES
            ]
        at = j * PIECE + blocks * each
        piece_scr[at : at + 8, :] = jnp.zeros((8, LANES), F32)
        for b in range(blocks):
            piece_scr[at + b : at + b + 1, :] = decay[:, b * LANES : (b + 1) * LANES]
    piece_ref[...] = piece_scr[...].astype(BF16)


def local_kernel(
    xc_ref, xc_rim_ref, bcc_ref, bcc_rim_ref, cum_ref, logstep_ref, z_hbm, skip_hbm,
    own_ref, reach_ref, c_ref, held, xs, bs, z_ref, skip_ref, sems,
):
    copies = fetch(sems, (skip_hbm, skip_ref), (z_hbm, z_ref))
    tokens, width = xc_ref.shape
    xs[...] = xc_ref[...]
    xs[0:RIM, :] = xc_rim_ref[...]
    bs[...] = bcc_ref[...]
    bs[0:RIM, :] = bcc_rim_ref[...]
    c_ref[...] = bs[:, STATE:]
    spread = head_spread(width, BF16)
    spread2 = jnp.concatenate([spread, spread], axis=0)
    spread_f = head_spread(width, F32)
    causal = iota((CHUNK, CHUNK), 0) >= iota((CHUNK, CHUNK), 1)
    left = iota((CHUNK, LANES), 1) < HEADDIM
    held[...] = jnp.zeros_like(held)
    before = jnp.zeros((PAD_HEADS, 1), F32)
    for copy in copies:
        copy.wait()
    skip = spread_row(as_column(skip_ref[...]), spread_f)
    for at in range(0, tokens, CHUNK):
        rows = slice(at, at + CHUNK)
        b_part, c_part = bs[rows, :STATE], bs[rows, STATE:]
        cum = cum_ref[:, rows]
        source = logstep_ref[:, rows] - cum
        cum_cols = cum.T
        last = cum[:, CHUNK - 1 :]
        cb = dot(c_part, b_part, NT)
        gate = silu(z_ref[rows, :].astype(F32))
        reach_ref[rows, :] = spread_tokens(jnp.exp(cum), spread2) * gate
        fresh = spread_tokens(jnp.exp(cum - before), spread2)
        carried = dot(c_part, held[...].astype(BF16)) * fresh
        for pair in range(width // LANES):
            cols = slice(pair * LANES, (pair + 1) * LANES)
            mixes = []
            for head in (2 * pair, 2 * pair + 1):
                power = cum_cols[:, head : head + 1] + source[head : head + 1, :]
                mixes.append((cb * jnp.exp(jnp.where(causal, power, MASKED))).astype(BF16))
            x_part = xs[rows, cols]
            blank = jnp.zeros_like(x_part)
            x_two = jnp.concatenate(
                [jnp.where(left, x_part, blank), jnp.where(left, blank, x_part)], axis=0
            )
            y = dot(jnp.concatenate(mixes, axis=1), x_two) + carried[:, cols]
            y += skip[:, cols] * x_part.astype(F32)
            own_ref[rows, cols] = y * gate[:, cols]
        if at + CHUNK < tokens:
            tail = spread_tokens(jnp.exp(last + source), spread2)
            fed = (xs[rows, :].astype(F32) * tail).astype(BF16)
            kept = spread_row(jnp.exp(last - before), spread_f)
            held[...] = held[...] * kept + dot(b_part, fed, TN)
            before = last


def decay_rows(wide, at):
    both = wide[at : at + 8, :]
    even = iota((8, LANES), 1) % 2 == 0
    return both + jnp.where(even, pltpu.roll(both, LANES - 1, 1), pltpu.roll(both, 1, 1))


def total_kernel(blocks, in_ref, out_ref, wide):
    wide[...] = in_ref[...].astype(F32)
    carry = [jnp.zeros((8, LANES), F32)] * blocks
    passed = jnp.zeros((8, LANES), F32)
    for place in range(Z_RING):
        at = place * PIECE
        logs = decay_rows(wide, at + 8 * blocks)
        passed += logs
        kept = jnp.exp(logs)
        carry = [
            kept[b : b + 1, :] * carry[b] + wide[at + 8 * b : at + 8 * b + 8, :]
            for b in range(blocks)
        ]
    for peer in range(out_ref.shape[0]):
        for b in range(blocks):
            out_ref[peer, 8 * b : 8 * b + 8, :] = carry[b]
        out_ref[peer, 8 * blocks : 8 * blocks + 8, :] = passed


def scan_kernel(blocks, in_ref, total_ref, place_ref, out_ref, wide):
    wide[...] = in_ref[...].astype(F32)
    carry = [jnp.zeros((8, LANES), F32)] * blocks
    for peer in range(total_ref.shape[0] - 1):
        earlier = peer < place_ref[0, 0]
        kept = jnp.exp(total_ref[peer, 8 * blocks : 8 * blocks + 8, :])
        carry = [
            jnp.where(
                earlier,
                kept[b : b + 1, :] * carry[b] + total_ref[peer, 8 * b : 8 * b + 8, :],
                carry[b],
            )
            for b in range(blocks)
        ]
    for place in range(Z_RING):
        at = place * PIECE
        kept = jnp.exp(decay_rows(wide, at + 8 * blocks))
        for b in range(blocks):
            part = wide[at + 8 * b : at + 8 * b + 8, :]
            wide[at + 8 * b : at + 8 * b + 8, :] = carry[b]
            carry[b] = kept[b : b + 1, :] * carry[b] + part
    out_ref[...] = wide[...].astype(BF16)


def back_kernel(
    own_ref, reach_ref, c_ref, piece_ref, w_hbm, gain_ref, place_ref, out_hbm,
    wide, state, gated, w_ref, acc, stage, sems, out_sems,
):
    columns = w_ref.shape[0]
    span = columns // 2
    copies = fetch(
        sems,
        *[(w_hbm.at[k * span : (k + 1) * span, :], w_ref.at[k * span : (k + 1) * span, :])
          for k in range(2)],
    )
    tokens, width = own_ref.shape
    blocks = width // LANES
    each = STATE // Z_RING
    wide[...] = piece_ref[...].astype(F32)
    for j in range(Z_RING):
        for b in range(blocks):
            at = j * PIECE + b * each
            state[j * each : (j + 1) * each, b * LANES : (b + 1) * LANES] = wide[at : at + each, :]
    incoming = state[...].astype(BF16)
    ones = jnp.ones((16, 2 * width), BF16)
    totals = []
    for at in range(0, tokens, CHUNK):
        rows = slice(at, at + CHUNK)
        y = own_ref[rows, :] + reach_ref[rows, :] * dot(c_ref[rows, :], incoming)
        gated[rows, :] = (y * gain_ref[...]).astype(BF16)
        hi, lo = split(y * y)
        totals.append(dot(ones, jnp.concatenate([hi, lo], axis=1), NT))
    hi, lo = split(jnp.concatenate(totals, axis=1))
    row = iota((16, tokens), 0)
    mine = 2 * place_ref[0, 1]
    zero = jnp.zeros((16, tokens), F32)
    squares = jnp.where(
        row == mine, hi.astype(F32), jnp.where(row == mine + 1, lo.astype(F32), zero)
    ).astype(BF16)
    targets = 8
    block = columns // targets
    shard = columns // 64
    per_z = columns // Z_RING
    sent = []
    for half in range(2):
        copies[half].wait()
        acc[...] = dot(w_ref[half * span : (half + 1) * span, :], gated[...], NT)
        for x in range(targets // 2):
            d = 2 * x + half
            to = d * (block + 16)
            stage[to : to + block, :] = jnp.concatenate(
                [
                    acc[z * per_z + x * shard : z * per_z + (x + 1) * shard, :]
                    for z in range(Z_RING // 2)
                ],
                axis=0,
            ).astype(BF16)
            stage[to + block : to + block + 16, :] = squares
            part = pl.ds(to, block + 16)
            copy = pltpu.make_async_copy(stage.at[part, :], out_hbm.at[part, :], out_sems.at[d])
            copy.start()
            sent.append(copy)
    for copy in sent:
        copy.wait()


def scale_kernel(in_ref, out_ref):
    each = out_ref.shape[0]
    total = jnp.sum(in_ref[each:, :].astype(F32), axis=0, keepdims=True)
    scale = lax.rsqrt(total / CHANNELS + EPSILON)
    out_ref[...] = (in_ref[:each, :].astype(F32) * scale).astype(BF16)


def shaped(shape, dtype):
    return jax.ShapeDtypeStruct(shape, dtype)


def held_like(*arrays):
    return tuple(pltpu.VMEM(a.shape, a.dtype) for a in arrays)


def front(x_in, bc_in, dt_t, conv_x, conv_bc, dt_bias, a_log):
    tokens, width = x_in.shape
    args = (x_in, bc_in, dt_t, conv_x, conv_bc, dt_bias, a_log)
    return call(
        front_kernel,
        [
            shaped((tokens, width), BF16),
            shaped((tokens, 2 * STATE), BF16),
            shaped((PAD_HEADS, tokens), F32),
            shaped((PAD_HEADS, tokens), F32),
            shaped((STATE, width), F32),
            shaped((RIM, width), F32),
        ],
        8 * tokens * width * STATE,
        *args,
        spaces=[pl.ANY] * 7,
        scratch=held_like(*args)
        + (
            pltpu.VMEM((tokens + 8, width), F32),
            pltpu.VMEM((tokens + 8, 2 * STATE), F32),
            pltpu.VMEM((PAD_HEADS, tokens), F32),
            pltpu.VMEM((tokens, width), BF16),
            pltpu.SemaphoreType.DMA((7,)),
        ),
    )


def add_rim(rim, x_in, bc_in, conv_x, conv_bc, cum, tail, state):
    width = x_in.shape[1]
    return call(
        rim_kernel,
        [
            shaped((RIM, width), BF16),
            shaped((RIM, 2 * STATE), BF16),
            shaped((Z_RING * PIECE, LANES), BF16),
        ],
        2 * 128 * width * STATE,
        rim, x_in, bc_in, conv_x, conv_bc, cum, tail, state,
        spaces=[pltpu.VMEM] + [pl.ANY] * 4 + [pltpu.VMEM] * 3,
        scratch=(
            pltpu.VMEM((RIM, width), BF16),
            pltpu.VMEM((RIM, 2 * STATE), BF16),
            *held_like(conv_x, conv_bc),
            pltpu.VMEM((RIM + 8, width), F32),
            pltpu.VMEM((RIM + 8, 2 * STATE), F32),
            pltpu.VMEM((Z_RING * PIECE, LANES), F32),
            pltpu.SemaphoreType.DMA((4,)),
        ),
    )


def local(xc, xc_rim, bcc, bcc_rim, cum, logstep, z_gate, d_skip):
    tokens, width = xc.shape
    return call(
        local_kernel,
        [shaped((tokens, width), F32)] * 2 + [shaped((tokens, STATE), BF16)],
        12 * tokens * width * STATE,
        xc, xc_rim, bcc, bcc_rim, cum, logstep, z_gate, d_skip,
        spaces=[pltpu.VMEM] * 6 + [pl.ANY] * 2,
        scratch=(pltpu.VMEM((STATE, width), F32),)
        + held_like(xc, bcc, z_gate, d_skip)
        + (pltpu.SemaphoreType.DMA((2,)),),
    )


def row_total(pieces, width, peers):
    def body(*refs):
        total_kernel(width // LANES, *refs)

    return call(
        body,
        [shaped((peers, PIECE, LANES), F32)],
        pieces.size * 4,
        pieces,
        scratch=(pltpu.VMEM(pieces.shape, F32),),
    )[0]


def scan(pieces, totals, place, width):
    def body(*refs):
        scan_kernel(width // LANES, *refs)

    return call(
        body,
        [shaped(pieces.shape, BF16)],
        pieces.size * 4,
        pieces, totals, place,
        spaces=[pltpu.VMEM, pltpu.VMEM, pltpu.SMEM],
        scratch=(pltpu.VMEM(pieces.shape, F32),),
    )[0]


def back(own, reach, c_part, pieces, weight, norm_gain, place):
    tokens, width = own.shape
    columns = weight.shape[0]
    out = shaped((columns + 8 * 16, tokens), BF16)
    return pl.pallas_call(
        back_kernel,
        out_shape=out,
        in_specs=[pl.BlockSpec(memory_space=pltpu.VMEM)] * 4
        + [
            pl.BlockSpec(memory_space=pl.ANY),
            pl.BlockSpec(memory_space=pltpu.VMEM),
            pl.BlockSpec(memory_space=pltpu.SMEM),
        ],
        out_specs=pl.BlockSpec(memory_space=pl.ANY),
        scratch_shapes=[
            pltpu.VMEM(pieces.shape, F32),
            pltpu.VMEM((STATE, width), F32),
            pltpu.VMEM((tokens, width), BF16),
            *held_like(weight),
            pltpu.VMEM((columns // 2, tokens), F32),
            *held_like(out),
            pltpu.SemaphoreType.DMA((2,)),
            pltpu.SemaphoreType.DMA((8,)),
        ],
        compiler_params=pltpu.CompilerParams(vmem_limit_bytes=40 * 2**20),
        cost_estimate=pl.CostEstimate(
            flops=2 * tokens * width * (columns + STATE), bytes_accessed=10**7, transcendentals=0
        ),
        interpret=INTERPRET,
    )(own, reach, c_part, pieces, weight, norm_gain[None], place)


def scaled(summed):
    rows, tokens = summed.shape
    return call(scale_kernel, [shaped((rows - 16, tokens), BF16)], rows * tokens, summed)[0]


def on_device(
    x_in, bc_in, z_gate, dt_in, conv_x, conv_bc, dt_bias, a_log, d_skip, norm_gain, out_weight
):
    tokens, width = x_in.shape
    count = lax.axis_size("seq")
    rows = count // Z_RING
    along_z = [[x * Z_RING + z for z in range(Z_RING)] for x in range(rows)]
    along_x = [[x * Z_RING + z for x in range(rows)] for z in range(Z_RING)]
    weight = lax.all_gather(
        out_weight.T, "seq", axis=0, tiled=True, axis_index_groups=along_x
    )
    weight = lax.all_gather(weight, "seq", axis=0, tiled=True, axis_index_groups=along_z)
    rim = jnp.concatenate([x_in[tokens - RIM :], bc_in[tokens - RIM :]], axis=1)
    rim = lax.ppermute(rim, "seq", [(i, i + 1) for i in range(count - 1)])
    place = jnp.stack(
        [lax.axis_index("seq") // Z_RING, lax.axis_index("tp")]
    ).astype(jnp.int32)[None]

    xc, bcc, cum, logstep, state, tail = front(
        x_in, bc_in, dt_in.T, conv_x, conv_bc, dt_bias[None], a_log[None]
    )
    xc_rim, bcc_rim, pieces = add_rim(rim, x_in, bc_in, conv_x, conv_bc, cum, tail, state)
    pieces = lax.all_to_all(pieces, "seq", 0, 0, tiled=True, axis_index_groups=along_z)
    totals = row_total(pieces, width, rows)
    totals = lax.all_to_all(totals, "seq", 0, 0, tiled=True, axis_index_groups=along_x)
    pieces = scan(pieces, totals, place, width)
    pieces = lax.all_to_all(pieces, "seq", 0, 0, tiled=True, axis_index_groups=along_z)
    own, reach, c_part = local(xc, xc_rim, bcc, bcc_rim, cum, logstep, z_gate, d_skip[None])
    partial = back(own, reach, c_part, pieces, weight, norm_gain, place)
    return scaled(lax.psum_scatter(partial, "tp", scatter_dimension=0, tiled=True)).T


def solution(mesh):
    in_specs = (
        P("seq", "tp"),
        P("seq", None),
        P("seq", "tp"),
        P("seq", "tp"),
        P(None, "tp"),
        P(),
        P("tp"),
        P("tp"),
        P("tp"),
        P("tp"),
        P("tp", "seq"),
    )
    return jax.shard_map(
        on_device, mesh=mesh, in_specs=in_specs, out_specs=P("seq", "tp"), check_vma=False
    )
```

time: 215 us -> 169 us (0.79)
  waiting for transfers between devices: 125 us -> 84.8 us
  blocking collectives: 38 us -> 12.8 us
  starting transfers between devices: 13.5 us -> 27.8 us
  Pallas kernels: 10.8 us -> 15.6 us
    all_gather x1, waiting for transfers between devices: 64.6 us -> 11.4 us  [on_device(): lax.all_gather(weight, 'seq', axis=0, tiled=True, axis_index_groups=along_z)]
    all_to_all x1 -> x0, blocking collectives: 38 us -> none  [on_device(): pieces = lax.all_to_all(pieces, 'seq', 0, 0, tiled=True)]
    all_to_all x1 -> x3, starting transfers between devices: 9.06 us -> 24.7 us  [the longest x2 21.4 us: on_device(): lax.all_to_all(pieces, 'seq', 0, 0, tiled=True, axis_index_groups=along_z)]
    all_gather x0 -> x1, blocking collectives: none -> 12.8 us  [on_device(): lax.all_gather(out_weight.T, 'seq', axis=0, tiled=True, axis_index_groups...]
    all_to_all x1 -> x3, waiting for transfers between devices: 15 us -> 27.7 us  [the longest x2 23.2 us: on_device(): lax.all_to_all(pieces, 'seq', 0, 0, tiled=True, axis_index_groups=along_z)]
    pallas_call x4 -> x6, Pallas kernels: 6.2 us -> 10.2 us  [call(): pl.pallas_call(body, out_shape=outs, in_specs=[pl.BlockSpec(memory_space=...]
    unnamed x27 -> x28, local copies, waits for them, and re-layouts: 10.7 us -> 11.4 us
  transfers between devices with their start and end apart: 4 -> 6, of which waited for: 4 -> 5; matrix products, arithmetic and copies ran while one was open for 1% -> 1% of each run, Pallas kernels for 3% -> 6%
where the time goes in v2:
time: 169 us; the launch traced here: 168 us
  waiting for transfers between devices  84.8 us (50%)
  starting transfers between devices  27.8 us (16%)
  Pallas kernels  15.6 us (9%)
  between operations  13.5 us (8%)
  local copies, waits for them, and re-layouts  12.8 us (8%)
  blocking collectives  12.8 us (8%)
    reduce_scatter x1, waiting for transfers between devices, on_device(): lax.psum_scatter(partial, 'tp', scatter_dimension=0, tiled=True)  45.6 us
    all_to_all x2, waiting for transfers between devices, on_device(): lax.all_to_all(pieces, 'seq', 0, 0, tiled=True, axis_index_groups=along_z)  23.2 us
    all_to_all x2, starting transfers between devices, on_device(): lax.all_to_all(pieces, 'seq', 0, 0, tiled=True, axis_index_groups=along_z)  21.4 us
    all_gather x1, blocking collectives, on_device(): lax.all_gather(out_weight.T, 'seq', axis=0, tiled=True, axis_index_groups...  12.8 us
    all_gather x1, waiting for transfers between devices, on_device(): lax.all_gather(weight, 'seq', axis=0, tiled=True, axis_index_groups=along_z)  11.4 us
    unnamed x28, local copies, waits for them, and re-layouts  11.4 us
    pallas_call x6, Pallas kernels, call(): pl.pallas_call(body, out_shape=outs, in_specs=[pl.BlockSpec(memory_space=...  10.2 us
    pallas_call x1, Pallas kernels, back(): pl.pallas_call(back_kernel, out_shape=out, in_specs=[pl.BlockSpec(memory_...  5.48 us
  transfers between devices with their start and end apart: 6, of which 5 were waited for; matrix products, arithmetic and copies ran while one was open for 1% of the time, Pallas kernels for 6%

profile of v2, /device:TPU:1, one launch (start us, length us, event | category | flops | bytes accessed | tf_op | source)
XLA Modules:
  0.0 167.5 jit_solution(6647718295185553796)
XLA Ops:
  6.5 12.8 %all_gather.6 = bf16[160,640]{1,0:T(8,128)(2,1)} all-gather(bf16[40,640]{1,0:T(8,128)(2,1)} %bitcast.21), channel_id=1, replica_groups={{0,128,256,384},{8,136,264,392},{16,144,272,400},{24,152,280,408},{32,1..., dimensions={0}, use_global_device_ids=true | all-gather | bytes 256000 | tf_op jit(solution)/shard_map/all_gather | solution.py:515
  19.4 0.7 slice.7
  20.1 0.7 slice.6
  20.9 3.1 %collective-permute-start = (bf16[16,896]{1,0:T(8,128)(2,1)S(1)}, bf16[16,896]{1,0:T(8,128)(2,1)S(1)}, u32[]{:S(2)}, u32[]{:S(2)}) collective-permute-start(bf16[16,896]{1,0:T(8,128)(2,1)S(1)} %pad_maximum_fusion), channel_id=1, source_target_pairs={{0,8},{8,16},{16,24},{24,32},{32,40},{40,48},{48,56},{56,64},{64,7... | collective-permute-start | bytes 86024 | tf_op jit(solution)/shard_map/ppermute | solution.py:520
  23.9 1.1 copy-done.1
  25.0 0.9 copy-done.3
  26.0 0.7 copy-done.4
  26.7 0.7 copy-done.5
  27.4 0.7 copy-done.7
  28.1 0.7 copy-done.8
  28.7 0.7 copy-done.9
  29.4 3.6 %shard_map.109 = (bf16[512,640]{1,0:T(8,128)(2,1)S(1)}, bf16[512,256]{1,0:T(8,128)(2,1)S(1)}, f32[16,512]{1,0:T(8,128)S(1)}, f32[16,512]{1,0:T(8,128)S(1)}, f32[...) custom-call(bf16[512,640]{1,0:T(8,128)(2,1)S(1)} %copy-done.1, bf16[512,256]{1,0:T(8,128)(2,1)S(1)} %copy-done.3, ...), custom_call_target="tpu_custom_call" | custom-call | flops 335544320 | bytes 2293840 | tf_op jit(solution)/shard_map/pallas_call | solution.py:39
  33.0 0.8 copy-done.11
  33.9 1.1 shard_map.110
  35.0 14.0 %all-to-all-start = ((bf16[16,48,128]{2,1,0:T(8,128)(2,1)}), bf16[16,48,128]{2,1,0:T(8,128)(2,1)S(1)}, u32[]{:S(2)}, u32[]{:S(2)}) async-start(bf16[16,48,128]{2,1,0:T(8,128)(2,1)} %bitcast.4), calls=%async_computation | async-start | bytes 393216 | tf_op jit(solution)/shard_map/all_to_all | solution.py:529
  49.1 14.1 %all-to-all-done = bf16[16,48,128]{2,1,0:T(8,128)(2,1)S(1)} async-done(((bf16[16,48,128]{2,1,0:T(8,128)(2,1)}), bf16[16,48,128]{2,1,0:T(8,128)(2,1)S(1)}, u32[]{:S(2)}, u32[]{:S(2)}) %all-to-all-start) | async-done | bytes 196640 | tf_op jit(solution)/shard_map/all_to_all | solution.py:529
  63.1 0.8 shard_map.112
  63.9 3.3 %all-to-all-start.1 = ((f32[4,48,128]{2,1,0:T(8,128)}), f32[4,48,128]{2,1,0:T(8,128)S(1)}, u32[]{:S(2)}, u32[]{:S(2)}) async-start(f32[4,48,128]{2,1,0:T(8,128)} %shard_map.112), calls=%async_computation.1 | async-start | bytes 196608 | tf_op jit(solution)/shard_map/all_to_all | solution.py:531
  67.2 0.1 add_bitcast_fusion.refs_2_.place_ref
  67.3 4.5 %all-to-all-done.1.refs_1_ = f32[4,48,128]{2,1,0:T(8,128)S(1)} async-done(((f32[4,48,128]{2,1,0:T(8,128)}), f32[4,48,128]{2,1,0:T(8,128)S(1)}, u32[]{:S(2)}, u32[]{:S(2)}) %all-to-all-start.1) | async-done | bytes 98336 | tf_op jit(solution)/shard_map/all_to_all | solution.py:531
  71.8 1.4 shard_map.113
  73.2 7.4 %all-to-all-start.2 = ((bf16[16,48,128]{2,1,0:T(8,128)(2,1)}), bf16[16,48,128]{2,1,0:T(8,128)(2,1)S(1)}, u32[]{:S(2)}, u32[]{:S(2)}) async-start(bf16[16,48,128]{2,1,0:T(8,128)(2,1)} %bitcast.9), calls=%async_computation.2 | async-start | bytes 393216 | tf_op jit(solution)/shard_map/all_to_all | solution.py:533
  80.6 1.1 copy-done.6
  81.7 1.1 copy-done.12
  82.8 2.5 %shard_map.111 = (f32[512,640]{1,0:T(8,128)S(1)}, f32[512,640]{1,0:T(8,128)S(1)}, bf16[512,128]{1,0:T(8,128)(2,1)S(1)}) custom-call(bf16[512,640]{1,0:T(8,128)(2,1)S(1)} %copy-done.12, bf16[16,640]{1,0:T(8,128)(2,1)S(1)} %get-tuple-element.21.xc_rim_ref, bf16[512,256]{1,0:T(8,128)(2,1)S(1)} %get-tuple-element.22.bcc_ref, ...), custom_call_target="tpu_custom_call" | custom-call | flops 503316480 | bytes 4419624 | tf_op jit(solution)/shard_map/pallas_call | solution.py:39
  85.3 9.1 %all-to-all-done.2 = bf16[16,48,128]{2,1,0:T(8,128)(2,1)S(1)} async-done(((bf16[16,48,128]{2,1,0:T(8,128)(2,1)}), bf16[16,48,128]{2,1,0:T(8,128)(2,1)S(1)}, u32[]{:S(2)}, u32[]{:S(2)}) %all-to-all-start.2) | async-done | bytes 196640 | tf_op jit(solution)/shard_map/all_to_all | solution.py:533
  94.5 11.4 %all-gather.2.cloned.1.call-done.w_hbm = bf16[2560,640]{1,0:T(8,128)(2,1)} async-done(((bf16[160,640]{1,0:T(8,128)(2,1)}), bf16[2560,640]{1,0:T(8,128)(2,1)}) %all-gather.2.cloned.1.call-update) | async-done | bytes 3276816 | tf_op jit(solution)/shard_map/all_gather | solution.py:518
  105.9 1.9 %copy-done = bf16[2560,640]{1,0:T(8,128)(2,1)S(1)} copy-done((bf16[2560,640]{1,0:T(8,128)(2,1)S(1)}, bf16[2560,640]{1,0:T(8,128)(2,1)}, u32[]{:S(2)}) %copy-start) | copy-done | bytes 3276824
  107.8 5.5 %shard_map.114 = bf16[2688,512]{1,0:T(8,128)(2,1)} custom-call(f32[512,640]{1,0:T(8,128)S(1)} %get-tuple-element.25.own_ref, f32[512,640]{1,0:T(8,128)S(1)} %get-tuple-element.26.reach_ref, bf16[512,128]{1,0:T(8,128)(2,1)S(1)} %get-tuple-element.27.c_ref, bf16[768,128]{1,0:T(8,128)(2,1)S(1)} %bitcast.16, bf16[2560,640]{1,0:T(8,128)(2,1)S(1)} %copy-done, ...), custom_call_target="tpu_custom_call" | custom-call | flops 1761607680 | bytes 10000000 | tf_op jit(solution)/shard_map/pallas_call | solution.py:474
  113.3 45.6 %reduce-scatter.2.cloned.1.call-done.in_ref = bf16[336,512]{1,0:T(8,128)(2,1)} async-done(((bf16[2688,512]{1,0:T(8,128)(2,1)}), bf16[336,512]{1,0:T(8,128)(2,1)}) %reduce-scatter.2.cloned.1.call-update) | async-done | bytes 344080 | tf_op jit(solution)/shard_map/reduce_scatter | solution.py:536
  158.9 1.0 copy-done.2
  159.9 0.8 shard_map.115
  (23 shorter events, 0.1 us)
Async XLA Ops:
  6.5 74.1 %copy-start.13 = (f32[640]{0:T(1024)S(1)}, f32[640]{0:T(1024)}, u32[]{:S(2)}) copy-start(f32[640]{0:T(1024)} %param.20) | copy-start | bytes 7684
  6.5 74.1 %copy-start.10 = (f32[10]{0:T(128)S(1)}, f32[10]{0:T(128)}, u32[]{:S(2)}) copy-start(f32[10]{0:T(128)} %param.19) | copy-start | bytes 124
  6.5 99.4 %all-gather.2.cloned.1.call-start = ((), (), s32[]{:S(2)}) async-start(), calls=%async_computation.4 | async-start | bytes 3481600 | tf_op jit(solution)/shard_map/all_gather | solution.py:518
  20.9 13.0 %collective-permute-start = (bf16[16,896]{1,0:T(8,128)(2,1)S(1)}, bf16[16,896]{1,0:T(8,128)(2,1)S(1)}, u32[]{:S(2)}, u32[]{:S(2)}) collective-permute-start(bf16[16,896]{1,0:T(8,128)(2,1)S(1)} %pad_maximum_fusion), channel_id=1, source_target_pairs={{0,8},{8,16},{16,24},{24,32},{32,40},{40,48},{48,56},{56,64},{64,7... | collective-permute-start | bytes 86024 | tf_op jit(solution)/shard_map/ppermute | solution.py:520
  23.9 1.1 copy-start.1
  25.0 0.9 copy-start.3
  26.0 0.7 copy-start.4
  26.7 0.7 copy-start.5
  27.4 0.7 copy-start.7
  28.1 0.7 copy-start.8
  28.7 0.7 copy-start.9
  33.0 0.8 copy-start.11
  35.0 28.1 %all-to-all-start = ((bf16[16,48,128]{2,1,0:T(8,128)(2,1)}), bf16[16,48,128]{2,1,0:T(8,128)(2,1)S(1)}, u32[]{:S(2)}, u32[]{:S(2)}) async-start(bf16[16,48,128]{2,1,0:T(8,128)(2,1)} %bitcast.4), calls=%async_computation | async-start | bytes 393216 | tf_op jit(solution)/shard_map/all_to_all | solution.py:529
  63.9 7.9 %all-to-all-start.1 = ((f32[4,48,128]{2,1,0:T(8,128)}), f32[4,48,128]{2,1,0:T(8,128)S(1)}, u32[]{:S(2)}, u32[]{:S(2)}) async-start(f32[4,48,128]{2,1,0:T(8,128)} %shard_map.112), calls=%async_computation.1 | async-start | bytes 196608 | tf_op jit(solution)/shard_map/all_to_all | solution.py:531
  73.2 21.3 %all-to-all-start.2 = ((bf16[16,48,128]{2,1,0:T(8,128)(2,1)}), bf16[16,48,128]{2,1,0:T(8,128)(2,1)S(1)}, u32[]{:S(2)}, u32[]{:S(2)}) async-start(bf16[16,48,128]{2,1,0:T(8,128)(2,1)} %bitcast.9), calls=%async_computation.2 | async-start | bytes 393216 | tf_op jit(solution)/shard_map/all_to_all | solution.py:533
  80.5 78.4 %reduce-scatter.2.cloned.1.call-start = ((), (), s32[]{:S(2)}) async-start(), calls=%async_computation.5 | async-start | bytes 3096576 | tf_op jit(solution)/shard_map/reduce_scatter | solution.py:536
  80.6 1.1 copy-start.6
  81.7 1.1 copy-start.12
  105.9 1.9 %copy-start = (bf16[2560,640]{1,0:T(8,128)(2,1)S(1)}, bf16[2560,640]{1,0:T(8,128)(2,1)}, u32[]{:S(2)}) copy-start(bf16[2560,640]{1,0:T(8,128)(2,1)} %all-gather.2.cloned.1.call-done.w_hbm) | copy-start | bytes 9830404
  158.9 1.0 copy-start.2
Sparse Core Ops, SparseCore 0:
  19.5 86.3 all-gather.1
  113.5 45.4 reduce-scatter.1

commit v3 on v2

--- a/solution.py
+++ b/solution.py
@@ -15,6 +15,8 @@
 PAD_HEADS = 16
 Z_RING = 16
 PIECE = 48
+TARGETS = 8
+FULL = 63
 EPSILON = 1e-05
 HIGH = lax.Precision.HIGHEST
 F32 = jnp.float32
@@ -31,8 +33,11 @@
     return lax.dot_general(a, b, dims, precision=precision, preferred_element_type=F32)
 
 
-def call(body, outs, flops, *args, scratch=(), spaces=None):
+def call(
+    body, outs, flops, *args, scratch=(), spaces=None, out_spaces=None, aliases=None, vmem=40
+):
     spaces = spaces or [pltpu.VMEM] * len(args)
+    out_spaces = out_spaces or [pltpu.VMEM] * len(outs)
     moved = sum(a.size * a.dtype.itemsize for a in args) + sum(
         o.size * o.dtype.itemsize for o in outs
     )
@@ -40,9 +45,10 @@
         body,
         out_shape=outs,
         in_specs=[pl.BlockSpec(memory_space=space) for space in spaces],
-        out_specs=[pl.BlockSpec(memory_space=pltpu.VMEM)] * len(outs),
+        out_specs=[pl.BlockSpec(memory_space=space) for space in out_spaces],
+        input_output_aliases=aliases or {},
         scratch_shapes=list(scratch),
-        compiler_params=pltpu.CompilerParams(vmem_limit_bytes=40 * 2**20),
+        compiler_params=pltpu.CompilerParams(vmem_limit_bytes=vmem * 2**20),
         cost_estimate=pl.CostEstimate(flops=flops, bytes_accessed=moved, transcendentals=0),
         interpret=INTERPRET,
     )(*args)
@@ -195,9 +201,10 @@
 
 
 def local_kernel(
-    xc_ref, xc_rim_ref, bcc_ref, bcc_rim_ref, cum_ref, logstep_ref, z_hbm, skip_hbm,
-    own_ref, reach_ref, c_ref, held, xs, bs, z_ref, skip_ref, sems,
+    xc_ref, xc_rim_ref, bcc_ref, bcc_rim_ref, cum_ref, logstep_ref, z_hbm, skip_hbm, w_ref,
+    own_ref, reach_ref, c_ref, w_out_ref, held, xs, bs, z_ref, skip_ref, sems,
 ):
+    del w_ref, w_out_ref
     copies = fetch(sems, (skip_hbm, skip_ref), (z_hbm, z_ref))
     tokens, width = xc_ref.shape
     xs[...] = xc_ref[...]
@@ -255,7 +262,8 @@
     return both + jnp.where(even, pltpu.roll(both, LANES - 1, 1), pltpu.roll(both, 1, 1))
 
 
-def total_kernel(blocks, in_ref, out_ref, wide):
+def total_kernel(blocks, in_ref, after_ref, out_ref, wide):
+    del after_ref
     wide[...] = in_ref[...].astype(F32)
     carry = [jnp.zeros((8, LANES), F32)] * blocks
     passed = jnp.zeros((8, LANES), F32)
@@ -298,17 +306,35 @@
     out_ref[...] = wide[...].astype(BF16)
 
 
+def rim_source_kernel(x_hbm, bc_hbm, out_ref, sems):
+    tokens, width = x_hbm.shape
+    for copy in fetch(
+        sems,
+        (x_hbm.at[tokens - RIM :, :], out_ref.at[:, 0:width]),
+        (bc_hbm.at[tokens - RIM :, :], out_ref.at[:, width:]),
+    ):
+        copy.wait()
+
+
+def fetch_half(w_hbm, w_ref, half, sems):
+    block = w_hbm.shape[0] // TARGETS
+    return fetch(
+        sems,
+        *[
+            (
+                w_hbm.at[pl.ds(pl.multiple_of((2 * y + half) * block, block), block), :],
+                w_ref.at[y * block : (y + 1) * block, :],
+            )
+            for y in range(TARGETS // 2)
+        ],
+    )
+
+
 def back_kernel(
-    own_ref, reach_ref, c_ref, piece_ref, w_hbm, gain_ref, place_ref, out_hbm,
-    wide, state, gated, w_ref, acc, stage, sems, out_sems,
+    own_ref, reach_ref, c_ref, piece_ref, w_hbm, gain_ref, place_ref,
+    out_ref, gated_ref, square_ref, wide, state, w_ref, sems,
 ):
-    columns = w_ref.shape[0]
-    span = columns // 2
-    copies = fetch(
-        sems,
-        *[(w_hbm.at[k * span : (k + 1) * span, :], w_ref.at[k * span : (k + 1) * span, :])
-          for k in range(2)],
-    )
+    copies = fetch_half(w_hbm, w_ref, 1 - place_ref[0, 1] % 2, sems)
     tokens, width = own_ref.shape
     blocks = width // LANES
     each = STATE // Z_RING
@@ -323,7 +349,7 @@
     for at in range(0, tokens, CHUNK):
         rows = slice(at, at + CHUNK)
         y = own_ref[rows, :] + reach_ref[rows, :] * dot(c_ref[rows, :], incoming)
-        gated[rows, :] = (y * gain_ref[...]).astype(BF16)
+        gated_ref[rows, :] = (y * gain_ref[...]).astype(BF16)
         hi, lo = split(y * y)
         totals.append(dot(ones, jnp.concatenate([hi, lo], axis=1), NT))
     hi, lo = split(jnp.concatenate(totals, axis=1))
@@ -333,38 +359,52 @@
     squares = jnp.where(
         row == mine, hi.astype(F32), jnp.where(row == mine + 1, lo.astype(F32), zero)
     ).astype(BF16)
-    targets = 8
-    block = columns // targets
-    shard = columns // 64
-    per_z = columns // Z_RING
-    sent = []
-    for half in range(2):
-        copies[half].wait()
-        acc[...] = dot(w_ref[half * span : (half + 1) * span, :], gated[...], NT)
-        for x in range(targets // 2):
-            d = 2 * x + half
-            to = d * (block + 16)
-            stage[to : to + block, :] = jnp.concatenate(
-                [
-                    acc[z * per_z + x * shard : z * per_z + (x + 1) * shard, :]
-                    for z in range(Z_RING // 2)
-                ],
-                axis=0,
-            ).astype(BF16)
-            stage[to + block : to + block + 16, :] = squares
-            part = pl.ds(to, block + 16)
-            copy = pltpu.make_async_copy(stage.at[part, :], out_hbm.at[part, :], out_sems.at[d])
-            copy.start()
-            sent.append(copy)
-    for copy in sent:
+    square_ref[...] = squares
+    for copy in copies:
         copy.wait()
+    block = w_ref.shape[0] // (TARGETS // 2)
+    for y in range(TARGETS // 2):
+        to = y * (block + 16)
+        out_ref[to : to + block, :] = dot(
+            w_ref[y * block : (y + 1) * block, :], gated_ref[...], NT
+        ).astype(BF16)
+        out_ref[to + block : to + block + 16, :] = squares
+
+
+def kept_kernel(gated_ref, w_hbm, place_ref, out_ref, w_ref, sems):
+    copies = fetch_half(w_hbm, w_ref, place_ref[0, 1] % 2, sems)
+    block = w_ref.shape[0] // (TARGETS // 2)
+    for y in range(TARGETS // 2):
+        rows = slice(y * block, (y + 1) * block)
+        copies[y].wait()
+        out_ref[rows, :] = dot(w_ref[rows, :], gated_ref[...], NT).astype(BF16)
+
+
+def pair_kernel(kept_ref, got_ref, square_ref, out_ref):
+    block = kept_ref.shape[0] // (TARGETS // 2)
+    for y in range(TARGETS // 2):
+        to = y * (block + 16)
+        rows = slice(to, to + block)
+        out_ref[rows, :] = (
+            kept_ref[y * block : (y + 1) * block, :].astype(F32) + got_ref[rows, :].astype(F32)
+        ).astype(BF16)
+        rows = slice(to + block, to + block + 16)
+        out_ref[rows, :] = (square_ref[...].astype(F32) + got_ref[rows, :].astype(F32)).astype(BF16)
 
 
 def scale_kernel(in_ref, out_ref):
-    each = out_ref.shape[0]
-    total = jnp.sum(in_ref[each:, :].astype(F32), axis=0, keepdims=True)
+    block = out_ref.shape[0]
+    parts = TARGETS // 2
+    each = block + 16
+    total = jnp.zeros((1, out_ref.shape[1]), F32)
+    for y in range(parts):
+        part = in_ref[y * each + block : (y + 1) * each, :].astype(F32)
+        total += jnp.sum(part, axis=0, keepdims=True)
     scale = lax.rsqrt(total / CHANNELS + EPSILON)
-    out_ref[...] = (in_ref[:each, :].astype(F32) * scale).astype(BF16)
+    mixed = in_ref[0:block, :].astype(F32)
+    for y in range(1, parts):
+        mixed += in_ref[y * each : y * each + block, :].astype(F32)
+    out_ref[...] = (mixed * scale).astype(BF16)
 
 
 def shaped(shape, dtype):
@@ -390,7 +430,8 @@
         ],
         8 * tokens * width * STATE,
         *args,
-        spaces=[pl.ANY] * 7,
+        spaces=[pltpu.HBM] * 7,
+        vmem=FULL,
         scratch=held_like(*args)
         + (
             pltpu.VMEM((tokens + 8, width), F32),
@@ -413,7 +454,8 @@
         ],
         2 * 128 * width * STATE,
         rim, x_in, bc_in, conv_x, conv_bc, cum, tail, state,
-        spaces=[pltpu.VMEM] + [pl.ANY] * 4 + [pltpu.VMEM] * 3,
+        spaces=[pltpu.VMEM] + [pltpu.HBM] * 4 + [pltpu.VMEM] * 3,
+        vmem=FULL,
         scratch=(
             pltpu.VMEM((RIM, width), BF16),
             pltpu.VMEM((RIM, 2 * STATE), BF16),
@@ -426,21 +468,24 @@
     )
 
 
-def local(xc, xc_rim, bcc, bcc_rim, cum, logstep, z_gate, d_skip):
+def local(xc, xc_rim, bcc, bcc_rim, cum, logstep, z_gate, d_skip, weight):
     tokens, width = xc.shape
     return call(
         local_kernel,
-        [shaped((tokens, width), F32)] * 2 + [shaped((tokens, STATE), BF16)],
+        [shaped((tokens, width), F32)] * 2
+        + [shaped((tokens, STATE), BF16), shaped(weight.shape, BF16)],
         12 * tokens * width * STATE,
-        xc, xc_rim, bcc, bcc_rim, cum, logstep, z_gate, d_skip,
-        spaces=[pltpu.VMEM] * 6 + [pl.ANY] * 2,
+        xc, xc_rim, bcc, bcc_rim, cum, logstep, z_gate, d_skip, weight,
+        spaces=[pltpu.VMEM] * 6 + [pltpu.HBM] * 3,
+        out_spaces=[pltpu.VMEM] * 3 + [pltpu.HBM],
+        aliases={8: 3},
         scratch=(pltpu.VMEM((STATE, width), F32),)
         + held_like(xc, bcc, z_gate, d_skip)
         + (pltpu.SemaphoreType.DMA((2,)),),
     )
 
 
-def row_total(pieces, width, peers):
+def row_total(pieces, width, peers, after):
     def body(*refs):
         total_kernel(width // LANES, *refs)
 
@@ -448,7 +493,8 @@
         body,
         [shaped((peers, PIECE, LANES), F32)],
         pieces.size * 4,
-        pieces,
+        pieces, after,
+        spaces=[pltpu.VMEM, pl.ANY],
         scratch=(pltpu.VMEM(pieces.shape, F32),),
     )[0]
 
@@ -467,41 +513,68 @@
     )[0]
 
 
+def rim_source(x_in, bc_in):
+    return call(
+        rim_source_kernel,
+        [shaped((RIM, x_in.shape[1] + bc_in.shape[1]), BF16)],
+        0,
+        x_in, bc_in,
+        spaces=[pltpu.HBM] * 2,
+        vmem=FULL,
+        scratch=(pltpu.SemaphoreType.DMA((2,)),),
+    )[0]
+
+
 def back(own, reach, c_part, pieces, weight, norm_gain, place):
     tokens, width = own.shape
     columns = weight.shape[0]
-    out = shaped((columns + 8 * 16, tokens), BF16)
-    return pl.pallas_call(
+    half = columns // 2
+    parts = TARGETS // 2
+    return call(
         back_kernel,
-        out_shape=out,
-        in_specs=[pl.BlockSpec(memory_space=pltpu.VMEM)] * 4
-        + [
-            pl.BlockSpec(memory_space=pl.ANY),
-            pl.BlockSpec(memory_space=pltpu.VMEM),
-            pl.BlockSpec(memory_space=pltpu.SMEM),
+        [
+            shaped((half + parts * 16, tokens), BF16),
+            shaped((tokens, width), BF16),
+            shaped((16, tokens), BF16),
         ],
-        out_specs=pl.BlockSpec(memory_space=pl.ANY),
-        scratch_shapes=[
+        2 * tokens * width * (half + STATE),
+        own, reach, c_part, pieces, weight, norm_gain[None], place,
+        spaces=[pltpu.VMEM] * 4 + [pltpu.HBM, pltpu.VMEM, pltpu.SMEM],
+        vmem=FULL - 5,
+        scratch=(
             pltpu.VMEM(pieces.shape, F32),
             pltpu.VMEM((STATE, width), F32),
-            pltpu.VMEM((tokens, width), BF16),
-            *held_like(weight),
-            pltpu.VMEM((columns // 2, tokens), F32),
-            *held_like(out),
-            pltpu.SemaphoreType.DMA((2,)),
-            pltpu.SemaphoreType.DMA((8,)),
-        ],
-        compiler_params=pltpu.CompilerParams(vmem_limit_bytes=40 * 2**20),
-        cost_estimate=pl.CostEstimate(
-            flops=2 * tokens * width * (columns + STATE), bytes_accessed=10**7, transcendentals=0
+            pltpu.VMEM((half, width), BF16),
+            pltpu.SemaphoreType.DMA((parts,)),
         ),
-        interpret=INTERPRET,
-    )(own, reach, c_part, pieces, weight, norm_gain[None], place)
-
-
-def scaled(summed):
-    rows, tokens = summed.shape
-    return call(scale_kernel, [shaped((rows - 16, tokens), BF16)], rows * tokens, summed)[0]
+    )
+
+
+def kept_part(gated, weight, place):
+    tokens, width = gated.shape
+    half = weight.shape[0] // 2
+    return call(
+        kept_kernel,
+        [shaped((half, tokens), BF16)],
+        2 * tokens * width * half,
+        gated, weight, place,
+        spaces=[pltpu.VMEM, pltpu.HBM, pltpu.SMEM],
+        vmem=FULL - 2,
+        scratch=(
+            pltpu.VMEM((half, width), BF16),
+            pltpu.SemaphoreType.DMA((TARGETS // 2,)),
+        ),
+    )[0]
+
+
+def pair_sum(kept, got, squares):
+    return call(pair_kernel, [shaped(got.shape, BF16)], got.size, kept, got, squares)[0]
+
+
+def scaled(parts):
+    rows, tokens = parts.shape
+    block = rows // (TARGETS // 2) - 16
+    return call(scale_kernel, [shaped((block, tokens), BF16)], rows * tokens, parts)[0]
 
 
 def on_device(
@@ -513,11 +586,9 @@
     along_z = [[x * Z_RING + z for z in range(Z_RING)] for x in range(rows)]
     along_x = [[x * Z_RING + z for x in range(rows)] for z in range(Z_RING)]
     weight = lax.all_gather(
-        out_weight.T, "seq", axis=0, tiled=True, axis_index_groups=along_x
-    )
-    weight = lax.all_gather(weight, "seq", axis=0, tiled=True, axis_index_groups=along_z)
-    rim = jnp.concatenate([x_in[tokens - RIM :], bc_in[tokens - RIM :]], axis=1)
-    rim = lax.ppermute(rim, "seq", [(i, i + 1) for i in range(count - 1)])
+        out_weight.T, "seq", axis=0, tiled=True, axis_index_groups=along_z
+    )
+    rim = lax.ppermute(rim_source(x_in, bc_in), "seq", [(i, i + 1) for i in range(count - 1)])
     place = jnp.stack(
         [lax.axis_index("seq") // Z_RING, lax.axis_index("tp")]
     ).astype(jnp.int32)[None]
@@ -527,13 +598,22 @@
     )
     xc_rim, bcc_rim, pieces = add_rim(rim, x_in, bc_in, conv_x, conv_bc, cum, tail, state)
     pieces = lax.all_to_all(pieces, "seq", 0, 0, tiled=True, axis_index_groups=along_z)
-    totals = row_total(pieces, width, rows)
+    own, reach, c_part, weight = local(
+        xc, xc_rim, bcc, bcc_rim, cum, logstep, z_gate, d_skip[None], weight
+    )
+    weight = lax.all_gather(weight, "seq", axis=0, tiled=True, axis_index_groups=along_x)
+    totals = row_total(pieces, width, rows, c_part)
     totals = lax.all_to_all(totals, "seq", 0, 0, tiled=True, axis_index_groups=along_x)
     pieces = scan(pieces, totals, place, width)
     pieces = lax.all_to_all(pieces, "seq", 0, 0, tiled=True, axis_index_groups=along_z)
-    own, reach, c_part = local(xc, xc_rim, bcc, bcc_rim, cum, logstep, z_gate, d_skip[None])
-    partial = back(own, reach, c_part, pieces, weight, norm_gain, place)
-    return scaled(lax.psum_scatter(partial, "tp", scatter_dimension=0, tiled=True)).T
+
+    given, gated, squares = back(own, reach, c_part, pieces, weight, norm_gain, place)
+    got = lax.ppermute(given, "tp", [(i, i ^ 1) for i in range(TARGETS)])
+    kept = kept_part(gated, weight, place)
+    parts = pair_sum(kept, got, squares)
+    along_y = [[core + 2 * y for y in range(TARGETS // 2)] for core in range(2)]
+    parts = lax.all_to_all(parts, "tp", 0, 0, tiled=True, axis_index_groups=along_y)
+    return scaled(parts).T
 
 
 def solution(mesh):

time: 169 us -> 170 us (level)
  waiting for transfers between devices: 84.8 us -> 34.7 us
  blocking collectives: 12.8 us -> 55.8 us
  Pallas kernels: 15.6 us -> 26.1 us
  local copies, waits for them, and re-layouts: 12.8 us -> 7.24 us
  starting transfers between devices: 27.8 us -> 31.7 us
    reduce_scatter x1 -> x0, waiting for transfers between devices: 45.6 us -> none  [on_device(): lax.psum_scatter(partial, 'tp', scatter_dimension=0, tiled=True)]
    all_to_all x0 -> x1, blocking collectives: none -> 22.1 us  [on_device(): lax.all_to_all(parts, 'tp', 0, 0, tiled=True, axis_index_groups=along_y)]
    all_gather x1, blocking collectives: 12.8 us -> 33.6 us  [on_device(): lax.all_gather(out_weight.T, 'seq', axis=0, tiled=True, axis_index_groups...]
    pallas_call x6 -> x10, Pallas kernels: 10.2 us -> 26.1 us  [call(): pl.pallas_call(body, out_shape=outs, in_specs=[pl.BlockSpec(memory_space=...]
    ppermute x1 -> x2, starting transfers between devices: 3.07 us -> 14.8 us  [the longest x1 9.79 us: on_device(): got = lax.ppermute(given, 'tp', [(i, i ^ 1) for i in range(TARGETS)])]
    all_to_all x2, starting transfers between devices: 21.4 us -> 13 us  [on_device(): lax.all_to_all(pieces, 'seq', 0, 0, tiled=True, axis_index_groups=along_z)]
    all_gather x1, waiting for transfers between devices: 11.4 us -> 4.96 us  [on_device(): lax.all_gather(weight, 'seq', axis=0, tiled=True, axis_index_groups=along_x)]
    pallas_call x1 -> x0, Pallas kernels: 5.48 us -> none  [back(): pl.pallas_call(back_kernel, out_shape=out, in_specs=[pl.BlockSpec(memory_...]
  transfers between devices with their start and end apart: 6 -> 6, of which waited for: 5 -> 4; matrix products, arithmetic and copies ran while one was open for 1% -> 0% of each run, Pallas kernels for 6% -> 7%
where the time goes in v3:
time: 170 us; the launch traced here: 169 us
  blocking collectives  55.8 us (33%)
  waiting for transfers between devices  34.7 us (20%)
  starting transfers between devices  31.7 us (19%)
  Pallas kernels  26.1 us (15%)
  between operations  13.6 us (8%)
  local copies, waits for them, and re-layouts  7.24 us (4%)
    all_gather x1, blocking collectives, on_device(): lax.all_gather(out_weight.T, 'seq', axis=0, tiled=True, axis_index_groups...  33.6 us
    pallas_call x10, Pallas kernels, call(): pl.pallas_call(body, out_shape=outs, in_specs=[pl.BlockSpec(memory_space=...  26.1 us
    all_to_all x2, waiting for transfers between devices, on_device(): lax.all_to_all(pieces, 'seq', 0, 0, tiled=True, axis_index_groups=along_z)  24 us
    all_to_all x1, blocking collectives, on_device(): lax.all_to_all(parts, 'tp', 0, 0, tiled=True, axis_index_groups=along_y)  22.1 us
    all_to_all x2, starting transfers between devices, on_device(): lax.all_to_all(pieces, 'seq', 0, 0, tiled=True, axis_index_groups=along_z)  13 us
    ppermute x1, starting transfers between devices, on_device(): got = lax.ppermute(given, 'tp', [(i, i ^ 1) for i in range(TARGETS)])  9.79 us
    unnamed x32, local copies, waits for them, and re-layouts  6.65 us
    all_to_all x1, waiting for transfers between devices, on_device(): lax.all_to_all(totals, 'seq', 0, 0, tiled=True, axis_index_groups=along_x)  5.64 us
  transfers between devices with their start and end apart: 6, of which 4 were waited for; matrix products, arithmetic and copies ran while one was open for 0% of the time, Pallas kernels for 7%

profile of v3, /device:TPU:1, one launch (start us, length us, event | category | flops | bytes accessed | tf_op | source)
XLA Modules:
  0.0 169.2 jit_solution(9977954476688106224)
XLA Ops:
  6.5 1.3 shard_map.110
  7.9 5.0 %collective-permute-start = (bf16[16,896]{1,0:T(8,128)(2,1)}, bf16[16,896]{1,0:T(8,128)(2,1)}, u32[]{:S(2)}, u32[]{:S(2)}) collective-permute-start(bf16[16,896]{1,0:T(8,128)(2,1)} %shard_map.110), channel_id=1, source_target_pairs={{0,8},{8,16},{16,24},{24,32},{32,40},{40,48},{48,56},{56,64},{64,7... | collective-permute-start | bytes 86024 | tf_op jit(solution)/shard_map/ppermute | solution.py:591
  12.9 33.6 %all_gather.6.w_ref = bf16[640,640]{1,0:T(8,128)(2,1)} all-gather(bf16[40,640]{1,0:T(8,128)(2,1)} %bitcast.22), channel_id=1, replica_groups={{0,8,16,24,32,40,48,56,64,72,80,88,96,104,112,120},{128,136,144,152,160..., dimensions={0}, use_global_device_ids=true | all-gather | bytes 870400 | tf_op jit(solution)/shard_map/all_gather | solution.py:588
  46.5 5.0 %shard_map.109 = (bf16[512,640]{1,0:T(8,128)(2,1)}, bf16[512,256]{1,0:T(8,128)(2,1)}, f32[16,512]{1,0:T(8,128)}, f32[16,512]{1,0:T(8,128)}, f32[128,640]{1,0:T(8,128)}, /*index=5*/f32[16,640]{1,0:T(8,128)}) custom-call(bf16[512,640]{1,0:T(8,128)(2,1)} %x_hbm.5, bf16[512,256]{1,0:T(8,128)(2,1)} %bc_hbm.5, bf16[10,512]{1,0:T(8,128)(2,1)} %bitcast.23, ...), custom_call_target="tpu_custom_call" | custom-call | flops 335544320 | bytes 2293840 | tf_op jit(solution)/shard_map/pallas_call | solution.py:44
  51.5 2.8 %shard_map.111 = (bf16[16,640]{1,0:T(8,128)(2,1)}, bf16[16,256]{1,0:T(8,128)(2,1)}, bf16[768,128]{1,0:T(8,128)(2,1)}) custom-call(bf16[16,896]{1,0:T(8,128)(2,1)} %collective-permute-done.rim_ref, bf16[512,640]{1,0:T(8,128)(2,1)} %x_hbm.5, bf16[512,256]{1,0:T(8,128)(2,1)} %bc_hbm.5, f32[4,640]{1,0:T(4,128)} %tap_x_hbm.3, f32[4,256]{1,0:T(4,128)} %tap_bc_hbm.3, ...), custom_call_target="tpu_custom_call" | custom-call | flops 20971520 | bytes 1587200 | tf_op jit(solution)/shard_map/pallas_call | solution.py:44
  54.4 1.1 copy-done.4
  55.5 0.7 copy-done.9
  56.2 0.7 copy-done.11
  56.9 0.7 copy-done.13
  57.6 2.5 %shard_map.112 = (f32[512,640]{1,0:T(8,128)S(1)}, f32[512,640]{1,0:T(8,128)S(1)}, bf16[512,128]{1,0:T(8,128)(2,1)S(1)}, bf16[640,640]{1,0:T(8,128)(2,1)}) custom-call(bf16[512,640]{1,0:T(8,128)(2,1)S(1)} %copy-done.4, bf16[16,640]{1,0:T(8,128)(2,1)S(1)} %copy-done.9, bf16[512,256]{1,0:T(8,128)(2,1)S(1)} %copy-done.6, ...), custom_call_target="tpu_custom_call", output_to_operand_aliasing={{3}: (8, {})} | custom-call | flops 503316480 | bytes 6058024 | tf_op jit(solution)/shard_map/pallas_call | solution.py:44
  60.1 1.1 copy-done.1
  61.2 1.1 copy-done.2
  62.2 0.0 all-gather.2.cloned.1.call-update
  62.3 8.2 %all-to-all-start = ((bf16[16,48,128]{2,1,0:T(8,128)(2,1)}), bf16[16,48,128]{2,1,0:T(8,128)(2,1)S(1)}, u32[]{:S(2)}, u32[]{:S(2)}) async-start(bf16[16,48,128]{2,1,0:T(8,128)(2,1)} %bitcast.5), calls=%async_computation | async-start | bytes 393216 | tf_op jit(solution)/shard_map/all_to_all | solution.py:600
  70.5 12.3 %all-to-all-done = bf16[16,48,128]{2,1,0:T(8,128)(2,1)S(1)} async-done(((bf16[16,48,128]{2,1,0:T(8,128)(2,1)}), bf16[16,48,128]{2,1,0:T(8,128)(2,1)S(1)}, u32[]{:S(2)}, u32[]{:S(2)}) %all-to-all-start) | async-done | bytes 196640 | tf_op jit(solution)/shard_map/all_to_all | solution.py:600
  82.8 0.8 shard_map.113
  83.6 4.0 %all-to-all-start.1 = ((f32[4,48,128]{2,1,0:T(8,128)}), f32[4,48,128]{2,1,0:T(8,128)S(1)}, u32[]{:S(2)}, u32[]{:S(2)}) async-start(f32[4,48,128]{2,1,0:T(8,128)} %shard_map.113), calls=%async_computation.1 | async-start | bytes 196608 | tf_op jit(solution)/shard_map/all_to_all | solution.py:606
  87.6 0.1 add_bitcast_fusion.refs_2_.place_ref
  87.7 5.6 %all-to-all-done.1.refs_1_ = f32[4,48,128]{2,1,0:T(8,128)S(1)} async-done(((f32[4,48,128]{2,1,0:T(8,128)}), f32[4,48,128]{2,1,0:T(8,128)S(1)}, u32[]{:S(2)}, u32[]{:S(2)}) %all-to-all-start.1) | async-done | bytes 98336 | tf_op jit(solution)/shard_map/all_to_all | solution.py:606
  93.3 1.4 shard_map.114
  94.7 4.7 %all-to-all-start.2 = ((bf16[16,48,128]{2,1,0:T(8,128)(2,1)}), bf16[16,48,128]{2,1,0:T(8,128)(2,1)S(1)}, u32[]{:S(2)}, u32[]{:S(2)}) async-start(bf16[16,48,128]{2,1,0:T(8,128)(2,1)} %bitcast.10), calls=%async_computation.2 | async-start | bytes 393216 | tf_op jit(solution)/shard_map/all_to_all | solution.py:608
  99.4 0.6 broadcast_in_dim.19.gain_ref
  100.0 11.7 %all-to-all-done.2 = bf16[16,48,128]{2,1,0:T(8,128)(2,1)S(1)} async-done(((bf16[16,48,128]{2,1,0:T(8,128)(2,1)}), bf16[16,48,128]{2,1,0:T(8,128)(2,1)S(1)}, u32[]{:S(2)}, u32[]{:S(2)}) %all-to-all-start.2) | async-done | bytes 196640 | tf_op jit(solution)/shard_map/all_to_all | solution.py:608
  111.8 5.0 %all-gather.2.cloned.1.call-done.w_hbm = bf16[2560,640]{1,0:T(8,128)(2,1)} async-done(((bf16[640,640]{1,0:T(8,128)(2,1)}), bf16[2560,640]{1,0:T(8,128)(2,1)}) %all-gather.2.cloned.1.call-update) | async-done | bytes 3276816 | tf_op jit(solution)/shard_map/all_gather | solution.py:604
  116.7 6.0 %shard_map.115 = (bf16[1344,512]{1,0:T(8,128)(2,1)}, bf16[512,640]{1,0:T(8,128)(2,1)}, bf16[16,512]{1,0:T(8,128)(2,1)}) custom-call(f32[512,640]{1,0:T(8,128)} %copy-done.1, f32[512,640]{1,0:T(8,128)} %copy-done.2, bf16[512,128]{1,0:T(8,128)(2,1)} %copy-done.5, bf16[768,128]{1,0:T(8,128)(2,1)} %bitcast.21, ...), custom_call_target="tpu_custom_call" | custom-call | flops 922746880 | bytes 8276488 | tf_op jit(solution)/shard_map/pallas_call | solution.py:44
  122.7 9.8 %collective-permute-start.1 = (bf16[1344,512]{1,0:T(8,128)(2,1)}, bf16[1344,512]{1,0:T(8,128)(2,1)S(1)}, u32[]{:S(2)}, u32[]{:S(2)}) collective-permute-start(bf16[1344,512]{1,0:T(8,128)(2,1)} %get-tuple-element.35), channel_id=1, source_target_pairs={{0,1},{1,0},{2,3},{3,2},{4,5},{5,4},{6,7},{7,6},{8,9},{9,8},{10,11... | collective-permute-start | bytes 4128776 | tf_op jit(solution)/shard_map/ppermute | solution.py:611
  132.6 5.1 %shard_map.116.kept_ref = bf16[1280,512]{1,0:T(8,128)(2,1)} custom-call(bf16[512,640]{1,0:T(8,128)(2,1)} %get-tuple-element.34.gated_ref, bf16[2560,640]{1,0:T(8,128)(2,1)} %all-gather.2.cloned.1.call-done.w_hbm, s32[1,2]{1,0:T(1,128)} %copy-done.12), custom_call_target="tpu_custom_call" | custom-call | flops 838860800 | bytes 5242888 | tf_op jit(solution)/shard_map/pallas_call | solution.py:44
  137.6 0.0 collective-permute-done.1.got_ref
  137.7 1.3 copy-done
  139.0 0.3 shard_map.117
  139.3 22.1 %all_to_all.38 = bf16[4,336,512]{2,1,0:T(8,128)(2,1)S(1)} all-to-all(bf16[4,336,512]{2,1,0:T(8,128)(2,1)S(1)} %bitcast.16), channel_id=1, replica_groups={{0,2,4,6},{1,3,5,7},{8,10,12,14},{9,11,13,15},{16,18,20,22},{17,19,21,2..., dimensions={0} | all-to-all | bytes 2752512 | tf_op jit(solution)/shard_map/all_to_all | solution.py:615
  161.4 0.9 shard_map.118
  (27 shorter events, 0.1 us)
Async XLA Ops:
  6.5 110.2 %all-gather.2.cloned.1.call-start = ((), (), s32[]{:S(2)}) async-start(), calls=%async_computation.4 | async-start | bytes 4096000 | tf_op jit(solution)/shard_map/all_gather | solution.py:604
  7.9 43.6 %collective-permute-start = (bf16[16,896]{1,0:T(8,128)(2,1)}, bf16[16,896]{1,0:T(8,128)(2,1)}, u32[]{:S(2)}, u32[]{:S(2)}) collective-permute-start(bf16[16,896]{1,0:T(8,128)(2,1)} %shard_map.110), channel_id=1, source_target_pairs={{0,8},{8,16},{16,24},{24,32},{32,40},{40,48},{48,56},{56,64},{64,7... | collective-permute-start | bytes 86024 | tf_op jit(solution)/shard_map/ppermute | solution.py:591
  46.5 7.9 %copy-start.3 = (bf16[512,640]{1,0:T(8,128)(2,1)S(1)}, bf16[512,640]{1,0:T(8,128)(2,1)}, u32[]{:S(2)}) copy-start(bf16[512,640]{1,0:T(8,128)(2,1)} %z_hbm.1) | copy-start | bytes 1966084
  51.5 2.9 %copy-start.6 = (bf16[512,256]{1,0:T(8,128)(2,1)S(1)}, bf16[512,256]{1,0:T(8,128)(2,1)}, u32[]{:S(2)}) copy-start(bf16[512,256]{1,0:T(8,128)(2,1)} %get-tuple-element.26.bcc_ref) | copy-start | bytes 786436
  51.5 2.9 %copy-start.7 = (f32[16,512]{1,0:T(8,128)S(1)}, f32[16,512]{1,0:T(8,128)}, u32[]{:S(2)}) copy-start(f32[16,512]{1,0:T(8,128)} %get-tuple-element.22.cum_ref) | copy-start | bytes 98308
  51.5 2.9 %copy-start.8 = (f32[16,512]{1,0:T(8,128)S(1)}, f32[16,512]{1,0:T(8,128)}, u32[]{:S(2)}) copy-start(f32[16,512]{1,0:T(8,128)} %get-tuple-element.28.logstep_ref) | copy-start | bytes 98308
  54.4 1.1 copy-start.4
  55.5 0.7 copy-start.9
  56.2 0.7 copy-start.11
  56.9 0.7 copy-start.13
  60.1 1.1 copy-start.1
  61.2 1.1 copy-start.2
  62.2 32.5 %copy-start.5 = (bf16[512,128]{1,0:T(8,128)(2,1)}, bf16[512,128]{1,0:T(8,128)(2,1)S(1)}, u32[]{:S(2)}) copy-start(bf16[512,128]{1,0:T(8,128)(2,1)S(1)} %get-tuple-element.31.refs_1_.c_ref) | copy-start | bytes 393220
  62.2 37.2 %copy-start.15 = (f32[640]{0:T(1024)S(1)}, f32[640]{0:T(1024)}, u32[]{:S(2)}) copy-start(f32[640]{0:T(1024)} %param.20) | copy-start | bytes 7684
  62.3 20.6 %all-to-all-start = ((bf16[16,48,128]{2,1,0:T(8,128)(2,1)}), bf16[16,48,128]{2,1,0:T(8,128)(2,1)S(1)}, u32[]{:S(2)}, u32[]{:S(2)}) async-start(bf16[16,48,128]{2,1,0:T(8,128)(2,1)} %bitcast.5), calls=%async_computation | async-start | bytes 393216 | tf_op jit(solution)/shard_map/all_to_all | solution.py:600
  83.6 9.7 %all-to-all-start.1 = ((f32[4,48,128]{2,1,0:T(8,128)}), f32[4,48,128]{2,1,0:T(8,128)S(1)}, u32[]{:S(2)}, u32[]{:S(2)}) async-start(f32[4,48,128]{2,1,0:T(8,128)} %shard_map.113), calls=%async_computation.1 | async-start | bytes 196608 | tf_op jit(solution)/shard_map/all_to_all | solution.py:606
  87.7 29.0 %copy-start.12 = (s32[1,2]{1,0:T(1,128)}, s32[1,2]{1,0:T(1,128)S(1)}, u32[]{:S(2)}) copy-start(s32[1,2]{1,0:T(1,128)S(1)} %add_bitcast_fusion.refs_2_.place_ref) | copy-start | bytes 28
  94.7 17.1 %all-to-all-start.2 = ((bf16[16,48,128]{2,1,0:T(8,128)(2,1)}), bf16[16,48,128]{2,1,0:T(8,128)(2,1)S(1)}, u32[]{:S(2)}, u32[]{:S(2)}) async-start(bf16[16,48,128]{2,1,0:T(8,128)(2,1)} %bitcast.10), calls=%async_computation.2 | async-start | bytes 393216 | tf_op jit(solution)/shard_map/all_to_all | solution.py:608
  111.8 5.0 %copy-start.14 = (bf16[16,48,128]{2,1,0:T(8,128)(2,1)}, bf16[16,48,128]{2,1,0:T(8,128)(2,1)S(1)}, u32[]{:S(2)}) copy-start(bf16[16,48,128]{2,1,0:T(8,128)(2,1)S(1)} %all-to-all-done.2) | copy-start | bytes 589828
  122.7 14.9 %collective-permute-start.1 = (bf16[1344,512]{1,0:T(8,128)(2,1)}, bf16[1344,512]{1,0:T(8,128)(2,1)S(1)}, u32[]{:S(2)}, u32[]{:S(2)}) collective-permute-start(bf16[1344,512]{1,0:T(8,128)(2,1)} %get-tuple-element.35), channel_id=1, source_target_pairs={{0,1},{1,0},{2,3},{3,2},{4,5},{5,4},{6,7},{7,6},{8,9},{9,8},{10,11... | collective-permute-start | bytes 4128776 | tf_op jit(solution)/shard_map/ppermute | solution.py:611
  132.5 5.1 %copy-start.10 = (bf16[16,512]{1,0:T(8,128)(2,1)S(1)}, bf16[16,512]{1,0:T(8,128)(2,1)}, u32[]{:S(2)}) copy-start(bf16[16,512]{1,0:T(8,128)(2,1)} %get-tuple-element.36.square_ref) | copy-start | bytes 49156
  137.6 1.3 copy-start
Sparse Core Ops, SparseCore 0:
  62.4 54.2 all-gather.1

commit v4 on v3

--- a/solution.py
+++ b/solution.py
@@ -16,6 +16,7 @@
 Z_RING = 16
 PIECE = 48
 TARGETS = 8
+Z_STRIDE = 4
 FULL = 63
 EPSILON = 1e-05
 HIGH = lax.Precision.HIGHEST
@@ -201,10 +202,9 @@
 
 
 def local_kernel(
-    xc_ref, xc_rim_ref, bcc_ref, bcc_rim_ref, cum_ref, logstep_ref, z_hbm, skip_hbm, w_ref,
-    own_ref, reach_ref, c_ref, w_out_ref, held, xs, bs, z_ref, skip_ref, sems,
+    xc_ref, xc_rim_ref, bcc_ref, bcc_rim_ref, cum_ref, logstep_ref, z_hbm, skip_hbm,
+    own_ref, reach_ref, c_ref, held, xs, bs, z_ref, skip_ref, sems,
 ):
-    del w_ref, w_out_ref
     copies = fetch(sems, (skip_hbm, skip_ref), (z_hbm, z_ref))
     tokens, width = xc_ref.shape
     xs[...] = xc_ref[...]
@@ -262,8 +262,7 @@
     return both + jnp.where(even, pltpu.roll(both, LANES - 1, 1), pltpu.roll(both, 1, 1))
 
 
-def total_kernel(blocks, in_ref, after_ref, out_ref, wide):
-    del after_ref
+def total_kernel(blocks, in_ref, out_ref, wide):
     wide[...] = in_ref[...].astype(F32)
     carry = [jnp.zeros((8, LANES), F32)] * blocks
     passed = jnp.zeros((8, LANES), F32)
@@ -317,15 +316,15 @@
 
 
 def fetch_half(w_hbm, w_ref, half, sems):
-    block = w_hbm.shape[0] // TARGETS
+    parts = w_ref.shape[0] // (TARGETS // 2 * Z_STRIDE)
     return fetch(
         sems,
         *[
             (
-                w_hbm.at[pl.ds(pl.multiple_of((2 * y + half) * block, block), block), :],
-                w_ref.at[y * block : (y + 1) * block, :],
+                w_hbm.at[pl.ds(pl.multiple_of((2 * k + half) * parts, parts), parts), :],
+                w_ref.at[k * parts : (k + 1) * parts, :],
             )
-            for y in range(TARGETS // 2)
+            for k in range(TARGETS // 2 * Z_STRIDE)
         ],
     )
 
@@ -376,7 +375,8 @@
     block = w_ref.shape[0] // (TARGETS // 2)
     for y in range(TARGETS // 2):
         rows = slice(y * block, (y + 1) * block)
-        copies[y].wait()
+        for copy in copies[y * Z_STRIDE : (y + 1) * Z_STRIDE]:
+            copy.wait()
         out_ref[rows, :] = dot(w_ref[rows, :], gated_ref[...], NT).astype(BF16)
 
 
@@ -404,7 +404,16 @@
     mixed = in_ref[0:block, :].astype(F32)
     for y in range(1, parts):
         mixed += in_ref[y * each : y * each + block, :].astype(F32)
-    out_ref[...] = (mixed * scale).astype(BF16)
+    mixed *= scale
+    shard = block // (2 * Z_STRIDE)
+    out_ref[...] = jnp.concatenate(
+        [
+            mixed[(low * 2 + high) * shard : (low * 2 + high + 1) * shard, :]
+            for high in range(2)
+            for low in range(Z_STRIDE)
+        ],
+        axis=0,
+    ).astype(BF16)
 
 
 def shaped(shape, dtype):
@@ -468,24 +477,21 @@
     )
 
 
-def local(xc, xc_rim, bcc, bcc_rim, cum, logstep, z_gate, d_skip, weight):
+def local(xc, xc_rim, bcc, bcc_rim, cum, logstep, z_gate, d_skip):
     tokens, width = xc.shape
     return call(
         local_kernel,
-        [shaped((tokens, width), F32)] * 2
-        + [shaped((tokens, STATE), BF16), shaped(weight.shape, BF16)],
+        [shaped((tokens, width), F32)] * 2 + [shaped((tokens, STATE), BF16)],
         12 * tokens * width * STATE,
-        xc, xc_rim, bcc, bcc_rim, cum, logstep, z_gate, d_skip, weight,
-        spaces=[pltpu.VMEM] * 6 + [pltpu.HBM] * 3,
-        out_spaces=[pltpu.VMEM] * 3 + [pltpu.HBM],
-        aliases={8: 3},
+        xc, xc_rim, bcc, bcc_rim, cum, logstep, z_gate, d_skip,
+        spaces=[pltpu.VMEM] * 6 + [pltpu.HBM] * 2,
         scratch=(pltpu.VMEM((STATE, width), F32),)
         + held_like(xc, bcc, z_gate, d_skip)
         + (pltpu.SemaphoreType.DMA((2,)),),
     )
 
 
-def row_total(pieces, width, peers, after):
+def row_total(pieces, width, peers):
     def body(*refs):
         total_kernel(width // LANES, *refs)
 
@@ -493,8 +499,7 @@
         body,
         [shaped((peers, PIECE, LANES), F32)],
         pieces.size * 4,
-        pieces, after,
-        spaces=[pltpu.VMEM, pl.ANY],
+        pieces,
         scratch=(pltpu.VMEM(pieces.shape, F32),),
     )[0]
 
@@ -545,7 +550,7 @@
             pltpu.VMEM(pieces.shape, F32),
             pltpu.VMEM((STATE, width), F32),
             pltpu.VMEM((half, width), BF16),
-            pltpu.SemaphoreType.DMA((parts,)),
+            pltpu.SemaphoreType.DMA((parts * Z_STRIDE,)),
         ),
     )
 
@@ -562,7 +567,7 @@
         vmem=FULL - 2,
         scratch=(
             pltpu.VMEM((half, width), BF16),
-            pltpu.SemaphoreType.DMA((TARGETS // 2,)),
+            pltpu.SemaphoreType.DMA((TARGETS // 2 * Z_STRIDE,)),
         ),
     )[0]
 
@@ -585,9 +590,12 @@
     rows = count // Z_RING
     along_z = [[x * Z_RING + z for z in range(Z_RING)] for x in range(rows)]
     along_x = [[x * Z_RING + z for x in range(rows)] for z in range(Z_RING)]
-    weight = lax.all_gather(
-        out_weight.T, "seq", axis=0, tiled=True, axis_index_groups=along_z
-    )
+    spans = range(Z_RING // Z_STRIDE)
+    far = [[x * Z_RING + h * Z_STRIDE + l for h in spans] for x in range(rows) for l in range(Z_STRIDE)]
+    near = [[x * Z_RING + h * Z_STRIDE + l for l in range(Z_STRIDE)] for x in range(rows) for h in spans]
+    weight = out_weight.T
+    for groups in (far, near, along_x):
+        weight = lax.all_gather(weight, "seq", axis=0, tiled=True, axis_index_groups=groups)
     rim = lax.ppermute(rim_source(x_in, bc_in), "seq", [(i, i + 1) for i in range(count - 1)])
     place = jnp.stack(
         [lax.axis_index("seq") // Z_RING, lax.axis_index("tp")]
@@ -598,11 +606,8 @@
     )
     xc_rim, bcc_rim, pieces = add_rim(rim, x_in, bc_in, conv_x, conv_bc, cum, tail, state)
     pieces = lax.all_to_all(pieces, "seq", 0, 0, tiled=True, axis_index_groups=along_z)
-    own, reach, c_part, weight = local(
-        xc, xc_rim, bcc, bcc_rim, cum, logstep, z_gate, d_skip[None], weight
-    )
-    weight = lax.all_gather(weight, "seq", axis=0, tiled=True, axis_index_groups=along_x)
-    totals = row_total(pieces, width, rows, c_part)
+    own, reach, c_part = local(xc, xc_rim, bcc, bcc_rim, cum, logstep, z_gate, d_skip[None])
+    totals = row_total(pieces, width, rows)
     totals = lax.all_to_all(totals, "seq", 0, 0, tiled=True, axis_index_groups=along_x)
     pieces = scan(pieces, totals, place, width)
     pieces = lax.all_to_all(pieces, "seq", 0, 0, tiled=True, axis_index_groups=along_z)

time: 170 us -> 164 us (0.965)
  waiting for transfers between devices: 34.7 us -> 24.4 us
  blocking collectives: 55.8 us -> 62.4 us
    all_gather x1 -> x2, blocking collectives: 33.6 us -> 40.3 us  [on_device(): lax.all_gather(weight, 'seq', axis=0, tiled=True, axis_index_groups=groups)]
    all_to_all x2, waiting for transfers between devices: 24 us -> 18.7 us  [on_device(): lax.all_to_all(pieces, 'seq', 0, 0, tiled=True, axis_index_groups=along_z)]
    all_gather x1, waiting for transfers between devices: 4.96 us -> 0.01 us  [on_device(): lax.all_gather(weight, 'seq', axis=0, tiled=True, axis_index_groups=groups)]
    ppermute x1, starting transfers between devices: 4.98 us -> 2.07 us  [on_device(): lax.ppermute(rim_source(x_in, bc_in), 'seq', [(i, i + 1) for i in range(c...]
    ppermute x1, starting transfers between devices: 9.79 us -> 12.7 us  [on_device(): got = lax.ppermute(given, 'tp', [(i, i ^ 1) for i in range(TARGETS)])]
    unnamed x32 -> x34, local copies, waits for them, and re-layouts: 6.65 us -> 5.44 us
  transfers between devices with their start and end apart: 6 -> 6, of which waited for: 4 -> 3; matrix products, arithmetic and copies ran while one was open for 0% -> 0% of each run, Pallas kernels for 7% -> 12%
where the time goes in v4:
time: 164 us
  blocking collectives  62.4 us (38%)
  starting transfers between devices  30.7 us (19%)
  Pallas kernels  26.3 us (16%)
  waiting for transfers between devices  24.4 us (15%)
  between operations  13.6 us (8%)
  local copies, waits for them, and re-layouts  6.03 us (4%)
    all_gather x2, blocking collectives, on_device(): lax.all_gather(weight, 'seq', axis=0, tiled=True, axis_index_groups=groups)  40.3 us
    pallas_call x10, Pallas kernels, call(): pl.pallas_call(body, out_shape=outs, in_specs=[pl.BlockSpec(memory_space=...  26.3 us
    all_to_all x1, blocking collectives, on_device(): lax.all_to_all(parts, 'tp', 0, 0, tiled=True, axis_index_groups=along_y)  22.1 us
    all_to_all x2, waiting for transfers between devices, on_device(): lax.all_to_all(pieces, 'seq', 0, 0, tiled=True, axis_index_groups=along_z)  18.7 us
    ppermute x1, starting transfers between devices, on_device(): got = lax.ppermute(given, 'tp', [(i, i ^ 1) for i in range(TARGETS)])  12.7 us
    all_to_all x2, starting transfers between devices, on_device(): lax.all_to_all(pieces, 'seq', 0, 0, tiled=True, axis_index_groups=along_z)  11.8 us
    all_to_all x1, waiting for transfers between devices, on_device(): lax.all_to_all(totals, 'seq', 0, 0, tiled=True, axis_index_groups=along_x)  5.64 us
    unnamed x34, local copies, waits for them, and re-layouts  5.44 us
  transfers between devices with their start and end apart: 6, of which 3 were waited for; matrix products, arithmetic and copies ran while one was open for 0% of the time, Pallas kernels for 12%

profile of v4, /device:TPU:1, one launch (start us, length us, event | category | flops | bytes accessed | tf_op | source)
XLA Modules:
  0.0 163.5 jit_solution(12007866081985674573)
XLA Ops:
  6.5 24.8 %all_gather.9 = bf16[160,640]{1,0:T(8,128)(2,1)S(1)} all-gather(bf16[40,640]{1,0:T(8,128)(2,1)} %bitcast.23), channel_id=1, replica_groups={{0,32,64,96},{8,40,72,104},{16,48,80,112},{24,56,88,120},{128,160,192,2..., dimensions={0}, use_global_device_ids=true | all-gather | bytes 256000 | tf_op jit(solution)/shard_map/all_gather | solution.py:598
  31.3 15.5 %all_gather.10 = bf16[640,640]{1,0:T(8,128)(2,1)} all-gather(bf16[160,640]{1,0:T(8,128)(2,1)S(1)} %all_gather.9), channel_id=1, replica_groups={{0,8,16,24},{32,40,48,56},{64,72,80,88},{96,104,112,120},{128,136,144,1..., dimensions={0}, use_global_device_ids=true | all-gather | bytes 1024000 | tf_op jit(solution)/shard_map/all_gather | solution.py:598
  46.8 0.0 all-gather.2.cloned.1.call-update
  46.8 1.4 shard_map.110
  48.2 2.1 %collective-permute-start = (bf16[16,896]{1,0:T(8,128)(2,1)}, bf16[16,896]{1,0:T(8,128)(2,1)S(1)}, u32[]{:S(2)}, u32[]{:S(2)}) collective-permute-start(bf16[16,896]{1,0:T(8,128)(2,1)} %shard_map.110), channel_id=1, source_target_pairs={{0,8},{8,16},{16,24},{24,32},{32,40},{40,48},{48,56},{56,64},{64,7... | collective-permute-start | bytes 86024 | tf_op jit(solution)/shard_map/ppermute | solution.py:599
  50.3 4.9 %shard_map.109 = (bf16[512,640]{1,0:T(8,128)(2,1)}, bf16[512,256]{1,0:T(8,128)(2,1)}, f32[16,512]{1,0:T(8,128)}, f32[16,512]{1,0:T(8,128)}, f32[128,640]{1,0:T(8,128)}, /*index=5*/f32[16,640]{1,0:T(8,128)}) custom-call(bf16[512,640]{1,0:T(8,128)(2,1)} %x_hbm.5, bf16[512,256]{1,0:T(8,128)(2,1)} %bc_hbm.5, bf16[10,512]{1,0:T(8,128)(2,1)} %bitcast.24, ...), custom_call_target="tpu_custom_call" | custom-call | flops 335544320 | bytes 2293840 | tf_op jit(solution)/shard_map/pallas_call | solution.py:45
  55.2 0.0 collective-permute-done.rim_ref
  55.2 0.6 copy-done.15
  55.8 2.9 %shard_map.111 = (bf16[16,640]{1,0:T(8,128)(2,1)}, bf16[16,256]{1,0:T(8,128)(2,1)}, bf16[768,128]{1,0:T(8,128)(2,1)}) custom-call(bf16[16,896]{1,0:T(8,128)(2,1)} %copy-done.15, bf16[512,640]{1,0:T(8,128)(2,1)} %x_hbm.5, bf16[512,256]{1,0:T(8,128)(2,1)} %bc_hbm.5, f32[4,640]{1,0:T(4,128)} %tap_x_hbm.3, f32[4,256]{1,0:T(4,128)} %tap_bc_hbm.3, ...), custom_call_target="tpu_custom_call" | custom-call | flops 20971520 | bytes 1587200 | tf_op jit(solution)/shard_map/pallas_call | solution.py:45
  58.7 0.0 copy-start.16
  58.8 6.8 %all-to-all-start = ((bf16[16,48,128]{2,1,0:T(8,128)(2,1)}), bf16[16,48,128]{2,1,0:T(8,128)(2,1)S(1)}, u32[]{:S(2)}, u32[]{:S(2)}) async-start(bf16[16,48,128]{2,1,0:T(8,128)(2,1)} %bitcast.22), calls=%async_computation | async-start | bytes 393216 | tf_op jit(solution)/shard_map/all_to_all | solution.py:608
  65.6 12.4 %all-to-all-done = bf16[16,48,128]{2,1,0:T(8,128)(2,1)S(1)} async-done(((bf16[16,48,128]{2,1,0:T(8,128)(2,1)}), bf16[16,48,128]{2,1,0:T(8,128)(2,1)S(1)}, u32[]{:S(2)}, u32[]{:S(2)}) %all-to-all-start) | async-done | bytes 196640 | tf_op jit(solution)/shard_map/all_to_all | solution.py:608
  78.0 0.8 shard_map.113
  78.8 4.1 %all-to-all-start.1 = ((f32[4,48,128]{2,1,0:T(8,128)}), f32[4,48,128]{2,1,0:T(8,128)S(1)}, u32[]{:S(2)}, u32[]{:S(2)}) async-start(f32[4,48,128]{2,1,0:T(8,128)} %shard_map.113), calls=%async_computation.1 | async-start | bytes 196608 | tf_op jit(solution)/shard_map/all_to_all | solution.py:611
  82.9 0.1 add_bitcast_fusion.refs_2_.place_ref
  83.0 5.6 %all-to-all-done.1.refs_1_ = f32[4,48,128]{2,1,0:T(8,128)S(1)} async-done(((f32[4,48,128]{2,1,0:T(8,128)}), f32[4,48,128]{2,1,0:T(8,128)S(1)}, u32[]{:S(2)}, u32[]{:S(2)}) %all-to-all-start.1) | async-done | bytes 98336 | tf_op jit(solution)/shard_map/all_to_all | solution.py:611
  88.6 1.4 shard_map.114
  90.0 5.0 %all-to-all-start.2 = ((bf16[16,48,128]{2,1,0:T(8,128)(2,1)}), bf16[16,48,128]{2,1,0:T(8,128)(2,1)S(1)}, u32[]{:S(2)}, u32[]{:S(2)}) async-start(bf16[16,48,128]{2,1,0:T(8,128)(2,1)} %bitcast.9), calls=%async_computation.2 | async-start | bytes 393216 | tf_op jit(solution)/shard_map/all_to_all | solution.py:613
  94.9 0.6 broadcast_in_dim.19.gain_ref
  95.6 2.5 %shard_map.112 = (f32[512,640]{1,0:T(8,128)S(1)}, f32[512,640]{1,0:T(8,128)S(1)}, bf16[512,128]{1,0:T(8,128)(2,1)S(1)}) custom-call(bf16[512,640]{1,0:T(8,128)(2,1)S(1)} %copy-done.11, bf16[16,640]{1,0:T(8,128)(2,1)S(1)} %copy-done.8, bf16[512,256]{1,0:T(8,128)(2,1)S(1)} %copy-done.12, bf16[16,256]{1,0:T(8,128)(2,1)S(1)} %copy-done.9, ...), custom_call_target="tpu_custom_call" | custom-call | flops 503316480 | bytes 4419624 | tf_op jit(solution)/shard_map/pallas_call | solution.py:45
  98.1 1.1 copy-done.1
  99.2 1.1 copy-done.2
  100.3 0.6 copy-done.3
  100.9 6.3 %all-to-all-done.2 = bf16[16,48,128]{2,1,0:T(8,128)(2,1)S(1)} async-done(((bf16[16,48,128]{2,1,0:T(8,128)(2,1)}), bf16[16,48,128]{2,1,0:T(8,128)(2,1)S(1)}, u32[]{:S(2)}, u32[]{:S(2)}) %all-to-all-start.2) | async-done | bytes 196640 | tf_op jit(solution)/shard_map/all_to_all | solution.py:613
  107.3 0.7 copy-done.14
  107.9 6.1 %shard_map.115 = (bf16[1344,512]{1,0:T(8,128)(2,1)}, bf16[512,640]{1,0:T(8,128)(2,1)}, bf16[16,512]{1,0:T(8,128)(2,1)}) custom-call(f32[512,640]{1,0:T(8,128)} %copy-done.1, f32[512,640]{1,0:T(8,128)} %copy-done.2, bf16[512,128]{1,0:T(8,128)(2,1)} %copy-done.3, bf16[768,128]{1,0:T(8,128)(2,1)} %bitcast.21, ...), custom_call_target="tpu_custom_call" | custom-call | flops 922746880 | bytes 8276488 | tf_op jit(solution)/shard_map/pallas_call | solution.py:45
  114.1 12.7 %collective-permute-start.1 = (bf16[1344,512]{1,0:T(8,128)(2,1)}, bf16[1344,512]{1,0:T(8,128)(2,1)S(1)}, u32[]{:S(2)}, u32[]{:S(2)}) collective-permute-start(bf16[1344,512]{1,0:T(8,128)(2,1)} %get-tuple-element.33), channel_id=1, source_target_pairs={{0,1},{1,0},{2,3},{3,2},{4,5},{5,4},{6,7},{7,6},{8,9},{9,8},{10,11... | collective-permute-start | bytes 4128776 | tf_op jit(solution)/shard_map/ppermute | solution.py:616
  126.8 5.2 %shard_map.116.kept_ref = bf16[1280,512]{1,0:T(8,128)(2,1)} custom-call(bf16[512,640]{1,0:T(8,128)(2,1)} %get-tuple-element.32.gated_ref, bf16[2560,640]{1,0:T(8,128)(2,1)} %all-gather.2.cloned.1.call-done.w_hbm, s32[1,2]{1,0:T(1,128)} %copy-done.6), custom_call_target="tpu_custom_call" | custom-call | flops 838860800 | bytes 5242888 | tf_op jit(solution)/shard_map/pallas_call | solution.py:45
  132.0 1.3 copy-done
  133.3 0.3 shard_map.117
  133.6 22.1 %all_to_all.38 = bf16[4,336,512]{2,1,0:T(8,128)(2,1)S(1)} all-to-all(bf16[4,336,512]{2,1,0:T(8,128)(2,1)S(1)} %bitcast.16), channel_id=1, replica_groups={{0,2,4,6},{1,3,5,7},{8,10,12,14},{9,11,13,15},{16,18,20,22},{17,19,21,2..., dimensions={0} | all-to-all | bytes 2752512 | tf_op jit(solution)/shard_map/all_to_all | solution.py:620
  155.8 0.9 shard_map.118
  (30 shorter events, 0.1 us)
Async XLA Ops:
  6.5 100.7 %all-gather.2.cloned.1.call-start = ((), (), s32[]{:S(2)}) async-start(), calls=%async_computation.4 | async-start | bytes 4096000 | tf_op jit(solution)/shard_map/all_gather | solution.py:598
  48.2 7.0 %collective-permute-start = (bf16[16,896]{1,0:T(8,128)(2,1)}, bf16[16,896]{1,0:T(8,128)(2,1)S(1)}, u32[]{:S(2)}, u32[]{:S(2)}) collective-permute-start(bf16[16,896]{1,0:T(8,128)(2,1)} %shard_map.110), channel_id=1, source_target_pairs={{0,8},{8,16},{16,24},{24,32},{32,40},{40,48},{48,56},{56,64},{64,7... | collective-permute-start | bytes 86024 | tf_op jit(solution)/shard_map/ppermute | solution.py:599
  55.2 0.6 copy-start.15
  55.8 39.7 %copy-start.4 = (f32[16,512]{1,0:T(8,128)S(1)}, f32[16,512]{1,0:T(8,128)}, u32[]{:S(2)}) copy-start(f32[16,512]{1,0:T(8,128)} %get-tuple-element.21.cum_ref) | copy-start | bytes 98308
  55.8 39.7 %copy-start.7 = (bf16[512,640]{1,0:T(8,128)(2,1)S(1)}, bf16[512,640]{1,0:T(8,128)(2,1)}, u32[]{:S(2)}) copy-start(bf16[512,640]{1,0:T(8,128)(2,1)} %z_hbm.1) | copy-start | bytes 1966084
  55.8 39.7 %copy-start.10 = (f32[10]{0:T(128)S(1)}, f32[10]{0:T(128)}, u32[]{:S(2)}) copy-start(f32[10]{0:T(128)} %param.19) | copy-start | bytes 124
  55.8 39.7 %copy-start.12 = (bf16[512,256]{1,0:T(8,128)(2,1)S(1)}, bf16[512,256]{1,0:T(8,128)(2,1)}, u32[]{:S(2)}) copy-start(bf16[512,256]{1,0:T(8,128)(2,1)} %get-tuple-element.25.bcc_ref) | copy-start | bytes 786436
  58.7 36.2 %copy-start.16 = (f32[640]{0:T(1024)S(1)}, f32[640]{0:T(1024)}, u32[]{:S(2)}) copy-start(f32[640]{0:T(1024)} %param.20) | copy-start | bytes 7684
  58.7 36.8 %copy-start.8 = (bf16[16,640]{1,0:T(8,128)(2,1)S(1)}, bf16[16,640]{1,0:T(8,128)(2,1)}, u32[]{:S(2)}) copy-start(bf16[16,640]{1,0:T(8,128)(2,1)} %get-tuple-element.24.xc_rim_ref) | copy-start | bytes 61444
  58.7 36.8 %copy-start.9 = (bf16[16,256]{1,0:T(8,128)(2,1)S(1)}, bf16[16,256]{1,0:T(8,128)(2,1)}, u32[]{:S(2)}) copy-start(bf16[16,256]{1,0:T(8,128)(2,1)} %get-tuple-element.26.bcc_rim_ref) | copy-start | bytes 24580
  58.7 36.8 %copy-start.11 = (bf16[512,640]{1,0:T(8,128)(2,1)S(1)}, bf16[512,640]{1,0:T(8,128)(2,1)}, u32[]{:S(2)}) copy-start(bf16[512,640]{1,0:T(8,128)(2,1)} %get-tuple-element.20.xc_ref) | copy-start | bytes 1966084
  58.7 36.8 %copy-start.13 = (f32[16,512]{1,0:T(8,128)S(1)}, f32[16,512]{1,0:T(8,128)}, u32[]{:S(2)}) copy-start(f32[16,512]{1,0:T(8,128)} %get-tuple-element.27.logstep_ref) | copy-start | bytes 98308
  58.8 19.2 %all-to-all-start = ((bf16[16,48,128]{2,1,0:T(8,128)(2,1)}), bf16[16,48,128]{2,1,0:T(8,128)(2,1)S(1)}, u32[]{:S(2)}, u32[]{:S(2)}) async-start(bf16[16,48,128]{2,1,0:T(8,128)(2,1)} %bitcast.22), calls=%async_computation | async-start | bytes 393216 | tf_op jit(solution)/shard_map/all_to_all | solution.py:608
  78.8 9.8 %all-to-all-start.1 = ((f32[4,48,128]{2,1,0:T(8,128)}), f32[4,48,128]{2,1,0:T(8,128)S(1)}, u32[]{:S(2)}, u32[]{:S(2)}) async-start(f32[4,48,128]{2,1,0:T(8,128)} %shard_map.113), calls=%async_computation.1 | async-start | bytes 196608 | tf_op jit(solution)/shard_map/all_to_all | solution.py:611
  83.0 15.1 %copy-start.6 = (s32[1,2]{1,0:T(1,128)}, s32[1,2]{1,0:T(1,128)S(1)}, u32[]{:S(2)}) copy-start(s32[1,2]{1,0:T(1,128)S(1)} %add_bitcast_fusion.refs_2_.place_ref) | copy-start | bytes 28
  90.0 17.3 %all-to-all-start.2 = ((bf16[16,48,128]{2,1,0:T(8,128)(2,1)}), bf16[16,48,128]{2,1,0:T(8,128)(2,1)S(1)}, u32[]{:S(2)}, u32[]{:S(2)}) async-start(bf16[16,48,128]{2,1,0:T(8,128)(2,1)} %bitcast.9), calls=%async_computation.2 | async-start | bytes 393216 | tf_op jit(solution)/shard_map/all_to_all | solution.py:613
  98.1 1.1 copy-start.1
  99.2 1.1 copy-start.2
  100.3 0.7 copy-start.3
  107.3 0.7 copy-start.14
  114.1 17.9 %collective-permute-start.1 = (bf16[1344,512]{1,0:T(8,128)(2,1)}, bf16[1344,512]{1,0:T(8,128)(2,1)S(1)}, u32[]{:S(2)}, u32[]{:S(2)}) collective-permute-start(bf16[1344,512]{1,0:T(8,128)(2,1)} %get-tuple-element.33), channel_id=1, source_target_pairs={{0,1},{1,0},{2,3},{3,2},{4,5},{5,4},{6,7},{7,6},{8,9},{9,8},{10,11... | collective-permute-start | bytes 4128776 | tf_op jit(solution)/shard_map/ppermute | solution.py:616
  126.8 5.2 %copy-start.5 = (bf16[16,512]{1,0:T(8,128)(2,1)S(1)}, bf16[16,512]{1,0:T(8,128)(2,1)}, u32[]{:S(2)}) copy-start(bf16[16,512]{1,0:T(8,128)(2,1)} %get-tuple-element.34.square_ref) | copy-start | bytes 49156
  132.0 1.3 copy-start
Sparse Core Ops, SparseCore 0:
  46.9 50.9 all-gather.1

commit v5 on v4

--- a/solution.py
+++ b/solution.py
@@ -16,7 +16,6 @@
 Z_RING = 16
 PIECE = 48
 TARGETS = 8
-Z_STRIDE = 4
 FULL = 63
 EPSILON = 1e-05
 HIGH = lax.Precision.HIGHEST
@@ -315,25 +314,9 @@
         copy.wait()
 
 
-def fetch_half(w_hbm, w_ref, half, sems):
-    parts = w_ref.shape[0] // (TARGETS // 2 * Z_STRIDE)
-    return fetch(
-        sems,
-        *[
-            (
-                w_hbm.at[pl.ds(pl.multiple_of((2 * k + half) * parts, parts), parts), :],
-                w_ref.at[k * parts : (k + 1) * parts, :],
-            )
-            for k in range(TARGETS // 2 * Z_STRIDE)
-        ],
-    )
-
-
-def back_kernel(
-    own_ref, reach_ref, c_ref, piece_ref, w_hbm, gain_ref, place_ref,
-    out_ref, gated_ref, square_ref, wide, state, w_ref, sems,
+def gate_kernel(
+    own_ref, reach_ref, c_ref, piece_ref, gain_ref, place_ref, gated_ref, square_ref, wide, state,
 ):
-    copies = fetch_half(w_hbm, w_ref, 1 - place_ref[0, 1] % 2, sems)
     tokens, width = own_ref.shape
     blocks = width // LANES
     each = STATE // Z_RING
@@ -355,29 +338,52 @@
     row = iota((16, tokens), 0)
     mine = 2 * place_ref[0, 1]
     zero = jnp.zeros((16, tokens), F32)
-    squares = jnp.where(
+    square_ref[...] = jnp.where(
         row == mine, hi.astype(F32), jnp.where(row == mine + 1, lo.astype(F32), zero)
     ).astype(BF16)
-    square_ref[...] = squares
-    for copy in copies:
+
+
+def project_half(w_hbm, gated, half, out_ref, w_ref, acc, sems, gap):
+    span = w_ref.shape[0]
+    parts = 2
+    step = span // parts
+    copies = fetch(
+        sems,
+        *[
+            (
+                w_hbm.at[pl.ds(pl.multiple_of(half * span + k * step, step), step), :],
+                w_ref.at[k * step : (k + 1) * step, :],
+            )
+            for k in range(parts)
+        ],
+    )
+    for k, copy in enumerate(copies):
+        rows = slice(k * step, (k + 1) * step)
         copy.wait()
-    block = w_ref.shape[0] // (TARGETS // 2)
-    for y in range(TARGETS // 2):
-        to = y * (block + 16)
-        out_ref[to : to + block, :] = dot(
-            w_ref[y * block : (y + 1) * block, :], gated_ref[...], NT
+        acc[rows, :] = dot(w_ref[rows, :], gated, NT)
+    block = span // (TARGETS // 2)
+    shard = block // (Z_RING // 2)
+    for x in range(TARGETS // 2):
+        to = x * (block + gap)
+        out_ref[to : to + block, :] = jnp.concatenate(
+            [
+                acc[z * block // 2 + x * shard : z * block // 2 + (x + 1) * shard, :]
+                for z in range(Z_RING // 2)
+            ],
+            axis=0,
         ).astype(BF16)
-        out_ref[to + block : to + block + 16, :] = squares
-
-
-def kept_kernel(gated_ref, w_hbm, place_ref, out_ref, w_ref, sems):
-    copies = fetch_half(w_hbm, w_ref, place_ref[0, 1] % 2, sems)
-    block = w_ref.shape[0] // (TARGETS // 2)
-    for y in range(TARGETS // 2):
-        rows = slice(y * block, (y + 1) * block)
-        for copy in copies[y * Z_STRIDE : (y + 1) * Z_STRIDE]:
-            copy.wait()
-        out_ref[rows, :] = dot(w_ref[rows, :], gated_ref[...], NT).astype(BF16)
+
+
+def given_kernel(gated_ref, square_ref, w_hbm, place_ref, out_ref, w_ref, acc, sems):
+    half = 1 - place_ref[0, 1] % 2
+    project_half(w_hbm, gated_ref[...], half, out_ref, w_ref, acc, sems, 16)
+    each = out_ref.shape[0] // (TARGETS // 2)
+    for x in range(TARGETS // 2):
+        out_ref[(x + 1) * each - 16 : (x + 1) * each, :] = square_ref[...]
+
+
+def kept_kernel(gated_ref, w_hbm, place_ref, out_ref, w_ref, acc, sems):
+    project_half(w_hbm, gated_ref[...], place_ref[0, 1] % 2, out_ref, w_ref, acc, sems, 0)
 
 
 def pair_kernel(kept_ref, got_ref, square_ref, out_ref):
@@ -404,16 +410,7 @@
     mixed = in_ref[0:block, :].astype(F32)
     for y in range(1, parts):
         mixed += in_ref[y * each : y * each + block, :].astype(F32)
-    mixed *= scale
-    shard = block // (2 * Z_STRIDE)
-    out_ref[...] = jnp.concatenate(
-        [
-            mixed[(low * 2 + high) * shard : (low * 2 + high + 1) * shard, :]
-            for high in range(2)
-            for low in range(Z_STRIDE)
-        ],
-        axis=0,
-    ).astype(BF16)
+    out_ref[...] = (mixed * scale).astype(BF16)
 
 
 def shaped(shape, dtype):
@@ -530,29 +527,39 @@
     )[0]
 
 
-def back(own, reach, c_part, pieces, weight, norm_gain, place):
+def gate(own, reach, c_part, pieces, norm_gain, place):
     tokens, width = own.shape
-    columns = weight.shape[0]
-    half = columns // 2
-    parts = TARGETS // 2
-    return call(
-        back_kernel,
-        [
-            shaped((half + parts * 16, tokens), BF16),
-            shaped((tokens, width), BF16),
-            shaped((16, tokens), BF16),
-        ],
-        2 * tokens * width * (half + STATE),
-        own, reach, c_part, pieces, weight, norm_gain[None], place,
-        spaces=[pltpu.VMEM] * 4 + [pltpu.HBM, pltpu.VMEM, pltpu.SMEM],
-        vmem=FULL - 5,
-        scratch=(
-            pltpu.VMEM(pieces.shape, F32),
-            pltpu.VMEM((STATE, width), F32),
-            pltpu.VMEM((half, width), BF16),
-            pltpu.SemaphoreType.DMA((parts * Z_STRIDE,)),
-        ),
-    )
+    return call(
+        gate_kernel,
+        [shaped((tokens, width), BF16), shaped((16, tokens), BF16)],
+        2 * tokens * width * STATE,
+        own, reach, c_part, pieces, norm_gain[None], place,
+        spaces=[pltpu.VMEM] * 5 + [pltpu.SMEM],
+        scratch=(pltpu.VMEM(pieces.shape, F32), pltpu.VMEM((STATE, width), F32)),
+    )
+
+
+def half_scratch(weight, tokens):
+    columns, width = weight.shape
+    return (
+        pltpu.VMEM((columns // 2, width), BF16),
+        pltpu.VMEM((columns // 2, tokens), F32),
+        pltpu.SemaphoreType.DMA((2,)),
+    )
+
+
+def given_part(gated, squares, weight, place):
+    tokens, width = gated.shape
+    half = weight.shape[0] // 2
+    return call(
+        given_kernel,
+        [shaped((half + TARGETS // 2 * 16, tokens), BF16)],
+        2 * tokens * width * half,
+        gated, squares, weight, place,
+        spaces=[pltpu.VMEM, pltpu.VMEM, pltpu.HBM, pltpu.SMEM],
+        vmem=FULL - 3,
+        scratch=half_scratch(weight, tokens),
+    )[0]
 
 
 def kept_part(gated, weight, place):
@@ -564,11 +571,8 @@
         2 * tokens * width * half,
         gated, weight, place,
         spaces=[pltpu.VMEM, pltpu.HBM, pltpu.SMEM],
-        vmem=FULL - 2,
-        scratch=(
-            pltpu.VMEM((half, width), BF16),
-            pltpu.SemaphoreType.DMA((TARGETS // 2 * Z_STRIDE,)),
-        ),
+        vmem=FULL - 3,
+        scratch=half_scratch(weight, tokens),
     )[0]
 
 
@@ -590,11 +594,8 @@
     rows = count // Z_RING
     along_z = [[x * Z_RING + z for z in range(Z_RING)] for x in range(rows)]
     along_x = [[x * Z_RING + z for x in range(rows)] for z in range(Z_RING)]
-    spans = range(Z_RING // Z_STRIDE)
-    far = [[x * Z_RING + h * Z_STRIDE + l for h in spans] for x in range(rows) for l in range(Z_STRIDE)]
-    near = [[x * Z_RING + h * Z_STRIDE + l for l in range(Z_STRIDE)] for x in range(rows) for h in spans]
     weight = out_weight.T
-    for groups in (far, near, along_x):
+    for groups in (along_x, along_z):
         weight = lax.all_gather(weight, "seq", axis=0, tiled=True, axis_index_groups=groups)
     rim = lax.ppermute(rim_source(x_in, bc_in), "seq", [(i, i + 1) for i in range(count - 1)])
     place = jnp.stack(
@@ -612,7 +613,8 @@
     pieces = scan(pieces, totals, place, width)
     pieces = lax.all_to_all(pieces, "seq", 0, 0, tiled=True, axis_index_groups=along_z)
 
-    given, gated, squares = back(own, reach, c_part, pieces, weight, norm_gain, place)
+    gated, squares = gate(own, reach, c_part, pieces, norm_gain, place)
+    given = given_part(gated, squares, weight, place)
     got = lax.ppermute(given, "tp", [(i, i ^ 1) for i in range(TARGETS)])
     kept = kept_part(gated, weight, place)
     parts = pair_sum(kept, got, squares)

time: 164 us -> 159 us (0.970)
  blocking collectives: 62.4 us -> 34.9 us
  waiting for transfers between devices: 24.4 us -> 40.2 us
  starting transfers between devices: 30.7 us -> 37.4 us
    all_gather x2 -> x1, blocking collectives: 40.3 us -> 12.7 us  [on_device(): lax.all_gather(weight, 'seq', axis=0, tiled=True, axis_index_groups=groups)]
    all_gather x1, waiting for transfers between devices: 0.01 us -> 12.4 us  [on_device(): lax.all_gather(weight, 'seq', axis=0, tiled=True, axis_index_groups=groups)]
    all_to_all x2, starting transfers between devices: 11.8 us -> 20.6 us  [on_device(): lax.all_to_all(pieces, 'seq', 0, 0, tiled=True, axis_index_groups=along_z)]
    all_to_all x2, waiting for transfers between devices: 18.7 us -> 23.2 us  [on_device(): lax.all_to_all(pieces, 'seq', 0, 0, tiled=True, axis_index_groups=along_z)]
    ppermute x1, starting transfers between devices: 12.7 us -> 10.5 us  [on_device(): got = lax.ppermute(given, 'tp', [(i, i ^ 1) for i in range(TARGETS)])]
    pallas_call x10 -> x11, Pallas kernels: 26.3 us -> 26 us  [call(): pl.pallas_call(body, out_shape=outs, in_specs=[pl.BlockSpec(memory_space=...]
    unnamed x34 -> x30, local copies, waits for them, and re-layouts: 5.44 us -> 5.59 us
  transfers between devices with their start and end apart: 6 -> 6, of which waited for: 3 -> 4; matrix products, arithmetic and copies ran while one was open for 0% -> 0% of each run, Pallas kernels for 12% -> 13%
where the time goes in v5:
time: 159 us; the launch traced here: 158 us
  waiting for transfers between devices  40.2 us (25%)
  starting transfers between devices  37.4 us (24%)
  blocking collectives  34.9 us (22%)
  Pallas kernels  26 us (16%)
  between operations  13.7 us (9%)
  local copies, waits for them, and re-layouts  5.59 us (4%)
    pallas_call x11, Pallas kernels, call(): pl.pallas_call(body, out_shape=outs, in_specs=[pl.BlockSpec(memory_space=...  26 us
    all_to_all x2, waiting for transfers between devices, on_device(): lax.all_to_all(pieces, 'seq', 0, 0, tiled=True, axis_index_groups=along_z)  23.2 us
    all_to_all x1, blocking collectives, on_device(): lax.all_to_all(parts, 'tp', 0, 0, tiled=True, axis_index_groups=along_y)  22.2 us
    all_to_all x2, starting transfers between devices, on_device(): lax.all_to_all(pieces, 'seq', 0, 0, tiled=True, axis_index_groups=along_z)  20.6 us
    all_gather x1, blocking collectives, on_device(): lax.all_gather(weight, 'seq', axis=0, tiled=True, axis_index_groups=groups)  12.7 us
    all_gather x1, waiting for transfers between devices, on_device(): lax.all_gather(weight, 'seq', axis=0, tiled=True, axis_index_groups=groups)  12.4 us
    ppermute x1, starting transfers between devices, on_device(): got = lax.ppermute(given, 'tp', [(i, i ^ 1) for i in range(TARGETS)])  10.5 us
    unnamed x30, local copies, waits for them, and re-layouts  5.59 us
  transfers between devices with their start and end apart: 6, of which 4 were waited for; matrix products, arithmetic and copies ran while one was open for 0% of the time, Pallas kernels for 13%

profile of v5, /device:TPU:1, one launch (start us, length us, event | category | flops | bytes accessed | tf_op | source)
XLA Modules:
  0.0 157.9 jit_solution(5173201676047097453)
XLA Ops:
  6.5 12.7 %all_gather.6 = bf16[160,640]{1,0:T(8,128)(2,1)} all-gather(bf16[40,640]{1,0:T(8,128)(2,1)} %bitcast.23), channel_id=1, replica_groups={{0,128,256,384},{8,136,264,392},{16,144,272,400},{24,152,280,408},{32,1..., dimensions={0}, use_global_device_ids=true | all-gather | bytes 256000 | tf_op jit(solution)/shard_map/all_gather | solution.py:599
  19.3 0.0 all-gather.2.cloned.1.call-update
  19.3 1.4 shard_map.110
  20.6 3.1 %collective-permute-start = (bf16[16,896]{1,0:T(8,128)(2,1)}, bf16[16,896]{1,0:T(8,128)(2,1)S(1)}, u32[]{:S(2)}, u32[]{:S(2)}) collective-permute-start(bf16[16,896]{1,0:T(8,128)(2,1)} %shard_map.110), channel_id=1, source_target_pairs={{0,8},{8,16},{16,24},{24,32},{32,40},{40,48},{48,56},{56,64},{64,7... | collective-permute-start | bytes 86024 | tf_op jit(solution)/shard_map/ppermute | solution.py:600
  23.7 4.9 %shard_map.109 = (bf16[512,640]{1,0:T(8,128)(2,1)}, bf16[512,256]{1,0:T(8,128)(2,1)}, f32[16,512]{1,0:T(8,128)}, f32[16,512]{1,0:T(8,128)}, f32[128,640]{1,0:T(8,128)}, /*index=5*/f32[16,640]{1,0:T(8,128)}) custom-call(bf16[512,640]{1,0:T(8,128)(2,1)} %x_hbm.5, bf16[512,256]{1,0:T(8,128)(2,1)} %bc_hbm.5, bf16[10,512]{1,0:T(8,128)(2,1)} %bitcast.24, ...), custom_call_target="tpu_custom_call" | custom-call | flops 335544320 | bytes 2293840 | tf_op jit(solution)/shard_map/pallas_call | solution.py:44
  28.7 0.6 copy-done.13
  29.3 2.8 %shard_map.111 = (bf16[16,640]{1,0:T(8,128)(2,1)}, bf16[16,256]{1,0:T(8,128)(2,1)}, bf16[768,128]{1,0:T(8,128)(2,1)}) custom-call(bf16[16,896]{1,0:T(8,128)(2,1)} %copy-done.13, bf16[512,640]{1,0:T(8,128)(2,1)} %x_hbm.5, bf16[512,256]{1,0:T(8,128)(2,1)} %bc_hbm.5, f32[4,640]{1,0:T(4,128)} %tap_x_hbm.3, f32[4,256]{1,0:T(4,128)} %tap_bc_hbm.3, ...), custom_call_target="tpu_custom_call" | custom-call | flops 20971520 | bytes 1587200 | tf_op jit(solution)/shard_map/pallas_call | solution.py:44
  32.2 14.2 %all-to-all-start = ((bf16[16,48,128]{2,1,0:T(8,128)(2,1)}), bf16[16,48,128]{2,1,0:T(8,128)(2,1)S(1)}, u32[]{:S(2)}, u32[]{:S(2)}) async-start(bf16[16,48,128]{2,1,0:T(8,128)(2,1)} %bitcast.22), calls=%async_computation | async-start | bytes 393216 | tf_op jit(solution)/shard_map/all_to_all | solution.py:609
  46.4 14.6 %all-to-all-done = bf16[16,48,128]{2,1,0:T(8,128)(2,1)S(1)} async-done(((bf16[16,48,128]{2,1,0:T(8,128)(2,1)}), bf16[16,48,128]{2,1,0:T(8,128)(2,1)S(1)}, u32[]{:S(2)}, u32[]{:S(2)}) %all-to-all-start) | async-done | bytes 196640 | tf_op jit(solution)/shard_map/all_to_all | solution.py:609
  61.0 0.8 shard_map.113
  61.8 3.3 %all-to-all-start.1 = ((f32[4,48,128]{2,1,0:T(8,128)}), f32[4,48,128]{2,1,0:T(8,128)S(1)}, u32[]{:S(2)}, u32[]{:S(2)}) async-start(f32[4,48,128]{2,1,0:T(8,128)} %shard_map.113), calls=%async_computation.1 | async-start | bytes 196608 | tf_op jit(solution)/shard_map/all_to_all | solution.py:612
  65.1 0.1 add_bitcast_fusion.refs_2_.place_ref
  65.2 4.5 %all-to-all-done.1.refs_1_ = f32[4,48,128]{2,1,0:T(8,128)S(1)} async-done(((f32[4,48,128]{2,1,0:T(8,128)}), f32[4,48,128]{2,1,0:T(8,128)S(1)}, u32[]{:S(2)}, u32[]{:S(2)}) %all-to-all-start.1) | async-done | bytes 98336 | tf_op jit(solution)/shard_map/all_to_all | solution.py:612
  69.7 1.4 shard_map.114
  71.0 6.4 %all-to-all-start.2 = ((bf16[16,48,128]{2,1,0:T(8,128)(2,1)}), bf16[16,48,128]{2,1,0:T(8,128)(2,1)S(1)}, u32[]{:S(2)}, u32[]{:S(2)}) async-start(bf16[16,48,128]{2,1,0:T(8,128)(2,1)} %bitcast.9), calls=%async_computation.2 | async-start | bytes 393216 | tf_op jit(solution)/shard_map/all_to_all | solution.py:614
  77.5 0.0 copy-start.6
  77.5 1.1 copy-done.6
  78.6 1.1 copy-done.10
  79.7 2.5 %shard_map.112 = (f32[512,640]{1,0:T(8,128)S(1)}, f32[512,640]{1,0:T(8,128)S(1)}, bf16[512,128]{1,0:T(8,128)(2,1)S(1)}) custom-call(bf16[512,640]{1,0:T(8,128)(2,1)S(1)} %copy-done.10, bf16[16,640]{1,0:T(8,128)(2,1)S(1)} %copy-done.7, bf16[512,256]{1,0:T(8,128)(2,1)S(1)} %copy-done.11, bf16[16,256]{1,0:T(8,128)(2,1)S(1)} %copy-done.8, ...), custom_call_target="tpu_custom_call" | custom-call | flops 503316480 | bytes 4419624 | tf_op jit(solution)/shard_map/pallas_call | solution.py:44
  82.2 8.6 %all-to-all-done.2 = bf16[16,48,128]{2,1,0:T(8,128)(2,1)S(1)} async-done(((bf16[16,48,128]{2,1,0:T(8,128)(2,1)}), bf16[16,48,128]{2,1,0:T(8,128)(2,1)S(1)}, u32[]{:S(2)}, u32[]{:S(2)}) %all-to-all-start.2) | async-done | bytes 196640 | tf_op jit(solution)/shard_map/all_to_all | solution.py:614
  90.8 1.5 shard_map.115
  92.3 0.9 copy-done.1
  93.2 0.6 copy-done.2
  93.8 12.4 %all-gather.2.cloned.1.call-done.w_hbm = bf16[2560,640]{1,0:T(8,128)(2,1)} async-done(((bf16[160,640]{1,0:T(8,128)(2,1)}), bf16[2560,640]{1,0:T(8,128)(2,1)}) %all-gather.2.cloned.1.call-update) | async-done | bytes 3276816 | tf_op jit(solution)/shard_map/all_gather | solution.py:599
  106.2 4.8 %shard_map.117 = bf16[1344,512]{1,0:T(8,128)(2,1)} custom-call(bf16[512,640]{1,0:T(8,128)(2,1)} %copy-done.1, bf16[16,512]{1,0:T(8,128)(2,1)} %copy-done.2, bf16[2560,640]{1,0:T(8,128)(2,1)} %all-gather.2.cloned.1.call-done.w_hbm, s32[1,2]{1,0:T(1,128)} %copy-done.5), custom_call_target="tpu_custom_call" | custom-call | flops 838860800 | bytes 5324808 | tf_op jit(solution)/shard_map/pallas_call | solution.py:44
  111.0 0.0 copy-start.3
  111.0 10.5 %collective-permute-start.1 = (bf16[1344,512]{1,0:T(8,128)(2,1)}, bf16[1344,512]{1,0:T(8,128)(2,1)S(1)}, u32[]{:S(2)}, u32[]{:S(2)}) collective-permute-start(bf16[1344,512]{1,0:T(8,128)(2,1)} %shard_map.117), channel_id=1, source_target_pairs={{0,1},{1,0},{2,3},{3,2},{4,5},{5,4},{6,7},{7,6},{8,9},{9,8},{10,11... | collective-permute-start | bytes 4128776 | tf_op jit(solution)/shard_map/ppermute | solution.py:618
  121.5 4.8 %shard_map.116.kept_ref = bf16[1280,512]{1,0:T(8,128)(2,1)} custom-call(bf16[512,640]{1,0:T(8,128)(2,1)} %copy-done.1, bf16[2560,640]{1,0:T(8,128)(2,1)} %all-gather.2.cloned.1.call-done.w_hbm, s32[1,2]{1,0:T(1,128)} %copy-done.5), custom_call_target="tpu_custom_call" | custom-call | flops 838860800 | bytes 5242888 | tf_op jit(solution)/shard_map/pallas_call | solution.py:44
  126.3 1.3 copy-done
  127.6 0.3 shard_map.118
  127.9 22.2 %all_to_all.38 = bf16[4,336,512]{2,1,0:T(8,128)(2,1)S(1)} all-to-all(bf16[4,336,512]{2,1,0:T(8,128)(2,1)S(1)} %bitcast.16), channel_id=1, replica_groups={{0,2,4,6},{1,3,5,7},{8,10,12,14},{9,11,13,15},{16,18,20,22},{17,19,21,2..., dimensions={0} | all-to-all | bytes 2752512 | tf_op jit(solution)/shard_map/all_to_all | solution.py:622
  150.2 0.9 shard_map.119
  (26 shorter events, 0.1 us)
Async XLA Ops:
  6.5 99.7 %all-gather.2.cloned.1.call-start = ((), (), s32[]{:S(2)}) async-start(), calls=%async_computation.4 | async-start | bytes 3481600 | tf_op jit(solution)/shard_map/all_gather | solution.py:599
  20.6 8.0 %collective-permute-start = (bf16[16,896]{1,0:T(8,128)(2,1)}, bf16[16,896]{1,0:T(8,128)(2,1)S(1)}, u32[]{:S(2)}, u32[]{:S(2)}) collective-permute-start(bf16[16,896]{1,0:T(8,128)(2,1)} %shard_map.110), channel_id=1, source_target_pairs={{0,8},{8,16},{16,24},{24,32},{32,40},{40,48},{48,56},{56,64},{64,7... | collective-permute-start | bytes 86024 | tf_op jit(solution)/shard_map/ppermute | solution.py:600
  28.7 0.6 copy-start.13
  29.3 48.2 %copy-start.14 = (f32[640]{0:T(1024)S(1)}, f32[640]{0:T(1024)}, u32[]{:S(2)}) copy-start(f32[640]{0:T(1024)} %param.20) | copy-start | bytes 7684
  29.3 48.2 %copy-start.4 = (f32[16,512]{1,0:T(8,128)S(1)}, f32[16,512]{1,0:T(8,128)}, u32[]{:S(2)}) copy-start(f32[16,512]{1,0:T(8,128)} %get-tuple-element.20.cum_ref) | copy-start | bytes 98308
  29.3 48.2 %copy-start.9 = (f32[10]{0:T(128)S(1)}, f32[10]{0:T(128)}, u32[]{:S(2)}) copy-start(f32[10]{0:T(128)} %param.19) | copy-start | bytes 124
  29.3 48.2 %copy-start.11 = (bf16[512,256]{1,0:T(8,128)(2,1)S(1)}, bf16[512,256]{1,0:T(8,128)(2,1)}, u32[]{:S(2)}) copy-start(bf16[512,256]{1,0:T(8,128)(2,1)} %get-tuple-element.24.bcc_ref) | copy-start | bytes 786436
  29.3 48.2 %copy-start.12 = (f32[16,512]{1,0:T(8,128)S(1)}, f32[16,512]{1,0:T(8,128)}, u32[]{:S(2)}) copy-start(f32[16,512]{1,0:T(8,128)} %get-tuple-element.26.logstep_ref) | copy-start | bytes 98308
  32.2 45.4 %copy-start.7 = (bf16[16,640]{1,0:T(8,128)(2,1)S(1)}, bf16[16,640]{1,0:T(8,128)(2,1)}, u32[]{:S(2)}) copy-start(bf16[16,640]{1,0:T(8,128)(2,1)} %get-tuple-element.23.xc_rim_ref) | copy-start | bytes 61444
  32.2 45.4 %copy-start.8 = (bf16[16,256]{1,0:T(8,128)(2,1)S(1)}, bf16[16,256]{1,0:T(8,128)(2,1)}, u32[]{:S(2)}) copy-start(bf16[16,256]{1,0:T(8,128)(2,1)} %get-tuple-element.25.bcc_rim_ref) | copy-start | bytes 24580
  32.2 28.8 %all-to-all-start = ((bf16[16,48,128]{2,1,0:T(8,128)(2,1)}), bf16[16,48,128]{2,1,0:T(8,128)(2,1)S(1)}, u32[]{:S(2)}, u32[]{:S(2)}) async-start(bf16[16,48,128]{2,1,0:T(8,128)(2,1)} %bitcast.22), calls=%async_computation | async-start | bytes 393216 | tf_op jit(solution)/shard_map/all_to_all | solution.py:609
  61.8 7.9 %all-to-all-start.1 = ((f32[4,48,128]{2,1,0:T(8,128)}), f32[4,48,128]{2,1,0:T(8,128)S(1)}, u32[]{:S(2)}, u32[]{:S(2)}) async-start(f32[4,48,128]{2,1,0:T(8,128)} %shard_map.113), calls=%async_computation.1 | async-start | bytes 196608 | tf_op jit(solution)/shard_map/all_to_all | solution.py:612
  65.2 25.7 %copy-start.5 = (s32[1,2]{1,0:T(1,128)}, s32[1,2]{1,0:T(1,128)S(1)}, u32[]{:S(2)}) copy-start(s32[1,2]{1,0:T(1,128)S(1)} %add_bitcast_fusion.refs_2_.place_ref) | copy-start | bytes 28
  71.0 19.8 %all-to-all-start.2 = ((bf16[16,48,128]{2,1,0:T(8,128)(2,1)}), bf16[16,48,128]{2,1,0:T(8,128)(2,1)S(1)}, u32[]{:S(2)}, u32[]{:S(2)}) async-start(bf16[16,48,128]{2,1,0:T(8,128)(2,1)} %bitcast.9), calls=%async_computation.2 | async-start | bytes 393216 | tf_op jit(solution)/shard_map/all_to_all | solution.py:614
  77.5 1.1 copy-start.6
  78.6 1.1 copy-start.10
  92.3 0.9 copy-start.1
  93.2 0.6 copy-start.2
  111.0 15.3 %copy-start.3 = (bf16[16,512]{1,0:T(8,128)(2,1)S(1)}, bf16[16,512]{1,0:T(8,128)(2,1)}, u32[]{:S(2)}) copy-start(bf16[16,512]{1,0:T(8,128)(2,1)} %copy-done.2) | copy-start | bytes 49156
  111.0 15.3 %collective-permute-start.1 = (bf16[1344,512]{1,0:T(8,128)(2,1)}, bf16[1344,512]{1,0:T(8,128)(2,1)S(1)}, u32[]{:S(2)}, u32[]{:S(2)}) collective-permute-start(bf16[1344,512]{1,0:T(8,128)(2,1)} %shard_map.117), channel_id=1, source_target_pairs={{0,1},{1,0},{2,3},{3,2},{4,5},{5,4},{6,7},{7,6},{8,9},{9,8},{10,11... | collective-permute-start | bytes 4128776 | tf_op jit(solution)/shard_map/ppermute | solution.py:618
  126.3 1.3 copy-start
Sparse Core Ops, SparseCore 0:
  19.4 86.7 all-gather.1

commit v6 on v5

--- a/solution.py
+++ b/solution.py
@@ -343,12 +343,15 @@
     ).astype(BF16)
 
 
-def project_half(w_hbm, gated, half, out_ref, w_ref, acc, sems, gap):
+def project_half(
+    gated_hbm, w_hbm, place_ref, half, out_hbm, gated, w_ref, acc, stage, sems, out_sems, gap
+):
     span = w_ref.shape[0]
-    parts = 2
+    parts = sems.shape[0] - 1
     step = span // parts
     copies = fetch(
         sems,
+        (gated_hbm, gated),
         *[
             (
                 w_hbm.at[pl.ds(pl.multiple_of(half * span + k * step, step), step), :],
@@ -357,33 +360,52 @@
             for k in range(parts)
         ],
     )
-    for k, copy in enumerate(copies):
+    copies[0].wait()
+    for k in range(parts):
         rows = slice(k * step, (k + 1) * step)
-        copy.wait()
-        acc[rows, :] = dot(w_ref[rows, :], gated, NT)
-    block = span // (TARGETS // 2)
+        copies[1 + k].wait()
+        acc[rows, :] = dot(w_ref[rows, :], gated[...], NT)
+    blocks = TARGETS // 2
+    block = span // blocks
     shard = block // (Z_RING // 2)
-    for x in range(TARGETS // 2):
-        to = x * (block + gap)
-        out_ref[to : to + block, :] = jnp.concatenate(
+    size = block + gap
+    sent = []
+    for back in range(blocks):
+        at = back * size
+        stage[at : at + block, :] = jnp.concatenate(
             [
-                acc[z * block // 2 + x * shard : z * block // 2 + (x + 1) * shard, :]
+                acc[z * block // 2 + back * shard : z * block // 2 + (back + 1) * shard, :]
                 for z in range(Z_RING // 2)
             ],
             axis=0,
         ).astype(BF16)
-
-
-def given_kernel(gated_ref, square_ref, w_hbm, place_ref, out_ref, w_ref, acc, sems):
-    half = 1 - place_ref[0, 1] % 2
-    project_half(w_hbm, gated_ref[...], half, out_ref, w_ref, acc, sems, 16)
-    each = out_ref.shape[0] // (TARGETS // 2)
+        to = pl.multiple_of(lax.rem(place_ref[0, 0] + blocks - back, blocks) * size, size)
+        copy = pltpu.make_async_copy(
+            stage.at[at : at + size, :], out_hbm.at[pl.ds(to, size), :], out_sems.at[back]
+        )
+        copy.start()
+        sent.append(copy)
+    for copy in sent:
+        copy.wait()
+
+
+def given_kernel(
+    gated_hbm, square_ref, w_hbm, place_ref, out_hbm, gated, w_ref, acc, stage, sems, out_sems
+):
+    size = stage.shape[0] // (TARGETS // 2)
     for x in range(TARGETS // 2):
-        out_ref[(x + 1) * each - 16 : (x + 1) * each, :] = square_ref[...]
-
-
-def kept_kernel(gated_ref, w_hbm, place_ref, out_ref, w_ref, acc, sems):
-    project_half(w_hbm, gated_ref[...], place_ref[0, 1] % 2, out_ref, w_ref, acc, sems, 0)
+        stage[(x + 1) * size - 16 : (x + 1) * size, :] = square_ref[...]
+    half = 1 - lax.rem(place_ref[0, 1], 2)
+    project_half(
+        gated_hbm, w_hbm, place_ref, half, out_hbm, gated, w_ref, acc, stage, sems, out_sems, 16
+    )
+
+
+def kept_kernel(gated_hbm, w_hbm, place_ref, out_hbm, gated, w_ref, acc, stage, sems, out_sems):
+    half = lax.rem(place_ref[0, 1], 2)
+    project_half(
+        gated_hbm, w_hbm, place_ref, half, out_hbm, gated, w_ref, acc, stage, sems, out_sems, 0
+    )
 
 
 def pair_kernel(kept_ref, got_ref, square_ref, out_ref):
@@ -539,26 +561,32 @@
     )
 
 
-def half_scratch(weight, tokens):
+def half_scratch(gated, weight, rows):
     columns, width = weight.shape
+    tokens = gated.shape[0]
     return (
+        *held_like(gated),
         pltpu.VMEM((columns // 2, width), BF16),
         pltpu.VMEM((columns // 2, tokens), F32),
-        pltpu.SemaphoreType.DMA((2,)),
+        pltpu.VMEM((rows, tokens), BF16),
+        pltpu.SemaphoreType.DMA((3,)),
+        pltpu.SemaphoreType.DMA((TARGETS // 2,)),
     )
 
 
 def given_part(gated, squares, weight, place):
     tokens, width = gated.shape
     half = weight.shape[0] // 2
+    rows = half + TARGETS // 2 * 16
     return call(
         given_kernel,
-        [shaped((half + TARGETS // 2 * 16, tokens), BF16)],
+        [shaped((rows, tokens), BF16)],
         2 * tokens * width * half,
         gated, squares, weight, place,
-        spaces=[pltpu.VMEM, pltpu.VMEM, pltpu.HBM, pltpu.SMEM],
-        vmem=FULL - 3,
-        scratch=half_scratch(weight, tokens),
+        spaces=[pltpu.HBM, pltpu.VMEM, pltpu.HBM, pltpu.SMEM],
+        out_spaces=[pltpu.HBM],
+        vmem=FULL - 2,
+        scratch=half_scratch(gated, weight, rows),
     )[0]
 
 
@@ -570,9 +598,10 @@
         [shaped((half, tokens), BF16)],
         2 * tokens * width * half,
         gated, weight, place,
-        spaces=[pltpu.VMEM, pltpu.HBM, pltpu.SMEM],
-        vmem=FULL - 3,
-        scratch=half_scratch(weight, tokens),
+        spaces=[pltpu.HBM, pltpu.HBM, pltpu.SMEM],
+        out_spaces=[pltpu.HBM],
+        vmem=FULL - 2,
+        scratch=half_scratch(gated, weight, half),
     )[0]
 
 
@@ -594,9 +623,17 @@
     rows = count // Z_RING
     along_z = [[x * Z_RING + z for z in range(Z_RING)] for x in range(rows)]
     along_x = [[x * Z_RING + z for x in range(rows)] for z in range(Z_RING)]
-    weight = out_weight.T
-    for groups in (along_x, along_z):
-        weight = lax.all_gather(weight, "seq", axis=0, tiled=True, axis_index_groups=groups)
+    weight = jnp.concatenate(
+        [out_weight.T]
+        + [
+            lax.ppermute(
+                out_weight.T, "seq", [(i, (i + back * Z_RING) % count) for i in range(count)]
+            )
+            for back in range(1, rows)
+        ],
+        axis=0,
+    )
+    weight = lax.all_gather(weight, "seq", axis=0, tiled=True, axis_index_groups=along_z)
     rim = lax.ppermute(rim_source(x_in, bc_in), "seq", [(i, i + 1) for i in range(count - 1)])
     place = jnp.stack(
         [lax.axis_index("seq") // Z_RING, lax.axis_index("tp")]

time: 159 us -> 161 us (1.013)
  blocking collectives: 34.9 us -> 21.9 us
  starting transfers between devices: 37.4 us -> 50.2 us
    all_gather x1 -> x0, blocking collectives: 12.7 us -> none  [on_device(): lax.all_gather(weight, 'seq', axis=0, tiled=True, axis_index_groups=groups)]
    ppermute x0 -> x3, starting transfers between devices: none -> 10.1 us  [on_device(): lax.ppermute(out_weight.T, 'seq', [(i, (i + back * Z_RING) % count) for i...]
    ppermute x0 -> x3, waiting for transfers between devices: none -> 3.75 us  [on_device(): lax.ppermute(out_weight.T, 'seq', [(i, (i + back * Z_RING) % count) for i...]
    all_gather x1, waiting for transfers between devices: 12.4 us -> 9.28 us  [on_device(): lax.all_gather(weight, 'seq', axis=0, tiled=True, axis_index_groups=along_z)]
  transfers between devices with their start and end apart: 6 -> 9, of which waited for: 4 -> 6; matrix products, arithmetic and copies ran while one was open for 0% -> 0% of each run, Pallas kernels for 13% -> 12%
where the time goes in v6:
time: 161 us; the launch traced here: 160 us
  starting transfers between devices  50.2 us (31%)
  waiting for transfers between devices  41.1 us (26%)
  Pallas kernels  25.7 us (16%)
  blocking collectives  21.9 us (14%)
  between operations  13.7 us (9%)
  local copies, waits for them, and re-layouts  5.62 us (3%)
    pallas_call x11, Pallas kernels, call(): pl.pallas_call(body, out_shape=outs, in_specs=[pl.BlockSpec(memory_space=...  25.7 us
    all_to_all x2, waiting for transfers between devices, on_device(): lax.all_to_all(pieces, 'seq', 0, 0, tiled=True, axis_index_groups=along_z)  23.4 us
    all_to_all x1, blocking collectives, on_device(): lax.all_to_all(parts, 'tp', 0, 0, tiled=True, axis_index_groups=along_y)  21.9 us
    all_to_all x2, starting transfers between devices, on_device(): lax.all_to_all(pieces, 'seq', 0, 0, tiled=True, axis_index_groups=along_z)  21.2 us
    ppermute x1, starting transfers between devices, on_device(): got = lax.ppermute(given, 'tp', [(i, i ^ 1) for i in range(TARGETS)])  11.2 us
    ppermute x3, starting transfers between devices, on_device(): lax.ppermute(out_weight.T, 'seq', [(i, (i + back * Z_RING) % count) for i...  10.1 us
    all_gather x1, waiting for transfers between devices, on_device(): lax.all_gather(weight, 'seq', axis=0, tiled=True, axis_index_groups=along_z)  9.28 us
    unnamed x30, local copies, waits for them, and re-layouts  5.61 us
  transfers between devices with their start and end apart: 9, of which 6 were waited for; matrix products, arithmetic and copies ran while one was open for 0% of the time, Pallas kernels for 12%

profile of v6, /device:TPU:1, one launch (start us, length us, event | category | flops | bytes accessed | tf_op | source)
XLA Modules:
  0.0 159.8 jit_solution(6022793878544916349)
XLA Ops:
  6.5 5.2 %collective-permute-start.3 = (bf16[40,640]{1,0:T(8,128)(2,1)}, bf16[40,640]{1,0:T(8,128)(2,1)S(1)}, u32[]{:S(2)}, u32[]{:S(2)}) collective-permute-start(bf16[40,640]{1,0:T(8,128)(2,1)} %bitcast.23), channel_id=1, source_target_pairs={{0,384},{8,392},{16,400},{24,408},{32,416},{40,424},{48,432},{56,4... | collective-permute-start | bytes 153608 | tf_op jit(solution)/shard_map/ppermute | solution.py:629
  11.7 2.4 %collective-permute-start.2 = (bf16[40,640]{1,0:T(8,128)(2,1)}, bf16[40,640]{1,0:T(8,128)(2,1)S(1)}, u32[]{:S(2)}, u32[]{:S(2)}) collective-permute-start(bf16[40,640]{1,0:T(8,128)(2,1)} %bitcast.24), channel_id=1, source_target_pairs={{0,256},{8,264},{16,272},{24,280},{32,288},{40,296},{48,304},{56,3... | collective-permute-start | bytes 153608 | tf_op jit(solution)/shard_map/ppermute | solution.py:629
  14.2 2.5 %collective-permute-start.1 = (bf16[40,640]{1,0:T(8,128)(2,1)}, bf16[40,640]{1,0:T(8,128)(2,1)S(1)}, u32[]{:S(2)}, u32[]{:S(2)}) collective-permute-start(bf16[40,640]{1,0:T(8,128)(2,1)} %bitcast.25), channel_id=1, source_target_pairs={{0,128},{8,136},{16,144},{24,152},{32,160},{40,168},{48,176},{56,1... | collective-permute-start | bytes 153608 | tf_op jit(solution)/shard_map/ppermute | solution.py:629
  16.7 1.6 %collective-permute-done.2 = bf16[40,640]{1,0:T(8,128)(2,1)S(1)} collective-permute-done((bf16[40,640]{1,0:T(8,128)(2,1)}, bf16[40,640]{1,0:T(8,128)(2,1)S(1)}, u32[]{:S(2)}, u32[]{:S(2)}) %collective-permute-start.2) | collective-permute-done | bytes 51232 | tf_op jit(solution)/shard_map/ppermute | solution.py:629
  18.3 2.1 %collective-permute-done.1 = bf16[40,640]{1,0:T(8,128)(2,1)S(1)} collective-permute-done((bf16[40,640]{1,0:T(8,128)(2,1)}, bf16[40,640]{1,0:T(8,128)(2,1)S(1)}, u32[]{:S(2)}, u32[]{:S(2)}) %collective-permute-start.1) | collective-permute-done | bytes 51232 | tf_op jit(solution)/shard_map/ppermute | solution.py:629
  20.5 1.5 pad_maximum_fusion
  22.0 1.4 shard_map.110
  23.4 3.5 %collective-permute-start = (bf16[16,896]{1,0:T(8,128)(2,1)}, bf16[16,896]{1,0:T(8,128)(2,1)S(1)}, u32[]{:S(2)}, u32[]{:S(2)}) collective-permute-start(bf16[16,896]{1,0:T(8,128)(2,1)} %shard_map.110), channel_id=1, source_target_pairs={{0,8},{8,16},{16,24},{24,32},{32,40},{40,48},{48,56},{56,64},{64,7... | collective-permute-start | bytes 86024 | tf_op jit(solution)/shard_map/ppermute | solution.py:637
  26.9 4.9 %shard_map.109 = (bf16[512,640]{1,0:T(8,128)(2,1)}, bf16[512,256]{1,0:T(8,128)(2,1)}, f32[16,512]{1,0:T(8,128)}, f32[16,512]{1,0:T(8,128)}, f32[128,640]{1,0:T(8,128)}, /*index=5*/f32[16,640]{1,0:T(8,128)}) custom-call(bf16[512,640]{1,0:T(8,128)(2,1)} %x_hbm.5, bf16[512,256]{1,0:T(8,128)(2,1)} %bc_hbm.5, bf16[10,512]{1,0:T(8,128)(2,1)} %bitcast.27, ...), custom_call_target="tpu_custom_call" | custom-call | flops 335544320 | bytes 2293840 | tf_op jit(solution)/shard_map/pallas_call | solution.py:44
  31.9 0.6 copy-done.13
  32.5 2.8 %shard_map.111 = (bf16[16,640]{1,0:T(8,128)(2,1)}, bf16[16,256]{1,0:T(8,128)(2,1)}, bf16[768,128]{1,0:T(8,128)(2,1)}) custom-call(bf16[16,896]{1,0:T(8,128)(2,1)} %copy-done.13, bf16[512,640]{1,0:T(8,128)(2,1)} %x_hbm.5, bf16[512,256]{1,0:T(8,128)(2,1)} %bc_hbm.5, f32[4,640]{1,0:T(4,128)} %tap_x_hbm.3, f32[4,256]{1,0:T(4,128)} %tap_bc_hbm.3, ...), custom_call_target="tpu_custom_call" | custom-call | flops 20971520 | bytes 1587200 | tf_op jit(solution)/shard_map/pallas_call | solution.py:44
  35.3 14.2 %all-to-all-start = ((bf16[16,48,128]{2,1,0:T(8,128)(2,1)}), bf16[16,48,128]{2,1,0:T(8,128)(2,1)S(1)}, u32[]{:S(2)}, u32[]{:S(2)}) async-start(bf16[16,48,128]{2,1,0:T(8,128)(2,1)} %bitcast.22), calls=%async_computation | async-start | bytes 393216 | tf_op jit(solution)/shard_map/all_to_all | solution.py:646
  49.5 14.3 %all-to-all-done = bf16[16,48,128]{2,1,0:T(8,128)(2,1)S(1)} async-done(((bf16[16,48,128]{2,1,0:T(8,128)(2,1)}), bf16[16,48,128]{2,1,0:T(8,128)(2,1)S(1)}, u32[]{:S(2)}, u32[]{:S(2)}) %all-to-all-start) | async-done | bytes 196640 | tf_op jit(solution)/shard_map/all_to_all | solution.py:646
  63.9 0.8 shard_map.113
  64.6 4.1 %all-to-all-start.1 = ((f32[4,48,128]{2,1,0:T(8,128)}), f32[4,48,128]{2,1,0:T(8,128)S(1)}, u32[]{:S(2)}, u32[]{:S(2)}) async-start(f32[4,48,128]{2,1,0:T(8,128)} %shard_map.113), calls=%async_computation.1 | async-start | bytes 196608 | tf_op jit(solution)/shard_map/all_to_all | solution.py:649
  68.9 4.6 %all-to-all-done.1.refs_1_ = f32[4,48,128]{2,1,0:T(8,128)S(1)} async-done(((f32[4,48,128]{2,1,0:T(8,128)}), f32[4,48,128]{2,1,0:T(8,128)S(1)}, u32[]{:S(2)}, u32[]{:S(2)}) %all-to-all-start.1) | async-done | bytes 98336 | tf_op jit(solution)/shard_map/all_to_all | solution.py:649
  73.5 1.4 shard_map.114
  74.8 7.0 %all-to-all-start.2 = ((bf16[16,48,128]{2,1,0:T(8,128)(2,1)}), bf16[16,48,128]{2,1,0:T(8,128)(2,1)S(1)}, u32[]{:S(2)}, u32[]{:S(2)}) async-start(bf16[16,48,128]{2,1,0:T(8,128)(2,1)} %bitcast.9), calls=%async_computation.2 | async-start | bytes 393216 | tf_op jit(solution)/shard_map/all_to_all | solution.py:651
  81.9 1.1 copy-done.6
  83.0 1.1 copy-done.10
  84.1 2.5 %shard_map.112 = (f32[512,640]{1,0:T(8,128)S(1)}, f32[512,640]{1,0:T(8,128)S(1)}, bf16[512,128]{1,0:T(8,128)(2,1)S(1)}) custom-call(bf16[512,640]{1,0:T(8,128)(2,1)S(1)} %copy-done.10, bf16[16,640]{1,0:T(8,128)(2,1)S(1)} %copy-done.7, bf16[512,256]{1,0:T(8,128)(2,1)S(1)} %copy-done.11, bf16[16,256]{1,0:T(8,128)(2,1)S(1)} %copy-done.8, ...), custom_call_target="tpu_custom_call" | custom-call | flops 503316480 | bytes 4419624 | tf_op jit(solution)/shard_map/pallas_call | solution.py:44
  86.6 9.1 %all-to-all-done.2 = bf16[16,48,128]{2,1,0:T(8,128)(2,1)S(1)} async-done(((bf16[16,48,128]{2,1,0:T(8,128)(2,1)}), bf16[16,48,128]{2,1,0:T(8,128)(2,1)S(1)}, u32[]{:S(2)}, u32[]{:S(2)}) %all-to-all-start.2) | async-done | bytes 196640 | tf_op jit(solution)/shard_map/all_to_all | solution.py:651
  95.7 1.5 shard_map.115
  97.2 0.9 copy-done.1
  98.1 0.6 copy-done.2
  98.7 9.3 %all-gather.2.cloned.1.call-done.w_hbm = bf16[2560,640]{1,0:T(8,128)(2,1)} async-done(((bf16[160,640]{1,0:T(8,128)(2,1)}), bf16[2560,640]{1,0:T(8,128)(2,1)}) %all-gather.2.cloned.1.call-update) | async-done | bytes 3276816 | tf_op jit(solution)/shard_map/all_gather | solution.py:636
  107.9 4.7 %shard_map.117 = bf16[1344,512]{1,0:T(8,128)(2,1)} custom-call(bf16[512,640]{1,0:T(8,128)(2,1)} %copy-done.1, bf16[16,512]{1,0:T(8,128)(2,1)} %copy-done.2, bf16[2560,640]{1,0:T(8,128)(2,1)} %all-gather.2.cloned.1.call-done.w_hbm, s32[1,2]{1,0:T(1,128)} %copy-done.5), custom_call_target="tpu_custom_call" | custom-call | flops 838860800 | bytes 5324808 | tf_op jit(solution)/shard_map/pallas_call | solution.py:44
  112.7 11.2 %collective-permute-start.4 = (bf16[1344,512]{1,0:T(8,128)(2,1)}, bf16[1344,512]{1,0:T(8,128)(2,1)S(1)}, u32[]{:S(2)}, u32[]{:S(2)}) collective-permute-start(bf16[1344,512]{1,0:T(8,128)(2,1)} %shard_map.117), channel_id=1, source_target_pairs={{0,1},{1,0},{2,3},{3,2},{4,5},{5,4},{6,7},{7,6},{8,9},{9,8},{10,11... | collective-permute-start | bytes 4128776 | tf_op jit(solution)/shard_map/ppermute | solution.py:655
  123.9 4.5 %shard_map.116.kept_ref = bf16[1280,512]{1,0:T(8,128)(2,1)} custom-call(bf16[512,640]{1,0:T(8,128)(2,1)} %copy-done.1, bf16[2560,640]{1,0:T(8,128)(2,1)} %all-gather.2.cloned.1.call-done.w_hbm, s32[1,2]{1,0:T(1,128)} %copy-done.5), custom_call_target="tpu_custom_call" | custom-call | flops 838860800 | bytes 5242888 | tf_op jit(solution)/shard_map/pallas_call | solution.py:44
  128.5 1.3 copy-done
  130.1 21.9 %all_to_all.38 = bf16[4,336,512]{2,1,0:T(8,128)(2,1)S(1)} all-to-all(bf16[4,336,512]{2,1,0:T(8,128)(2,1)S(1)} %bitcast.16), channel_id=1, replica_groups={{0,2,4,6},{1,3,5,7},{8,10,12,14},{9,11,13,15},{16,18,20,22},{17,19,21,2..., dimensions={0} | all-to-all | bytes 2752512 | tf_op jit(solution)/shard_map/all_to_all | solution.py:659
  152.0 0.9 shard_map.119
  (32 shorter events, 0.5 us)
Async XLA Ops:
  6.5 101.4 %all-gather.2.cloned.1.call-start = ((), (), s32[]{:S(2)}) async-start(), calls=%async_computation.4 | async-start | bytes 3481600 | tf_op jit(solution)/shard_map/all_gather | solution.py:636
  6.5 10.2 %collective-permute-start.3 = (bf16[40,640]{1,0:T(8,128)(2,1)}, bf16[40,640]{1,0:T(8,128)(2,1)S(1)}, u32[]{:S(2)}, u32[]{:S(2)}) collective-permute-start(bf16[40,640]{1,0:T(8,128)(2,1)} %bitcast.23), channel_id=1, source_target_pairs={{0,384},{8,392},{16,400},{24,408},{32,416},{40,424},{48,432},{56,4... | collective-permute-start | bytes 153608 | tf_op jit(solution)/shard_map/ppermute | solution.py:629
  11.7 6.6 %collective-permute-start.2 = (bf16[40,640]{1,0:T(8,128)(2,1)}, bf16[40,640]{1,0:T(8,128)(2,1)S(1)}, u32[]{:S(2)}, u32[]{:S(2)}) collective-permute-start(bf16[40,640]{1,0:T(8,128)(2,1)} %bitcast.24), channel_id=1, source_target_pairs={{0,256},{8,264},{16,272},{24,280},{32,288},{40,296},{48,304},{56,3... | collective-permute-start | bytes 153608 | tf_op jit(solution)/shard_map/ppermute | solution.py:629
  14.2 6.3 %collective-permute-start.1 = (bf16[40,640]{1,0:T(8,128)(2,1)}, bf16[40,640]{1,0:T(8,128)(2,1)S(1)}, u32[]{:S(2)}, u32[]{:S(2)}) collective-permute-start(bf16[40,640]{1,0:T(8,128)(2,1)} %bitcast.25), channel_id=1, source_target_pairs={{0,128},{8,136},{16,144},{24,152},{32,160},{40,168},{48,176},{56,1... | collective-permute-start | bytes 153608 | tf_op jit(solution)/shard_map/ppermute | solution.py:629
  23.4 8.5 %collective-permute-start = (bf16[16,896]{1,0:T(8,128)(2,1)}, bf16[16,896]{1,0:T(8,128)(2,1)S(1)}, u32[]{:S(2)}, u32[]{:S(2)}) collective-permute-start(bf16[16,896]{1,0:T(8,128)(2,1)} %shard_map.110), channel_id=1, source_target_pairs={{0,8},{8,16},{16,24},{24,32},{32,40},{40,48},{48,56},{56,64},{64,7... | collective-permute-start | bytes 86024 | tf_op jit(solution)/shard_map/ppermute | solution.py:637
  31.9 0.6 copy-start.13
  32.5 49.4 %copy-start.14 = (f32[640]{0:T(1024)S(1)}, f32[640]{0:T(1024)}, u32[]{:S(2)}) copy-start(f32[640]{0:T(1024)} %param.20) | copy-start | bytes 7684
  32.5 49.4 %copy-start.4 = (f32[16,512]{1,0:T(8,128)S(1)}, f32[16,512]{1,0:T(8,128)}, u32[]{:S(2)}) copy-start(f32[16,512]{1,0:T(8,128)} %get-tuple-element.20.cum_ref) | copy-start | bytes 98308
  32.5 49.4 %copy-start.9 = (f32[10]{0:T(128)S(1)}, f32[10]{0:T(128)}, u32[]{:S(2)}) copy-start(f32[10]{0:T(128)} %param.19) | copy-start | bytes 124
  32.5 49.4 %copy-start.11 = (bf16[512,256]{1,0:T(8,128)(2,1)S(1)}, bf16[512,256]{1,0:T(8,128)(2,1)}, u32[]{:S(2)}) copy-start(bf16[512,256]{1,0:T(8,128)(2,1)} %get-tuple-element.24.bcc_ref) | copy-start | bytes 786436
  32.5 49.4 %copy-start.12 = (f32[16,512]{1,0:T(8,128)S(1)}, f32[16,512]{1,0:T(8,128)}, u32[]{:S(2)}) copy-start(f32[16,512]{1,0:T(8,128)} %get-tuple-element.26.logstep_ref) | copy-start | bytes 98308
  35.3 46.6 %copy-start.7 = (bf16[16,640]{1,0:T(8,128)(2,1)S(1)}, bf16[16,640]{1,0:T(8,128)(2,1)}, u32[]{:S(2)}) copy-start(bf16[16,640]{1,0:T(8,128)(2,1)} %get-tuple-element.23.xc_rim_ref) | copy-start | bytes 61444
  35.3 46.6 %copy-start.8 = (bf16[16,256]{1,0:T(8,128)(2,1)S(1)}, bf16[16,256]{1,0:T(8,128)(2,1)}, u32[]{:S(2)}) copy-start(bf16[16,256]{1,0:T(8,128)(2,1)} %get-tuple-element.25.bcc_rim_ref) | copy-start | bytes 24580
  35.3 28.5 %all-to-all-start = ((bf16[16,48,128]{2,1,0:T(8,128)(2,1)}), bf16[16,48,128]{2,1,0:T(8,128)(2,1)S(1)}, u32[]{:S(2)}, u32[]{:S(2)}) async-start(bf16[16,48,128]{2,1,0:T(8,128)(2,1)} %bitcast.22), calls=%async_computation | async-start | bytes 393216 | tf_op jit(solution)/shard_map/all_to_all | solution.py:646
  64.6 8.8 %all-to-all-start.1 = ((f32[4,48,128]{2,1,0:T(8,128)}), f32[4,48,128]{2,1,0:T(8,128)S(1)}, u32[]{:S(2)}, u32[]{:S(2)}) async-start(f32[4,48,128]{2,1,0:T(8,128)} %shard_map.113), calls=%async_computation.1 | async-start | bytes 196608 | tf_op jit(solution)/shard_map/all_to_all | solution.py:649
  68.9 26.8 %copy-start.5 = (s32[1,2]{1,0:T(1,128)}, s32[1,2]{1,0:T(1,128)S(1)}, u32[]{:S(2)}) copy-start(s32[1,2]{1,0:T(1,128)S(1)} %add_bitcast_fusion.refs_2_.place_ref) | copy-start | bytes 28
  74.8 20.9 %all-to-all-start.2 = ((bf16[16,48,128]{2,1,0:T(8,128)(2,1)}), bf16[16,48,128]{2,1,0:T(8,128)(2,1)S(1)}, u32[]{:S(2)}, u32[]{:S(2)}) async-start(bf16[16,48,128]{2,1,0:T(8,128)(2,1)} %bitcast.9), calls=%async_computation.2 | async-start | bytes 393216 | tf_op jit(solution)/shard_map/all_to_all | solution.py:651
  81.9 1.1 copy-start.6
  83.0 1.1 copy-start.10
  97.2 0.9 copy-start.1
  98.1 0.6 copy-start.2
  112.6 15.8 %copy-start.3 = (bf16[16,512]{1,0:T(8,128)(2,1)S(1)}, bf16[16,512]{1,0:T(8,128)(2,1)}, u32[]{:S(2)}) copy-start(bf16[16,512]{1,0:T(8,128)(2,1)} %copy-done.2) | copy-start | bytes 49156
  112.7 15.8 %collective-permute-start.4 = (bf16[1344,512]{1,0:T(8,128)(2,1)}, bf16[1344,512]{1,0:T(8,128)(2,1)S(1)}, u32[]{:S(2)}, u32[]{:S(2)}) collective-permute-start(bf16[1344,512]{1,0:T(8,128)(2,1)} %shard_map.117), channel_id=1, source_target_pairs={{0,1},{1,0},{2,3},{3,2},{4,5},{5,4},{6,7},{7,6},{8,9},{9,8},{10,11... | collective-permute-start | bytes 4128776 | tf_op jit(solution)/shard_map/ppermute | solution.py:655
  128.5 1.3 copy-start
Sparse Core Ops, SparseCore 0:
  22.1 85.7 all-gather.1

commit v7 on v6

--- a/solution.py
+++ b/solution.py
@@ -331,7 +331,7 @@
     for at in range(0, tokens, CHUNK):
         rows = slice(at, at + CHUNK)
         y = own_ref[rows, :] + reach_ref[rows, :] * dot(c_ref[rows, :], incoming)
-        gated_ref[rows, :] = (y * gain_ref[...]).astype(BF16)
+        gated_ref[:, rows] = (y * gain_ref[...]).T.astype(BF16)
         hi, lo = split(y * y)
         totals.append(dot(ones, jnp.concatenate([hi, lo], axis=1), NT))
     hi, lo = split(jnp.concatenate(totals, axis=1))
@@ -344,7 +344,7 @@
 
 
 def project_half(
-    gated_hbm, w_hbm, place_ref, half, out_hbm, gated, w_ref, acc, stage, sems, out_sems, gap
+    gated_hbm, w_hbm, half, out_hbm, gated, w_ref, acc, stage, sems, out_sems, gap
 ):
     span = w_ref.shape[0]
     parts = sems.shape[0] - 1
@@ -364,25 +364,23 @@
     for k in range(parts):
         rows = slice(k * step, (k + 1) * step)
         copies[1 + k].wait()
-        acc[rows, :] = dot(w_ref[rows, :], gated[...], NT)
+        acc[rows, :] = dot(w_ref[rows, :], gated[...])
     blocks = TARGETS // 2
     block = span // blocks
     shard = block // (Z_RING // 2)
     size = block + gap
     sent = []
-    for back in range(blocks):
-        at = back * size
+    for x in range(blocks):
+        at = x * size
         stage[at : at + block, :] = jnp.concatenate(
             [
-                acc[z * block // 2 + back * shard : z * block // 2 + (back + 1) * shard, :]
+                acc[z * block // 2 + x * shard : z * block // 2 + (x + 1) * shard, :]
                 for z in range(Z_RING // 2)
             ],
             axis=0,
         ).astype(BF16)
-        to = pl.multiple_of(lax.rem(place_ref[0, 0] + blocks - back, blocks) * size, size)
-        copy = pltpu.make_async_copy(
-            stage.at[at : at + size, :], out_hbm.at[pl.ds(to, size), :], out_sems.at[back]
-        )
+        part = slice(at, at + size)
+        copy = pltpu.make_async_copy(stage.at[part, :], out_hbm.at[part, :], out_sems.at[x])
         copy.start()
         sent.append(copy)
     for copy in sent:
@@ -397,14 +395,14 @@
         stage[(x + 1) * size - 16 : (x + 1) * size, :] = square_ref[...]
     half = 1 - lax.rem(place_ref[0, 1], 2)
     project_half(
-        gated_hbm, w_hbm, place_ref, half, out_hbm, gated, w_ref, acc, stage, sems, out_sems, 16
+        gated_hbm, w_hbm, half, out_hbm, gated, w_ref, acc, stage, sems, out_sems, 16
     )
 
 
 def kept_kernel(gated_hbm, w_hbm, place_ref, out_hbm, gated, w_ref, acc, stage, sems, out_sems):
     half = lax.rem(place_ref[0, 1], 2)
     project_half(
-        gated_hbm, w_hbm, place_ref, half, out_hbm, gated, w_ref, acc, stage, sems, out_sems, 0
+        gated_hbm, w_hbm, half, out_hbm, gated, w_ref, acc, stage, sems, out_sems, 0
     )
 
 
@@ -553,7 +551,7 @@
     tokens, width = own.shape
     return call(
         gate_kernel,
-        [shaped((tokens, width), BF16), shaped((16, tokens), BF16)],
+        [shaped((width, tokens), BF16), shaped((16, tokens), BF16)],
         2 * tokens * width * STATE,
         own, reach, c_part, pieces, norm_gain[None], place,
         spaces=[pltpu.VMEM] * 5 + [pltpu.SMEM],
@@ -563,7 +561,7 @@
 
 def half_scratch(gated, weight, rows):
     columns, width = weight.shape
-    tokens = gated.shape[0]
+    tokens = gated.shape[1]
     return (
         *held_like(gated),
         pltpu.VMEM((columns // 2, width), BF16),
@@ -575,7 +573,7 @@
 
 
 def given_part(gated, squares, weight, place):
-    tokens, width = gated.shape
+    width, tokens = gated.shape
     half = weight.shape[0] // 2
     rows = half + TARGETS // 2 * 16
     return call(
@@ -591,7 +589,7 @@
 
 
 def kept_part(gated, weight, place):
-    tokens, width = gated.shape
+    width, tokens = gated.shape
     half = weight.shape[0] // 2
     return call(
         kept_kernel,
@@ -623,17 +621,9 @@
     rows = count // Z_RING
     along_z = [[x * Z_RING + z for z in range(Z_RING)] for x in range(rows)]
     along_x = [[x * Z_RING + z for x in range(rows)] for z in range(Z_RING)]
-    weight = jnp.concatenate(
-        [out_weight.T]
-        + [
-            lax.ppermute(
-                out_weight.T, "seq", [(i, (i + back * Z_RING) % count) for i in range(count)]
-            )
-            for back in range(1, rows)
-        ],
-        axis=0,
-    )
-    weight = lax.all_gather(weight, "seq", axis=0, tiled=True, axis_index_groups=along_z)
+    weight = out_weight.T
+    for groups in (along_x, along_z):
+        weight = lax.all_gather(weight, "seq", axis=0, tiled=True, axis_index_groups=groups)
     rim = lax.ppermute(rim_source(x_in, bc_in), "seq", [(i, i + 1) for i in range(count - 1)])
     place = jnp.stack(
         [lax.axis_index("seq") // Z_RING, lax.axis_index("tp")]

time: 161 us -> 158 us (0.981)
  blocking collectives: 21.9 us -> 35 us
  starting transfers between devices: 50.2 us -> 37.4 us
    all_gather x0 -> x1, blocking collectives: none -> 12.7 us  [on_device(): lax.all_gather(weight, 'seq', axis=0, tiled=True, axis_index_groups=groups)]
    ppermute x3 -> x0, starting transfers between devices: 10.1 us -> none  [on_device(): lax.ppermute(out_weight.T, 'seq', [(i, (i + back * Z_RING) % count) for i...]
    ppermute x3 -> x0, waiting for transfers between devices: 3.75 us -> none  [on_device(): lax.ppermute(out_weight.T, 'seq', [(i, (i + back * Z_RING) % count) for i...]
    all_gather x1, waiting for transfers between devices: 9.28 us -> 12.4 us  [on_device(): lax.all_gather(weight, 'seq', axis=0, tiled=True, axis_index_groups=groups)]
  transfers between devices with their start and end apart: 9 -> 6, of which waited for: 6 -> 4; matrix products, arithmetic and copies ran while one was open for 0% -> 0% of each run, Pallas kernels for 12% -> 13%
where the time goes in v7:
time: 158 us
  waiting for transfers between devices  40.2 us (25%)
  starting transfers between devices  37.4 us (24%)
  blocking collectives  35 us (22%)
  Pallas kernels  25.6 us (16%)
  between operations  13.7 us (9%)
  local copies, waits for them, and re-layouts  5.56 us (4%)
    pallas_call x11, Pallas kernels, call(): pl.pallas_call(body, out_shape=outs, in_specs=[pl.BlockSpec(memory_space=...  25.6 us
    all_to_all x2, waiting for transfers between devices, on_device(): lax.all_to_all(pieces, 'seq', 0, 0, tiled=True, axis_index_groups=along_z)  23.2 us
    all_to_all x1, blocking collectives, on_device(): lax.all_to_all(parts, 'tp', 0, 0, tiled=True, axis_index_groups=along_y)  22.3 us
    all_to_all x2, starting transfers between devices, on_device(): lax.all_to_all(pieces, 'seq', 0, 0, tiled=True, axis_index_groups=along_z)  20.6 us
    all_gather x1, blocking collectives, on_device(): lax.all_gather(weight, 'seq', axis=0, tiled=True, axis_index_groups=groups)  12.7 us
    all_gather x1, waiting for transfers between devices, on_device(): lax.all_gather(weight, 'seq', axis=0, tiled=True, axis_index_groups=groups)  12.4 us
    ppermute x1, starting transfers between devices, on_device(): got = lax.ppermute(given, 'tp', [(i, i ^ 1) for i in range(TARGETS)])  10.5 us
    unnamed x30, local copies, waits for them, and re-layouts  5.56 us
  transfers between devices with their start and end apart: 6, of which 4 were waited for; matrix products, arithmetic and copies ran while one was open for 0% of the time, Pallas kernels for 13%

profile of v7, /device:TPU:1, one launch (start us, length us, event | category | flops | bytes accessed | tf_op | source)
XLA Modules:
  0.0 157.5 jit_solution(1789857847440358623)
XLA Ops:
  6.5 12.7 %all_gather.6 = bf16[160,640]{1,0:T(8,128)(2,1)} all-gather(bf16[40,640]{1,0:T(8,128)(2,1)} %bitcast.23), channel_id=1, replica_groups={{0,128,256,384},{8,136,264,392},{16,144,272,400},{24,152,280,408},{32,1..., dimensions={0}, use_global_device_ids=true | all-gather | bytes 256000 | tf_op jit(solution)/shard_map/all_gather | solution.py:626
  19.3 0.0 all-gather.2.cloned.1.call-update
  19.3 1.4 shard_map.110
  20.6 3.1 %collective-permute-start = (bf16[16,896]{1,0:T(8,128)(2,1)}, bf16[16,896]{1,0:T(8,128)(2,1)S(1)}, u32[]{:S(2)}, u32[]{:S(2)}) collective-permute-start(bf16[16,896]{1,0:T(8,128)(2,1)} %shard_map.110), channel_id=1, source_target_pairs={{0,8},{8,16},{16,24},{24,32},{32,40},{40,48},{48,56},{56,64},{64,7... | collective-permute-start | bytes 86024 | tf_op jit(solution)/shard_map/ppermute | solution.py:627
  23.7 4.9 %shard_map.109 = (bf16[512,640]{1,0:T(8,128)(2,1)}, bf16[512,256]{1,0:T(8,128)(2,1)}, f32[16,512]{1,0:T(8,128)}, f32[16,512]{1,0:T(8,128)}, f32[128,640]{1,0:T(8,128)}, /*index=5*/f32[16,640]{1,0:T(8,128)}) custom-call(bf16[512,640]{1,0:T(8,128)(2,1)} %x_hbm.5, bf16[512,256]{1,0:T(8,128)(2,1)} %bc_hbm.5, bf16[10,512]{1,0:T(8,128)(2,1)} %bitcast.24, ...), custom_call_target="tpu_custom_call" | custom-call | flops 335544320 | bytes 2293840 | tf_op jit(solution)/shard_map/pallas_call | solution.py:44
  28.7 0.6 copy-done.13
  29.3 2.8 %shard_map.111 = (bf16[16,640]{1,0:T(8,128)(2,1)}, bf16[16,256]{1,0:T(8,128)(2,1)}, bf16[768,128]{1,0:T(8,128)(2,1)}) custom-call(bf16[16,896]{1,0:T(8,128)(2,1)} %copy-done.13, bf16[512,640]{1,0:T(8,128)(2,1)} %x_hbm.5, bf16[512,256]{1,0:T(8,128)(2,1)} %bc_hbm.5, f32[4,640]{1,0:T(4,128)} %tap_x_hbm.3, f32[4,256]{1,0:T(4,128)} %tap_bc_hbm.3, ...), custom_call_target="tpu_custom_call" | custom-call | flops 20971520 | bytes 1587200 | tf_op jit(solution)/shard_map/pallas_call | solution.py:44
  32.2 14.2 %all-to-all-start = ((bf16[16,48,128]{2,1,0:T(8,128)(2,1)}), bf16[16,48,128]{2,1,0:T(8,128)(2,1)S(1)}, u32[]{:S(2)}, u32[]{:S(2)}) async-start(bf16[16,48,128]{2,1,0:T(8,128)(2,1)} %bitcast.22), calls=%async_computation | async-start | bytes 393216 | tf_op jit(solution)/shard_map/all_to_all | solution.py:636
  46.4 14.6 %all-to-all-done = bf16[16,48,128]{2,1,0:T(8,128)(2,1)S(1)} async-done(((bf16[16,48,128]{2,1,0:T(8,128)(2,1)}), bf16[16,48,128]{2,1,0:T(8,128)(2,1)S(1)}, u32[]{:S(2)}, u32[]{:S(2)}) %all-to-all-start) | async-done | bytes 196640 | tf_op jit(solution)/shard_map/all_to_all | solution.py:636
  61.0 0.8 shard_map.113
  61.8 3.3 %all-to-all-start.1 = ((f32[4,48,128]{2,1,0:T(8,128)}), f32[4,48,128]{2,1,0:T(8,128)S(1)}, u32[]{:S(2)}, u32[]{:S(2)}) async-start(f32[4,48,128]{2,1,0:T(8,128)} %shard_map.113), calls=%async_computation.1 | async-start | bytes 196608 | tf_op jit(solution)/shard_map/all_to_all | solution.py:639
  65.1 0.1 add_bitcast_fusion.refs_2_.place_ref
  65.2 4.5 %all-to-all-done.1.refs_1_ = f32[4,48,128]{2,1,0:T(8,128)S(1)} async-done(((f32[4,48,128]{2,1,0:T(8,128)}), f32[4,48,128]{2,1,0:T(8,128)S(1)}, u32[]{:S(2)}, u32[]{:S(2)}) %all-to-all-start.1) | async-done | bytes 98336 | tf_op jit(solution)/shard_map/all_to_all | solution.py:639
  69.7 1.4 shard_map.114
  71.0 6.4 %all-to-all-start.2 = ((bf16[16,48,128]{2,1,0:T(8,128)(2,1)}), bf16[16,48,128]{2,1,0:T(8,128)(2,1)S(1)}, u32[]{:S(2)}, u32[]{:S(2)}) async-start(bf16[16,48,128]{2,1,0:T(8,128)(2,1)} %bitcast.9), calls=%async_computation.2 | async-start | bytes 393216 | tf_op jit(solution)/shard_map/all_to_all | solution.py:641
  77.5 0.0 copy-start.6
  77.5 1.1 copy-done.6
  78.6 1.1 copy-done.10
  79.7 2.5 %shard_map.112 = (f32[512,640]{1,0:T(8,128)S(1)}, f32[512,640]{1,0:T(8,128)S(1)}, bf16[512,128]{1,0:T(8,128)(2,1)S(1)}) custom-call(bf16[512,640]{1,0:T(8,128)(2,1)S(1)} %copy-done.10, bf16[16,640]{1,0:T(8,128)(2,1)S(1)} %copy-done.7, bf16[512,256]{1,0:T(8,128)(2,1)S(1)} %copy-done.11, bf16[16,256]{1,0:T(8,128)(2,1)S(1)} %copy-done.8, ...), custom_call_target="tpu_custom_call" | custom-call | flops 503316480 | bytes 4419624 | tf_op jit(solution)/shard_map/pallas_call | solution.py:44
  82.2 8.6 %all-to-all-done.2 = bf16[16,48,128]{2,1,0:T(8,128)(2,1)S(1)} async-done(((bf16[16,48,128]{2,1,0:T(8,128)(2,1)}), bf16[16,48,128]{2,1,0:T(8,128)(2,1)S(1)}, u32[]{:S(2)}, u32[]{:S(2)}) %all-to-all-start.2) | async-done | bytes 196640 | tf_op jit(solution)/shard_map/all_to_all | solution.py:641
  90.8 1.5 shard_map.115
  92.3 0.8 copy-done.1
  93.2 0.6 copy-done.2
  93.8 12.4 %all-gather.2.cloned.1.call-done.w_hbm = bf16[2560,640]{1,0:T(8,128)(2,1)} async-done(((bf16[160,640]{1,0:T(8,128)(2,1)}), bf16[2560,640]{1,0:T(8,128)(2,1)}) %all-gather.2.cloned.1.call-update) | async-done | bytes 3276816 | tf_op jit(solution)/shard_map/all_gather | solution.py:626
  106.2 4.6 %shard_map.117 = bf16[1344,512]{1,0:T(8,128)(2,1)} custom-call(bf16[640,512]{1,0:T(8,128)(2,1)} %copy-done.1, bf16[16,512]{1,0:T(8,128)(2,1)} %copy-done.2, bf16[2560,640]{1,0:T(8,128)(2,1)} %all-gather.2.cloned.1.call-done.w_hbm, s32[1,2]{1,0:T(1,128)} %copy-done.5), custom_call_target="tpu_custom_call" | custom-call | flops 838860800 | bytes 5324808 | tf_op jit(solution)/shard_map/pallas_call | solution.py:44
  110.8 0.0 copy-start.3
  110.9 10.5 %collective-permute-start.1 = (bf16[1344,512]{1,0:T(8,128)(2,1)}, bf16[1344,512]{1,0:T(8,128)(2,1)S(1)}, u32[]{:S(2)}, u32[]{:S(2)}) collective-permute-start(bf16[1344,512]{1,0:T(8,128)(2,1)} %shard_map.117), channel_id=1, source_target_pairs={{0,1},{1,0},{2,3},{3,2},{4,5},{5,4},{6,7},{7,6},{8,9},{9,8},{10,11... | collective-permute-start | bytes 4128776 | tf_op jit(solution)/shard_map/ppermute | solution.py:645
  121.3 4.5 %shard_map.116.kept_ref = bf16[1280,512]{1,0:T(8,128)(2,1)} custom-call(bf16[640,512]{1,0:T(8,128)(2,1)} %copy-done.1, bf16[2560,640]{1,0:T(8,128)(2,1)} %all-gather.2.cloned.1.call-done.w_hbm, s32[1,2]{1,0:T(1,128)} %copy-done.5), custom_call_target="tpu_custom_call" | custom-call | flops 838860800 | bytes 5242888 | tf_op jit(solution)/shard_map/pallas_call | solution.py:44
  125.8 1.3 copy-done
  127.2 0.3 shard_map.118
  127.5 22.3 %all_to_all.38 = bf16[4,336,512]{2,1,0:T(8,128)(2,1)S(1)} all-to-all(bf16[4,336,512]{2,1,0:T(8,128)(2,1)S(1)} %bitcast.16), channel_id=1, replica_groups={{0,2,4,6},{1,3,5,7},{8,10,12,14},{9,11,13,15},{16,18,20,22},{17,19,21,2..., dimensions={0} | all-to-all | bytes 2752512 | tf_op jit(solution)/shard_map/all_to_all | solution.py:649
  149.7 0.9 shard_map.119
  (26 shorter events, 0.1 us)
Async XLA Ops:
  6.5 99.7 %all-gather.2.cloned.1.call-start = ((), (), s32[]{:S(2)}) async-start(), calls=%async_computation.4 | async-start | bytes 3481600 | tf_op jit(solution)/shard_map/all_gather | solution.py:626
  20.6 8.0 %collective-permute-start = (bf16[16,896]{1,0:T(8,128)(2,1)}, bf16[16,896]{1,0:T(8,128)(2,1)S(1)}, u32[]{:S(2)}, u32[]{:S(2)}) collective-permute-start(bf16[16,896]{1,0:T(8,128)(2,1)} %shard_map.110), channel_id=1, source_target_pairs={{0,8},{8,16},{16,24},{24,32},{32,40},{40,48},{48,56},{56,64},{64,7... | collective-permute-start | bytes 86024 | tf_op jit(solution)/shard_map/ppermute | solution.py:627
  28.7 0.6 copy-start.13
  29.3 48.2 %copy-start.14 = (f32[640]{0:T(1024)S(1)}, f32[640]{0:T(1024)}, u32[]{:S(2)}) copy-start(f32[640]{0:T(1024)} %param.20) | copy-start | bytes 7684
  29.3 48.2 %copy-start.4 = (f32[16,512]{1,0:T(8,128)S(1)}, f32[16,512]{1,0:T(8,128)}, u32[]{:S(2)}) copy-start(f32[16,512]{1,0:T(8,128)} %get-tuple-element.20.cum_ref) | copy-start | bytes 98308
  29.3 48.2 %copy-start.9 = (f32[10]{0:T(128)S(1)}, f32[10]{0:T(128)}, u32[]{:S(2)}) copy-start(f32[10]{0:T(128)} %param.19) | copy-start | bytes 124
  29.3 48.2 %copy-start.11 = (bf16[512,256]{1,0:T(8,128)(2,1)S(1)}, bf16[512,256]{1,0:T(8,128)(2,1)}, u32[]{:S(2)}) copy-start(bf16[512,256]{1,0:T(8,128)(2,1)} %get-tuple-element.24.bcc_ref) | copy-start | bytes 786436
  29.3 48.2 %copy-start.12 = (f32[16,512]{1,0:T(8,128)S(1)}, f32[16,512]{1,0:T(8,128)}, u32[]{:S(2)}) copy-start(f32[16,512]{1,0:T(8,128)} %get-tuple-element.26.logstep_ref) | copy-start | bytes 98308
  32.2 45.4 %copy-start.7 = (bf16[16,640]{1,0:T(8,128)(2,1)S(1)}, bf16[16,640]{1,0:T(8,128)(2,1)}, u32[]{:S(2)}) copy-start(bf16[16,640]{1,0:T(8,128)(2,1)} %get-tuple-element.23.xc_rim_ref) | copy-start | bytes 61444
  32.2 45.4 %copy-start.8 = (bf16[16,256]{1,0:T(8,128)(2,1)S(1)}, bf16[16,256]{1,0:T(8,128)(2,1)}, u32[]{:S(2)}) copy-start(bf16[16,256]{1,0:T(8,128)(2,1)} %get-tuple-element.25.bcc_rim_ref) | copy-start | bytes 24580
  32.2 28.8 %all-to-all-start = ((bf16[16,48,128]{2,1,0:T(8,128)(2,1)}), bf16[16,48,128]{2,1,0:T(8,128)(2,1)S(1)}, u32[]{:S(2)}, u32[]{:S(2)}) async-start(bf16[16,48,128]{2,1,0:T(8,128)(2,1)} %bitcast.22), calls=%async_computation | async-start | bytes 393216 | tf_op jit(solution)/shard_map/all_to_all | solution.py:636
  61.8 7.9 %all-to-all-start.1 = ((f32[4,48,128]{2,1,0:T(8,128)}), f32[4,48,128]{2,1,0:T(8,128)S(1)}, u32[]{:S(2)}, u32[]{:S(2)}) async-start(f32[4,48,128]{2,1,0:T(8,128)} %shard_map.113), calls=%async_computation.1 | async-start | bytes 196608 | tf_op jit(solution)/shard_map/all_to_all | solution.py:639
  65.2 25.7 %copy-start.5 = (s32[1,2]{1,0:T(1,128)}, s32[1,2]{1,0:T(1,128)S(1)}, u32[]{:S(2)}) copy-start(s32[1,2]{1,0:T(1,128)S(1)} %add_bitcast_fusion.refs_2_.place_ref) | copy-start | bytes 28
  71.0 19.8 %all-to-all-start.2 = ((bf16[16,48,128]{2,1,0:T(8,128)(2,1)}), bf16[16,48,128]{2,1,0:T(8,128)(2,1)S(1)}, u32[]{:S(2)}, u32[]{:S(2)}) async-start(bf16[16,48,128]{2,1,0:T(8,128)(2,1)} %bitcast.9), calls=%async_computation.2 | async-start | bytes 393216 | tf_op jit(solution)/shard_map/all_to_all | solution.py:641
  77.5 1.1 copy-start.6
  78.6 1.1 copy-start.10
  92.3 0.8 copy-start.1
  93.2 0.6 copy-start.2
  110.8 15.0 %copy-start.3 = (bf16[16,512]{1,0:T(8,128)(2,1)S(1)}, bf16[16,512]{1,0:T(8,128)(2,1)}, u32[]{:S(2)}) copy-start(bf16[16,512]{1,0:T(8,128)(2,1)} %copy-done.2) | copy-start | bytes 49156
  110.9 15.0 %collective-permute-start.1 = (bf16[1344,512]{1,0:T(8,128)(2,1)}, bf16[1344,512]{1,0:T(8,128)(2,1)S(1)}, u32[]{:S(2)}, u32[]{:S(2)}) collective-permute-start(bf16[1344,512]{1,0:T(8,128)(2,1)} %shard_map.117), channel_id=1, source_target_pairs={{0,1},{1,0},{2,3},{3,2},{4,5},{5,4},{6,7},{7,6},{8,9},{9,8},{10,11... | collective-permute-start | bytes 4128776 | tf_op jit(solution)/shard_map/ppermute | solution.py:645
  125.8 1.3 copy-start
Sparse Core Ops, SparseCore 0:
  19.4 86.7 all-gather.1
